TPU v7x, 128 devices: a whole 4x4x4 slice. The times are simulated.
128 devices in a mesh: lon: 32 (over y, z, core), lat: 4 (over x).
Axes of the slice: x: 4, y: 4, z: 4, core: 2. Of those that a mesh axis runs over, the one named last changes fastest.
Arguments:
- atmos_flux: float32 [32768, 6, 128], P(('lon', 'lat')), may hold values from -6 to 6
- remap_blocks: bfloat16 [32768, 128, 128], P(('lon', 'lat')), may hold values from -0.5 to 0.5
- row_owner: int32 [32768, 1], P(('lon', 'lat')), may hold values from 0 to 127; in each aligned block of 256 rows (0 to 255, 256 to 511, ...) at most 4 rows name the same one
- row_target: int32 [32768], P(('lon', 'lat')), may hold values from 0 to 31
- tracers: float32 [2, 8, 128, 4096], P(None, None, 'lat', 'lon'), may hold values from -6 to 6
- east_vel: float32 [8, 128, 4096], P(None, 'lat', 'lon'), may hold values from -0.2 to 0.2
- north_vel: float32 [8, 128, 4096], P(None, 'lat', 'lon'), may hold values from -0.2 to 0.2
- mix_kappa: float32 [8, 128, 4096], P(None, 'lat', 'lon'), may hold values from 0.05 to 2
- levels: int32 [128, 4096], P('lat', 'lon'), may hold values from 0 to 8
Outputs:
- tracers_next: float32 [2, 8, 128, 4096], P(None, None, 'lat', 'lon')
- atmos_state: float32 [32768, 2, 128], P(('lon', 'lat'))
Inputs may be any that keep to these rules, and one draw needn't show every extreme that they name: `row_owner`: in the rows of one device no ocean device is named more than 4 times, and some ocean device is named exactly 4 times.
All inputs are finite; a program needn't handle non-finite values.
Results may differ from a plain program's by a relative error of at most 0.0003.
Values sent between devices are 32-bit elements; how exact they have to be, the bound alone decides.
No kernel may reach another device: no remote copies, remote signals or barrier semaphores. Data moves between devices by JAX's collectives and lax.ppermute only.
A program may use at most 64 MiB of HBM per device.

v0:
```python
import jax
import jax.numpy as jnp
from jax import lax
from jax.sharding import PartitionSpec as P

sw_decay = 0.5
heat_coef = 0.5
fresh_coef = 0.5
stir_coef = 0.25
depth_decay = 0.5


def with_halo(block, sides, width, periodic):
    for axis, dim in sides:
        count = lax.axis_size(axis)
        forward = [(i, i + 1) for i in range(count - 1)]
        if periodic:
            forward.append((count - 1, 0))
        backward = [(target, source) for source, target in forward]
        low = lax.ppermute(
            lax.slice_in_dim(block, block.shape[dim] - width, None, axis=dim), axis, forward
        )
        high = lax.ppermute(lax.slice_in_dim(block, 0, width, axis=dim), axis, backward)
        block = jnp.concatenate([low, block, high], axis=dim)
    return block


def upwind(velocity, left_val, right_val, wet_left, wet_right):
    return (jnp.maximum(velocity, 0.0) * left_val + jnp.minimum(velocity, 0.0) * right_val) * (
        wet_left * wet_right
    )


def tridiagonal_pair(rhs_list, air_sea_link):
    depth_count = len(rhs_list)
    zero_plane = jnp.zeros_like(air_sea_link[0])
    gain_list = []
    offset_list = []
    for level_idx in range(depth_count):
        low_coef = air_sea_link[level_idx - 1] if level_idx > 0 else zero_plane
        up_coef = air_sea_link[level_idx] if level_idx < depth_count - 1 else zero_plane
        diagonal = 1.0 + low_coef + up_coef
        if level_idx > 0:
            denominator = diagonal - low_coef * gain_list[-1]
            numerator = rhs_list[level_idx] + low_coef[None] * offset_list[-1]
        else:
            denominator = diagonal
            numerator = rhs_list[0]
        gain_list.append(up_coef / denominator)
        offset_list.append(numerator / denominator[None])
    solved = [offset_list[-1]]
    for level_idx in range(depth_count - 2, -1, -1):
        solved.append(offset_list[level_idx] + gain_list[level_idx][None] * solved[-1])
    return jnp.stack(solved[::-1], 0)


def step_tracers(ext_tracer, ext_east, ext_north, ext_wet, forcing, mix_kappa):
    eastward = upwind(
        ext_east[:, 1:-1, :-1],
        ext_tracer[:, :, 1:-1, :-1],
        ext_tracer[:, :, 1:-1, 1:],
        ext_wet[:, 1:-1, :-1],
        ext_wet[:, 1:-1, 1:],
    )
    poleward_speed = upwind(
        ext_north[:, :-1, 1:-1],
        ext_tracer[:, :, :-1, 1:-1],
        ext_tracer[:, :, 1:, 1:-1],
        ext_wet[:, :-1, 1:-1],
        ext_wet[:, 1:, 1:-1],
    )
    centre_cells = ext_tracer[:, :, 1:-1, 1:-1]
    wetness = ext_wet[:, 1:-1, 1:-1]
    carried_tracer = (
        centre_cells
        - (eastward[..., 1:] - eastward[..., :-1])
        - (poleward_speed[:, :, 1:, :] - poleward_speed[:, :, :-1, :])
    )
    carried_levels = jnp.swapaxes(carried_tracer, 0, 1)
    depth_count = wetness.shape[0]
    depth_rank = jnp.arange(depth_count, dtype=jnp.float32)
    sw_fraction = jnp.exp(-sw_decay * depth_rank) - jnp.exp(-sw_decay * (depth_rank + 1.0))
    temp_pick = jnp.array([1.0, 0.0], jnp.float32)[:, None, None]
    salt_pick = jnp.array([0.0, 1.0], jnp.float32)[:, None, None]
    rhs_list = []
    for level_idx in range(depth_count):
        heat_level = wetness[level_idx] * sw_fraction[level_idx] * forcing[0]
        if level_idx == 0:
            heat_level = heat_level + wetness[0] * heat_coef * (
                forcing[1] + forcing[2] + forcing[3]
            )
            salt_level = wetness[0] * fresh_coef * forcing[4]
            source = heat_level[None] * temp_pick + salt_level[None] * salt_pick
        else:
            source = heat_level[None] * temp_pick
        rhs_list.append(carried_levels[level_idx] + source)
    stirring = stir_coef * forcing[5] * forcing[5]
    air_sea_link = (
        mix_kappa[1:] + stirring[None] * jnp.exp(-depth_decay * depth_rank[1:])[:, None, None]
    ) * wetness[1:]
    return jnp.swapaxes(tridiagonal_pair(rhs_list, air_sea_link), 0, 1)


def on_device(
    atmos_flux, remap_blocks, row_owner, row_target, tracers, east_vel, north_vel, mix_kappa, levels
):
    lon_count = lax.axis_size("lon")
    lat_count = lax.axis_size("lat")
    dev_count = lon_count * lat_count
    atm_rows = atmos_flux.shape[0]
    flux_count = atmos_flux.shape[1]
    capacity = 2 * atm_rows // dev_count
    slot_total = dev_count * capacity
    depth_count = tracers.shape[1]
    rows_local = tracers.shape[2]
    cells_local = tracers.shape[3]
    blocks_wide = remap_blocks.astype(jnp.float32)
    contrib = jnp.einsum("rfp,rpc->rfc", atmos_flux, blocks_wide, precision=lax.Precision.HIGHEST)
    owner_dev = row_owner[:, 0]
    member = (owner_dev[:, None] == jnp.arange(dev_count, dtype=jnp.int32)[None, :]).astype(
        jnp.int32
    )
    earlier = jnp.cumsum(member, axis=0) - member
    rank_in = jnp.sum(earlier * member, axis=1)
    slot_pos = owner_dev * capacity + rank_in
    placing = (jnp.arange(slot_total, dtype=jnp.int32)[:, None] == slot_pos[None, :]).astype(
        jnp.float32
    )
    send_flux = jnp.dot(
        placing,
        contrib.reshape(atm_rows, flux_count * cells_local),
        precision=lax.Precision.HIGHEST,
    )
    send_tag = jnp.dot(
        placing, (row_target + 1).astype(jnp.float32), precision=lax.Precision.HIGHEST
    )
    got_flux, got_tag = (
        lax.all_to_all(
            send_flux.reshape(dev_count, capacity, flux_count * cells_local),
            ("lon", "lat"),
            split_axis=0,
            concat_axis=0,
            tiled=True,
        ),
        lax.all_to_all(
            send_tag.reshape(dev_count, capacity),
            ("lon", "lat"),
            split_axis=0,
            concat_axis=0,
            tiled=True,
        ),
    )
    got_flux = got_flux.reshape(slot_total, flux_count * cells_local)
    got_tag = got_tag.reshape(slot_total)
    row_labels = (jnp.arange(rows_local, dtype=jnp.int32) + 1).astype(jnp.float32)
    select = (got_tag[None, :] == row_labels[:, None]).astype(jnp.float32)
    forcing_rows = jnp.dot(select, got_flux, precision=lax.Precision.HIGHEST)
    forcing = tuple(
        (
            forcing_rows[:, flux_idx * cells_local : (flux_idx + 1) * cells_local]
            for flux_idx in range(flux_count)
        )
    )
    wetness = (jnp.arange(depth_count, dtype=jnp.int32)[:, None, None] < levels[None]).astype(
        jnp.float32
    )
    stacked = jnp.concatenate(
        [tracers.reshape(2 * depth_count, rows_local, cells_local), east_vel, north_vel, wetness], 0
    )
    side_ext = with_halo(stacked, (("lon", 2),), 1, True)
    whole_ext = with_halo(side_ext, (("lat", 1),), 1, False)
    ext_tracer = whole_ext[: 2 * depth_count].reshape(
        2, depth_count, rows_local + 2, cells_local + 2
    )
    ext_east = whole_ext[2 * depth_count : 3 * depth_count]
    ext_north = whole_ext[3 * depth_count : 4 * depth_count]
    ext_wet = whole_ext[4 * depth_count :]
    tracers_next = step_tracers(ext_tracer, ext_east, ext_north, ext_wet, forcing, mix_kappa)
    surface = jnp.concatenate([tracers_next[0, 0], tracers_next[1, 0]], 1)
    answer = jnp.einsum("ys,yk->sk", select, surface, precision=lax.Precision.HIGHEST)
    returned = lax.all_to_all(
        answer.reshape(dev_count, capacity, 2 * cells_local),
        ("lon", "lat"),
        split_axis=0,
        concat_axis=0,
        tiled=True,
    )
    returned = returned.reshape(slot_total, 2 * cells_local)
    own_rows = jnp.einsum("sr,sk->rk", placing, returned, precision=lax.Precision.HIGHEST)
    own_rows = own_rows.reshape(atm_rows, 2, cells_local)
    atmos_state = jnp.einsum("rfc,rpc->rfp", own_rows, blocks_wide, precision=lax.Precision.HIGHEST)
    return (tracers_next, atmos_state)


def solution(mesh):
    in_specs = (
        P(("lon", "lat"), None, None),
        P(("lon", "lat"), None, None),
        P(("lon", "lat"), None),
        P(("lon", "lat")),
        P(None, None, "lat", "lon"),
        P(None, "lat", "lon"),
        P(None, "lat", "lon"),
        P(None, "lat", "lon"),
        P("lat", "lon"),
    )
    out_specs = (P(None, None, "lat", "lon"), P(("lon", "lat"), None, None))
    return jax.shard_map(
        on_device, mesh=mesh, in_specs=in_specs, out_specs=out_specs, check_vma=False
    )
```

profile of v0, /device:TPU:1, one launch (start us, length us, event | category | flops | bytes accessed | tf_op | source)
XLA Modules:
  0.0 121.9 jit_solution(15754718425440353138)
XLA Ops:
  0.7 0.7 add_convert_fusion
  1.4 0.8 copy.90
  2.5 0.9 fusion.33
  3.3 0.7 multiply_add_fusion.7
  4.0 0.3 fusion.13
  4.4 0.7 all_to_all.12
  5.1 11.5 %all-to-all-start = ((f32[128,1,4]{2,1,0:T(1,128)}), f32[128,1,4]{2,1,0:T(1,128)S(1)}, u32[]{:S(2)}, u32[]{:S(2)}) async-start(f32[128,1,4]{2,1,0:T(1,128)} %bitcast.12), calls=%async_computation | async-start | bytes 131072 | tf_op jit(solution)/shard_map/all_to_all | solution.py:145
  16.6 0.7 fusion.35
  17.3 1.0 copy.70
  18.7 0.2 fusion.79
  18.9 0.9 copy.73
  19.8 1.1 collective-permute-start.1
  20.9 0.3 copy.72
  21.1 0.8 collective-permute-start
  21.9 0.7 multiply_exponential_fusion
  22.6 0.7 fusion.84
  23.2 1.3 %fusion.82 = (f32[1,32,128]{2,0,1:T(1,128)}, f32[1,32,128]{2,0,1:T(1,128)}, f32[1,32,128]{2,0,1:T(1,128)}, f32[1,32,128]{2,0,1:T(1,128)}, f32[1,32,128]{2,0,1:T(...) fusion(f32[8,32,128]{2,0,1:T(8,128)S(1)} %fusion.35, f32[]{:T(128)} %bitcast.48), kind=kLoop, calls=%fused_computation.183 | loop fusion | flops 4096 | bytes 262148 | tf_op jit(solution)/shard_map/slice | solution.py:87
  24.6 9.0 %fusion = f32[256,6,128]{2,1,0:T(8,128)S(1)} fusion(bf16[256,128,128]{2,1,0:T(8,128)(2,1)} %param.12, f32[256,6,128]{2,0,1:T(8,128)S(1)} %copy-done), kind=kOutput, calls=%fused_computation.2 | convolution fusion | flops 301989888 | bytes 9961472 | tf_op jit(solution)/shard_map/rfp,rpc->rfc/dot_general | solution.py:118
  33.5 0.3 copy.94
  33.9 0.9 fusion.16
  34.8 0.5 add_convert_fusion.1
  35.3 2.2 %copy.96 = f32[128,4,768]{2,1,0:T(4,128)} copy(f32[128,4,768]{2,0,1:T(8,128)S(1)} %fusion.16) | data formatting | bytes 3145728 | tf_op jit(solution)/shard_map/dot_general | solution.py:129
  37.5 0.6 copy-done.2
  38.1 12.6 %all-to-all-start.1 = ((f32[128,4,768]{2,1,0:T(4,128)}), f32[128,4,768]{2,1,0:T(4,128)S(1)}, u32[]{:S(2)}, u32[]{:S(2)}) async-start(f32[128,4,768]{2,1,0:T(4,128)} %copy.96), calls=%async_computation.1 | async-start | bytes 3145728 | tf_op jit(solution)/shard_map/all_to_all | solution.py:138
  50.7 0.5 broadcast.584
  51.2 1.6 %reduce.3 = f32[128,4]{1,0:T(8,128)S(1)} reduce(f32[128,1,4]{2,1,0:T(1,128)} %copy-done.2, f32[]{:T(128)} %broadcast.584), dimensions={1}, to_apply=%all_to_all.13.reduce_sub_computation.3 | reduce | bytes 4100 | tf_op jit(solution)/shard_map/all_to_all | solution.py:145
  52.9 0.7 eq.78
  53.6 0.3 copy.74
  53.9 1.0 copy.75
  55.2 3.3 %collective-permute-start.2 = (f32[40,1,130]{2,0,1:T(8,128)S(1)}, f32[40,1,130]{2,0,1:T(8,128)S(1)}, u32[]{:S(2)}, u32[]{:S(2)}) collective-permute-start(f32[40,1,130]{2,0,1:T(8,128)S(1)} %get-tuple-element.35), channel_id=1, source_target_pairs={{0,1},{1,2},{2,3},{4,5},{5,6},{6,7},{8,9},{9,10},{10,11},{12,13},{... | collective-permute-start | bytes 62408 | tf_op jit(solution)/shard_map/ppermute | solution.py:20
  58.5 1.5 %collective-permute-start.3 = (f32[40,1,130]{2,0,1:T(8,128)S(1)}, f32[40,1,130]{2,0,1:T(8,128)S(1)}, u32[]{:S(2)}, u32[]{:S(2)}) collective-permute-start(f32[40,1,130]{2,0,1:T(8,128)S(1)} %get-tuple-element.36), channel_id=1, source_target_pairs={{1,0},{2,1},{3,2},{5,4},{6,5},{7,6},{9,8},{10,9},{11,10},{13,12},{... | collective-permute-start | bytes 62408 | tf_op jit(solution)/shard_map/ppermute | solution.py:23
  60.3 6.9 %collective-permute-done.2 = f32[40,1,130]{2,0,1:T(8,128)S(1)} collective-permute-done((f32[40,1,130]{2,0,1:T(8,128)S(1)}, f32[40,1,130]{2,0,1:T(8,128)S(1)}, u32[]{:S(2)}, u32[]{:S(2)}) %collective-permute-start.2) | collective-permute-done | bytes 20832 | tf_op jit(solution)/shard_map/ppermute | solution.py:20
  67.2 2.8 %collective-permute-done.3 = f32[40,1,130]{2,0,1:T(8,128)S(1)} collective-permute-done((f32[40,1,130]{2,0,1:T(8,128)S(1)}, f32[40,1,130]{2,0,1:T(8,128)S(1)}, u32[]{:S(2)}, u32[]{:S(2)}) %collective-permute-start.3) | collective-permute-done | bytes 20832 | tf_op jit(solution)/shard_map/ppermute | solution.py:23
  70.3 0.3 fusion.9
  71.3 0.6 fusion.11
  72.1 4.4 %all-to-all-done.1 = f32[128,4,768]{2,1,0:T(4,128)S(1)} async-done(((f32[128,4,768]{2,1,0:T(4,128)}), f32[128,4,768]{2,1,0:T(4,128)S(1)}, u32[]{:S(2)}, u32[]{:S(2)}) %all-to-all-start.1) | async-done | bytes 1572896 | tf_op jit(solution)/shard_map/all_to_all | solution.py:138
  76.5 0.5 reshape.150
  77.2 1.5 %fusion.38 = f32[32,768]{1,0:T(8,128)S(1)} fusion(f32[512,768]{1,0:T(8,128)S(1)} %reshape.150, f32[512]{0:T(512)} %eq.78, f32[32]{0:T(128)} %add_convert_fusion.1), kind=kOutput, calls=%fused_computation.77 | convolution fusion | flops 151011328 | bytes 1673344 | tf_op jit(solution)/shard_map/dot_general | solution.py:157
  78.7 3.1 %bitcast_multiply_fusion = (f32[32,128]{1,0:T(8,128)S(1)}, f32[32,128]{1,0:T(8,128)S(1)}, f32[32,128]{1,0:T(8,128)S(1)}, f32[32,128]{1,0:T(8,128)S(1)}, f32[32,1...) fusion(f32[1,32,128]{2,1,0:T(8,128)S(1)} %bitcast.120, f32[32,768]{1,0:T(8,128)S(1)} %fusion.38, ...), kind=kLoop, calls=%fused_computation.144 | loop fusion | flops 53248 | bytes 245780 | tf_op jit(solution)/shard_map/mul | solution.py:87
  82.0 0.3 fusion.83
  82.3 1.3 %fusion.65 = (f32[32,128]{1,0:T(8,128)S(1)}, f32[32,128]{1,0:T(8,128)S(1)}, f32[32,128]{1,0:T(8,128)S(1)}) fusion(f32[32,768]{1,0:T(8,128)S(1)} %fusion.38, f32[1,32,128]{2,1,0:T(8,128)S(1)} %bitcast.119, f32[]{:T(128)} %bitcast.3, f32[1,32,128]{2,1,0:T(8,128)S(1)} %bitcast.118, f32[]{:T(128)} %bitcast.18), kind=kLoop, calls=%fused_computation.142 | loop fusion | flops 40960 | bytes 163848 | tf_op jit(solution)/shard_map/add | solution.py:89
  83.9 0.5 fusion.36
  84.4 1.0 reshape.151
  85.4 5.4 %all-to-all-start.2 = ((f32[128,4,256]{2,1,0:T(4,128)}), f32[128,4,256]{2,1,0:T(4,128)S(1)}, u32[]{:S(2)}, u32[]{:S(2)}) async-start(f32[128,4,256]{2,1,0:T(4,128)} %reshape.151), calls=%async_computation.2 | async-start | bytes 1048576 | tf_op jit(solution)/shard_map/all_to_all | solution.py:181
  90.9 0.7 copy.107
  91.6 13.4 %all-to-all-done.2 = f32[128,4,256]{2,1,0:T(4,128)S(1)} async-done(((f32[128,4,256]{2,1,0:T(4,128)}), f32[128,4,256]{2,1,0:T(4,128)S(1)}, u32[]{:S(2)}, u32[]{:S(2)}) %all-to-all-start.2) | async-done | bytes 524320 | tf_op jit(solution)/shard_map/all_to_all | solution.py:181
  105.4 0.5 fusion.14
  105.8 16.0 %fusion.24 = f32[256,2,128]{2,1,0:T(2,128)} fusion(bf16[256,128,128]{2,1,0:T(8,128)(2,1)} %param.12, f32[256,2,128]{2,0,1:T(8,128)S(1)} %fusion.14), kind=kOutput, calls=%fused_computation.42 | convolution fusion | flops 100663296 | bytes 8912896 | tf_op jit(solution)/shard_map/rfc,rpc->rfp/dot_general | solution.py:191
  (82 shorter events, 3.2 us)
Async XLA Ops:
  0.6 17.7 %copy-start.3 = (f32[8,32,128]{2,1,0:T(8,128)S(1)}, f32[8,32,128]{2,1,0:T(8,128)}, u32[]{:S(2)}) copy-start(f32[8,32,128]{2,1,0:T(8,128)} %param.17) | copy-start | bytes 393220
  0.6 17.8 %copy-start.1 = (f32[2,8,32,128]{3,2,1,0:T(8,128)S(1)}, f32[2,8,32,128]{3,2,1,0:T(8,128)}, u32[]{:S(2)}) copy-start(f32[2,8,32,128]{3,2,1,0:T(8,128)} %param.15) | copy-start | bytes 786436
  4.0 29.8 %copy-start.12 = (s32[256]{0:T(256)}, s32[256]{0:T(256)S(1)}, u32[]{:S(2)}) copy-start(s32[256]{0:T(256)S(1)} %multiply_add_fusion.7) | copy-start | bytes 3076
  5.1 32.4 %all-to-all-start = ((f32[128,1,4]{2,1,0:T(1,128)}), f32[128,1,4]{2,1,0:T(1,128)S(1)}, u32[]{:S(2)}, u32[]{:S(2)}) async-start(f32[128,1,4]{2,1,0:T(1,128)} %bitcast.12), calls=%async_computation | async-start | bytes 131072 | tf_op jit(solution)/shard_map/all_to_all | solution.py:145
  18.7 5.9 %copy-start = (f32[256,6,128]{2,0,1:T(8,128)S(1)}, f32[256,6,128]{2,0,1:T(8,128)}, u32[]{:S(2)}) copy-start(f32[256,6,128]{2,0,1:T(8,128)} %param.11) | copy-start | bytes 2359300
  19.8 34.1 %collective-permute-start.1 = (f32[40,32,1]{0,1,2:T(8,128)}, f32[40,32,1]{0,1,2:T(8,128)}, u32[]{:S(2)}, u32[]{:S(2)}) collective-permute-start(f32[40,32,1]{0,1,2:T(8,128)} %copy.73), channel_id=1, source_target_pairs={{4,0},{8,4},{12,8},{16,12},{20,16},{24,20},{28,24},{32,28},{36,32}... | collective-permute-start | bytes 15368 | tf_op jit(solution)/shard_map/ppermute | solution.py:23
  21.1 32.4 %collective-permute-start = (f32[40,32,1]{0,1,2:T(8,128)S(1)}, f32[40,32,1]{0,1,2:T(8,128)S(1)}, u32[]{:S(2)}, u32[]{:S(2)}) collective-permute-start(f32[40,32,1]{0,1,2:T(8,128)S(1)} %copy.72), channel_id=1, source_target_pairs={{0,4},{4,8},{8,12},{12,16},{16,20},{20,24},{24,28},{28,32},{32,36}... | collective-permute-start | bytes 15368 | tf_op jit(solution)/shard_map/ppermute | solution.py:20
  37.5 0.6 copy-start.2
  38.1 38.4 %all-to-all-start.1 = ((f32[128,4,768]{2,1,0:T(4,128)}), f32[128,4,768]{2,1,0:T(4,128)S(1)}, u32[]{:S(2)}, u32[]{:S(2)}) async-start(f32[128,4,768]{2,1,0:T(4,128)} %copy.96), calls=%async_computation.1 | async-start | bytes 3145728 | tf_op jit(solution)/shard_map/all_to_all | solution.py:138
  55.2 12.0 %collective-permute-start.2 = (f32[40,1,130]{2,0,1:T(8,128)S(1)}, f32[40,1,130]{2,0,1:T(8,128)S(1)}, u32[]{:S(2)}, u32[]{:S(2)}) collective-permute-start(f32[40,1,130]{2,0,1:T(8,128)S(1)} %get-tuple-element.35), channel_id=1, source_target_pairs={{0,1},{1,2},{2,3},{4,5},{5,6},{6,7},{8,9},{9,10},{10,11},{12,13},{... | collective-permute-start | bytes 62408 | tf_op jit(solution)/shard_map/ppermute | solution.py:20
  58.5 11.4 %collective-permute-start.3 = (f32[40,1,130]{2,0,1:T(8,128)S(1)}, f32[40,1,130]{2,0,1:T(8,128)S(1)}, u32[]{:S(2)}, u32[]{:S(2)}) collective-permute-start(f32[40,1,130]{2,0,1:T(8,128)S(1)} %get-tuple-element.36), channel_id=1, source_target_pairs={{1,0},{2,1},{3,2},{5,4},{6,5},{7,6},{9,8},{10,9},{11,10},{13,12},{... | collective-permute-start | bytes 62408 | tf_op jit(solution)/shard_map/ppermute | solution.py:23
  77.1 1.6 %copy-start.5 = (f32[1,32,128]{2,0,1:T(1,128)S(1)}, f32[1,32,128]{2,0,1:T(1,128)}, u32[]{:S(2)}) copy-start(f32[1,32,128]{2,0,1:T(1,128)} %get-tuple-element.44) | copy-start | bytes 49156
  77.1 1.6 %copy-start.6 = (f32[1,32,128]{2,0,1:T(1,128)S(1)}, f32[1,32,128]{2,0,1:T(1,128)}, u32[]{:S(2)}) copy-start(f32[1,32,128]{2,0,1:T(1,128)} %get-tuple-element.45) | copy-start | bytes 49156
  77.1 1.6 %copy-start.7 = (f32[1,32,128]{2,0,1:T(1,128)S(1)}, f32[1,32,128]{2,0,1:T(1,128)}, u32[]{:S(2)}) copy-start(f32[1,32,128]{2,0,1:T(1,128)} %get-tuple-element.46) | copy-start | bytes 49156
  77.1 1.6 %copy-start.8 = (f32[1,32,128]{2,0,1:T(1,128)S(1)}, f32[1,32,128]{2,0,1:T(1,128)}, u32[]{:S(2)}) copy-start(f32[1,32,128]{2,0,1:T(1,128)} %get-tuple-element.47) | copy-start | bytes 49156
  77.1 1.6 %copy-start.9 = (f32[1,32,128]{2,0,1:T(1,128)S(1)}, f32[1,32,128]{2,0,1:T(1,128)}, u32[]{:S(2)}) copy-start(f32[1,32,128]{2,0,1:T(1,128)} %get-tuple-element.48) | copy-start | bytes 49156
  77.1 1.6 %copy-start.10 = (f32[1,32,128]{2,0,1:T(1,128)S(1)}, f32[1,32,128]{2,0,1:T(1,128)}, u32[]{:S(2)}) copy-start(f32[1,32,128]{2,0,1:T(1,128)} %get-tuple-element.51) | copy-start | bytes 49156
  77.1 4.7 %slice-start = ((f32[8,32,128]{2,1,0:T(8,128)}), f32[7,32,128]{2,1,0:T(8,128)S(1)}, s32[]{:S(2)}) async-start(f32[8,32,128]{2,1,0:T(8,128)} %param.18), calls=%async_computation.3 | async-start | bytes 229376 | tf_op jit(solution)/shard_map/slice | solution.py:99
  77.1 4.7 %copy-start.16 = (f32[7]{0:T(128)S(1)}, f32[7]{0:T(128)}, u32[]{:S(2)}) copy-start(f32[7]{0:T(128)} %multiply_exponential_fusion) | copy-start | bytes 88
  77.2 5.1 %copy-start.4 = (f32[1,32,128]{2,0,1:T(1,128)S(1)}, f32[1,32,128]{2,0,1:T(1,128)}, u32[]{:S(2)}) copy-start(f32[1,32,128]{2,0,1:T(1,128)} %get-tuple-element.50) | copy-start | bytes 49156
  77.2 6.4 %copy-start.15 = (f32[2]{0:T(128)S(1)}, f32[2]{0:T(128)}, u32[]{:S(2)}) copy-start(f32[2]{0:T(128)} %constant.8.clone) | copy-start | bytes 28
  82.0 2.0 %copy-start.11 = (f32[512]{0:T(512)S(1)}, f32[512]{0:T(512)}, u32[]{:S(2)}) copy-start(f32[512]{0:T(512)} %eq.78) | copy-start | bytes 6148
  82.0 2.0 %copy-start.14 = (f32[32]{0:T(128)S(1)}, f32[32]{0:T(128)}, u32[]{:S(2)}) copy-start(f32[32]{0:T(128)} %add_convert_fusion.1) | copy-start | bytes 388
  85.4 19.6 %all-to-all-start.2 = ((f32[128,4,256]{2,1,0:T(4,128)}), f32[128,4,256]{2,1,0:T(4,128)S(1)}, u32[]{:S(2)}, u32[]{:S(2)}) async-start(f32[128,4,256]{2,1,0:T(4,128)} %reshape.151), calls=%async_computation.2 | async-start | bytes 1048576 | tf_op jit(solution)/shard_map/all_to_all | solution.py:181
  90.8 14.5 %copy-start.13 = (s32[256]{0:T(256)S(1)}, s32[256]{0:T(256)}, u32[]{:S(2)}) copy-start(s32[256]{0:T(256)} %copy-done.12) | copy-start | bytes 3076
where the time goes:
time: 123 us; the launch traced here: 122 us
  starting transfers between devices  36.1 us (29%)
  matrix products  28.6 us (23%)
  waiting for transfers between devices  27.4 us (22%)
  other arithmetic  14.3 us (12%)
  local copies, waits for them, and re-layouts  14.2 us (12%)
  between operations  1.27 us (1%)
    dot_general x1, matrix products, on_device(): jnp.einsum('rfc,rpc->rfp', own_rows, blocks_wide, precision=lax.Precision...  16 us
    all_to_all x1, waiting for transfers between devices, on_device(): lax.all_to_all(answer.reshape(dev_count, capacity, 2 * cells_local), ('lo...  13.4 us
    all_to_all x1, starting transfers between devices, on_device(): lax.all_to_all(send_flux.reshape(dev_count, capacity, flux_count * cells_...  12.6 us
    all_to_all x1, starting transfers between devices, on_device(): lax.all_to_all(send_tag.reshape(dev_count, capacity), ('lon', 'lat'), spl...  11.5 us
    dot_general x1, matrix products, on_device(): jnp.einsum('rfp,rpc->rfc', atmos_flux, blocks_wide, precision=lax.Precisi...  8.96 us
    ppermute x2, waiting for transfers between devices, with_halo(): lax.ppermute(lax.slice_in_dim(block, block.shape[dim] - width, None, axis...  6.87 us
    all_to_all x1, starting transfers between devices, on_device(): lax.all_to_all(answer.reshape(dev_count, capacity, 2 * cells_local), ('lo...  5.42 us
    all_to_all x1, waiting for transfers between devices, on_device(): lax.all_to_all(send_flux.reshape(dev_count, capacity, flux_count * cells_...  4.38 us
  transfers between devices with their start and end apart: 7, of which 4 were waited for; matrix products, arithmetic and copies ran while one was open for 22% of the time, Pallas kernels for 0%

commit v1 on v0

v1 whole, which is shorter than its diff:
```python
import math

import jax
import jax.numpy as jnp
from jax import lax
from jax.experimental import pallas as pl
from jax.experimental.pallas import tpu as pltpu
from jax.sharding import PartitionSpec as P

F32 = jnp.float32
BF16 = jnp.bfloat16

ROWS = 256
DEV = 128
CAP = 4
CELLS = 128
SENT = 4
BLOCK = CAP * SENT + 1
LEV = 8
CY = 32
CHUNKS = 8
PER = ROWS // CHUNKS

VMEM = pltpu.VMEM
SMEM = pltpu.SMEM


def split(x):
    high = x.astype(BF16)
    return high, (x - high.astype(F32)).astype(BF16)


def iota(shape, axis):
    return lax.broadcasted_iota(jnp.int32, shape, axis)


def params(mib):
    return pltpu.CompilerParams(vmem_limit_bytes=mib * 1024 * 1024)


def vmem_specs(count):
    return [pl.BlockSpec(memory_space=VMEM)] * count


def contrib_kernel(owner, target, flux_hbm, remap_hbm, send, slot_out, weights, flux, fields, slot_v, slot_s, sems, sem2):
    chunk_copies = [
        pltpu.make_async_copy(
            remap_hbm.at[pl.ds(c * PER, PER)], weights.at[pl.ds(c * PER, PER)], sems.at[c]
        )
        for c in range(CHUNKS)
    ]
    flux_copy = pltpu.make_async_copy(flux_hbm, flux, sem2.at[0])
    flux_copy.start()
    for copy in chunk_copies:
        copy.start()

    dev_iota = iota((DEV, 128), 0)
    own = owner[...]
    tgt = target[...].astype(F32) + 1.0
    member = jnp.concatenate(
        [(own[h : h + 1, :] == dev_iota).astype(F32) for h in range(2)], axis=1
    )
    before = (iota((ROWS, ROWS), 0) < iota((ROWS, ROWS), 1)).astype(BF16)
    earlier = jnp.dot(member.astype(BF16), before, preferred_element_type=F32)
    rank = jnp.sum(member * earlier, axis=0, keepdims=True)
    rank_i = rank.astype(jnp.int32)
    for h in range(2):
        slot_v[h : h + 1, :] = own[h : h + 1, :] * BLOCK + rank_i[:, h * 128 : (h + 1) * 128] * SENT
        slot_out[h : h + 1, :] = own[h : h + 1, :] * (2 * CAP) + rank_i[:, h * 128 : (h + 1) * 128] * 2
    slot_copy = pltpu.make_async_copy(slot_v, slot_s, sem2.at[1])
    slot_copy.start()
    tgt_row = jnp.concatenate([tgt[0:1, :], tgt[1:2, :]], axis=1)
    slot_tags = jnp.where(iota((DEV, ROWS), 0) == rank_i, tgt_row, 0.0).astype(BF16)
    tags = lax.dot_general(
        member.astype(BF16), slot_tags, (((1,), (1,)), ((), ())), preferred_element_type=F32
    )
    send[...] = jnp.zeros_like(send)
    send[pl.ds(CAP * SENT, DEV, stride=BLOCK), :] = tags

    flux_copy.wait()
    fields[pl.ds(0, ROWS, stride=SENT), :] = flux[0]
    fields[pl.ds(1, ROWS, stride=SENT), :] = flux[1] + flux[2] + flux[3]
    fields[pl.ds(2, ROWS, stride=SENT), :] = flux[4]
    fields[pl.ds(3, ROWS, stride=SENT), :] = flux[5]
    slot_copy.wait()

    def pair(r):
        high, low = split(fields[pl.ds(pl.multiple_of(r * SENT, 8), 8), :])
        left = jnp.concatenate([high, low], axis=0)
        right = jnp.concatenate([weights[r], weights[r + 1]], axis=1)
        both = jnp.dot(left, right, preferred_element_type=F32)
        both = both[:8] + both[8:]
        first = slot_s[r // 128, r % 128]
        second = slot_s[(r + 1) // 128, (r + 1) % 128]
        send[pl.ds(first, SENT), :] = both[:4, :CELLS]
        send[pl.ds(second, SENT), :] = both[4:, CELLS:]

    def chunk(c, carry):
        pltpu.make_async_copy(
            remap_hbm.at[pl.ds(c * PER, PER)], weights.at[pl.ds(c * PER, PER)], sems.at[c]
        ).wait()
        for i in range(0, PER, 2):
            pair(c * PER + i)
        return carry

    lax.fori_loop(0, CHUNKS, chunk, 0)


def contributions(row_owner, row_target, flux, remap):
    return pl.pallas_call(
        contrib_kernel,
        out_shape=(
            jax.ShapeDtypeStruct((DEV * BLOCK, CELLS), F32),
            jax.ShapeDtypeStruct((2, 128), jnp.int32),
        ),
        in_specs=vmem_specs(2) + [pl.BlockSpec(memory_space=pl.ANY)] * 2,
        out_specs=tuple(vmem_specs(2)),
        scratch_shapes=[
            VMEM((ROWS, 128, 128), BF16),
            VMEM((6, ROWS, 128), F32),
            VMEM((ROWS * SENT, 128), F32),
            VMEM((2, 128), jnp.int32),
            SMEM((2, 128), jnp.int32),
            pltpu.SemaphoreType.DMA((CHUNKS,)),
            pltpu.SemaphoreType.DMA((2,)),
        ],
        compiler_params=params(24),
        cost_estimate=pl.CostEstimate(flops=10**9, bytes_accessed=10_000_000, transcendentals=0),
        name="contrib",
    )(row_owner, row_target, flux, remap)


def edge_kernel(tracers, east_vel, north_vel, levels, to_east, to_west, to_north, to_south):
    lev = levels[...].astype(F32)
    lane = iota((CY, 128), 1)
    zero = jnp.zeros((CY, 128), F32)
    east, west = zero, zero
    planes = [tracers[p] for p in range(16)] + [lev] + [east_vel[k] for k in range(LEV)]
    for p, plane in enumerate(planes):
        east = jnp.where(lane == p, pltpu.roll(plane, (p + 1) % 128, 1), east)
        if p < 17:
            west = jnp.where(lane == p, plane if p == 0 else pltpu.roll(plane, p, 1), west)
    to_east[...] = east
    to_west[...] = west
    to_north[...] = zero
    to_south[...] = zero
    for p in range(16):
        to_north[p : p + 1, :] = tracers[p, CY - 1 : CY, :]
        to_south[p : p + 1, :] = tracers[p, 0:1, :]
    to_north[16:17, :] = lev[CY - 1 : CY]
    to_south[16:17, :] = lev[0:1]
    for k in range(LEV):
        to_north[17 + k : 18 + k, :] = north_vel[k, CY - 1 : CY, :]


def edges(tracers, east_vel, north_vel, levels):
    return pl.pallas_call(
        edge_kernel,
        out_shape=tuple(jax.ShapeDtypeStruct((CY, 128), F32) for _ in range(4)),
        in_specs=vmem_specs(4),
        out_specs=tuple(vmem_specs(4)),
        compiler_params=params(8),
        cost_estimate=pl.CostEstimate(flops=10**5, bytes_accessed=1_000_000, transcendentals=0),
        name="edges",
    )(tracers, east_vel, north_vel, levels)


def advect_kernel(tracers, east_vel, north_vel, levels, west_in, east_in, south_in, north_in, out):
    lane0 = iota((CY, 128), 1) == 0
    lane_last = iota((CY, 128), 1) == 127
    row0 = iota((CY, 128), 0) == 0
    row_last = iota((CY, 128), 0) == CY - 1
    lev = levels[...].astype(F32)

    def from_west(p):
        return west_in[...] if p == 0 else pltpu.roll(west_in[...], 128 - p, 1)

    def from_east(p):
        return pltpu.roll(east_in[...], 127 - p, 1)

    lev_w = from_west(16)
    lev_e = jnp.where(lane_last, from_east(16), pltpu.roll(lev, 127, 1))
    lev_s = south_in[16:17, :]
    lev_n = jnp.where(row_last, north_in[16:17, :], pltpu.roll(lev, CY - 1, 0))
    for k in range(LEV):
        depth = float(k)
        wet = (lev > depth).astype(F32)
        wet_w = wet * (lev_w > depth).astype(F32)
        wet_e = wet * (lev_e > depth).astype(F32)
        wet_s = wet * (lev_s > depth).astype(F32)
        wet_n = wet * (lev_n > depth).astype(F32)
        vel_e, vel_n = east_vel[k], north_vel[k]
        vel_w, vel_s = from_west(17 + k), south_in[17 + k : 18 + k, :]
        e_pos, e_neg = jnp.maximum(vel_e, 0.0), jnp.minimum(vel_e, 0.0)
        n_pos, n_neg = jnp.maximum(vel_n, 0.0), jnp.minimum(vel_n, 0.0)
        w_pos, w_neg = jnp.maximum(vel_w, 0.0), jnp.minimum(vel_w, 0.0)
        s_pos, s_neg = jnp.maximum(vel_s, 0.0), jnp.minimum(vel_s, 0.0)
        for t in range(2):
            p = t * LEV + k
            here = tracers[p]
            at_e = jnp.where(lane_last, from_east(p), pltpu.roll(here, 127, 1))
            at_n = jnp.where(row_last, north_in[p : p + 1, :], pltpu.roll(here, CY - 1, 0))
            flux_e = (e_pos * here + e_neg * at_e) * wet_e
            flux_n = (n_pos * here + n_neg * at_n) * wet_n
            edge_w = (w_pos * from_west(p) + w_neg * here) * wet_w
            edge_s = (s_pos * south_in[p : p + 1, :] + s_neg * here) * wet_s
            flux_w = jnp.where(lane0, edge_w, pltpu.roll(flux_e, 1, 1))
            flux_s = jnp.where(row0, edge_s, pltpu.roll(flux_n, 1, 0))
            out[p] = here - (flux_e - flux_w) - (flux_n - flux_s)


def advected(*args):
    return pl.pallas_call(
        advect_kernel,
        out_shape=jax.ShapeDtypeStruct((16, CY, 128), F32),
        in_specs=vmem_specs(8),
        out_specs=pl.BlockSpec(memory_space=VMEM),
        compiler_params=params(8),
        cost_estimate=pl.CostEstimate(flops=10**6, bytes_accessed=2_000_000, transcendentals=0),
        name="advect",
    )(*args)


def ocean_kernel(got, carried, kappa, levels, after, answer):
    tags = jnp.transpose(got[pl.ds(CAP * SENT, DEV, stride=BLOCK), :])
    labels = iota((CY, DEV), 0).astype(F32) + 1.0
    select = jnp.concatenate(
        [(tags[s : s + 1, :] == labels).astype(F32) for s in range(CAP)], axis=1
    ).astype(BF16)
    forcing = []
    for f in range(SENT):
        rows = jnp.concatenate(
            [got[pl.ds(s * SENT + f, DEV, stride=BLOCK), :] for s in range(CAP)], axis=0
        )
        high, low = split(rows)
        both = jnp.dot(select, jnp.concatenate([high, low], axis=1), preferred_element_type=F32)
        forcing.append(both[:, :CELLS] + both[:, CELLS:])
    short, surface_heat, fresh, wind = forcing
    lev = levels[...]
    stirring = 0.25 * wind * wind
    wet = [(lev > k).astype(F32) for k in range(LEV)]
    link = [None] + [
        (kappa[k] + stirring * math.exp(-0.5 * k)) * wet[k] for k in range(1, LEV)
    ]
    gains, offsets = [], []
    for k in range(LEV):
        fraction = math.exp(-0.5 * k) - math.exp(-0.5 * (k + 1))
        heat = wet[k] * (fraction * short)
        warmth, salt = carried[k] + heat, carried[LEV + k]
        if k == 0:
            warmth = warmth + 0.5 * wet[0] * surface_heat
            salt = salt + 0.5 * wet[0] * fresh
        diagonal = 1.0 if k == 0 else 1.0 + link[k]
        if k < LEV - 1:
            diagonal = diagonal + link[k + 1]
        if k > 0:
            diagonal = diagonal - link[k] * gains[-1]
            warmth = warmth + link[k] * offsets[-1][0]
            salt = salt + link[k] * offsets[-1][1]
        inverse = 1.0 / diagonal
        if k < LEV - 1:
            gains.append(link[k + 1] * inverse)
        offsets.append((warmth * inverse, salt * inverse))
    warmth, salt = offsets[-1]
    after[LEV - 1], after[2 * LEV - 1] = warmth, salt
    for k in range(LEV - 2, -1, -1):
        warmth = offsets[k][0] + gains[k] * warmth
        salt = offsets[k][1] + gains[k] * salt
        after[k], after[LEV + k] = warmth, salt
    high, low = split(jnp.concatenate([warmth, salt], axis=1))
    picked = lax.dot_general(
        select,
        jnp.concatenate([high, low], axis=1),
        (((0,), (0,)), ((), ())),
        preferred_element_type=F32,
    )
    for s in range(CAP):
        for f in range(2):
            rows = picked[s * DEV : (s + 1) * DEV]
            answer[:, 2 * s + f, :] = (
                rows[:, f * CELLS : (f + 1) * CELLS] + rows[:, (2 + f) * CELLS : (3 + f) * CELLS]
            )


def ocean(got, carried, kappa, levels):
    return pl.pallas_call(
        ocean_kernel,
        out_shape=(
            jax.ShapeDtypeStruct((16, CY, 128), F32),
            jax.ShapeDtypeStruct((DEV, 2 * CAP, CELLS), F32),
        ),
        in_specs=vmem_specs(4),
        out_specs=tuple(vmem_specs(2)),
        compiler_params=params(24),
        cost_estimate=pl.CostEstimate(flops=10**8, bytes_accessed=4_000_000, transcendentals=0),
        name="ocean",
    )(got, carried, kappa, levels)


def state_kernel(slots, returned, remap_hbm, out, weights, rows, sems):
    for c in range(CHUNKS):
        pltpu.make_async_copy(
            remap_hbm.at[pl.ds(c * PER, PER)], weights.at[pl.ds(c * PER, PER)], sems.at[c]
        ).start()

    def gather(g, carry):
        for i in range(16):
            r = g * 16 + i
            rows[pl.ds(2 * r, 2), :] = returned[pl.ds(slots[r // 128, r % 128], 2), :]
        return carry

    lax.fori_loop(0, ROWS // 16, gather, 0)

    def chunk(c, carry):
        pltpu.make_async_copy(
            remap_hbm.at[pl.ds(c * PER, PER)], weights.at[pl.ds(c * PER, PER)], sems.at[c]
        ).wait()
        for i in range(0, PER, 4):
            r = c * PER + i
            high, low = split(rows[pl.ds(pl.multiple_of(2 * r, 8), 8), :])
            left = jnp.concatenate([high, low], axis=0)
            right = weights[pl.ds(r, 4)].reshape(4 * 128, 128)
            four = lax.dot_general(
                left, right, (((1,), (1,)), ((), ())), preferred_element_type=F32
            )
            four = four[:8] + four[8:]
            for j in range(4):
                out[r + j] = four[2 * j : 2 * j + 2, j * 128 : (j + 1) * 128]
        return carry

    lax.fori_loop(0, CHUNKS, chunk, 0)


def state(slots, returned, remap):
    return pl.pallas_call(
        state_kernel,
        out_shape=jax.ShapeDtypeStruct((ROWS, 2, 128), F32),
        in_specs=[
            pl.BlockSpec(memory_space=SMEM),
            pl.BlockSpec(memory_space=VMEM),
            pl.BlockSpec(memory_space=pl.ANY),
        ],
        out_specs=pl.BlockSpec(memory_space=VMEM),
        scratch_shapes=[
            VMEM((ROWS, 128, 128), BF16),
            VMEM((2 * ROWS, 128), F32),
            pltpu.SemaphoreType.DMA((CHUNKS,)),
        ],
        compiler_params=params(24),
        cost_estimate=pl.CostEstimate(flops=10**9, bytes_accessed=9_000_000, transcendentals=0),
        name="state",
    )(slots, returned, remap)


def shifts(count, wraps):
    up = [(i, i + 1) for i in range(count - 1)] + ([(count - 1, 0)] if wraps else [])
    return up, [(b, a) for a, b in up]


def on_device(
    atmos_flux, remap_blocks, row_owner, row_target, tracers, east_vel, north_vel, mix_kappa, levels
):
    axes = ("lon", "lat")
    planes = tracers.reshape(2 * LEV, CY, CELLS)
    to_east, to_west, to_north, to_south = edges(planes, east_vel, north_vel, levels)
    eastward, westward = shifts(lax.axis_size("lon"), True)
    northward, southward = shifts(lax.axis_size("lat"), False)
    west_in = lax.ppermute(to_east, "lon", eastward)
    east_in = lax.ppermute(to_west, "lon", westward)
    south_in = lax.ppermute(to_north, "lat", northward)
    north_in = lax.ppermute(to_south, "lat", southward)
    send, slots = contributions(
        row_owner.reshape(2, 128),
        row_target.reshape(2, 128),
        jnp.transpose(atmos_flux, (1, 0, 2)),
        remap_blocks,
    )
    got = lax.all_to_all(
        send.reshape(DEV, BLOCK, 1, CELLS), axes, split_axis=0, concat_axis=0, tiled=True
    )
    carried = advected(planes, east_vel, north_vel, levels, west_in, east_in, south_in, north_in)
    after, answer = ocean(got.reshape(DEV * BLOCK, CELLS), carried, mix_kappa, levels)
    returned = lax.all_to_all(answer, axes, split_axis=0, concat_axis=0, tiled=True)
    atmos_state = state(slots, returned.reshape(DEV * 2 * CAP, CELLS), remap_blocks)
    return after.reshape(2, LEV, CY, CELLS), atmos_state


def solution(mesh):
    row = ("lon", "lat")
    in_specs = (
        P(row, None, None),
        P(row, None, None),
        P(row, None),
        P(row),
        P(None, None, "lat", "lon"),
        P(None, "lat", "lon"),
        P(None, "lat", "lon"),
        P(None, "lat", "lon"),
        P("lat", "lon"),
    )
    out_specs = (P(None, None, "lat", "lon"), P(row, None, None))
    return jax.shard_map(
        on_device, mesh=mesh, in_specs=in_specs, out_specs=out_specs, check_vma=False
    )
```

time: 123 us -> 73.3 us (0.60)
  matrix products: 28.6 us -> 0 us
  starting transfers between devices: 36.1 us -> 17.7 us
  blocking collectives: 0 us -> 17.9 us
  other arithmetic: 14.3 us -> 0 us
  waiting for transfers between devices: 27.4 us -> 13.1 us
  Pallas kernels: 0 us -> 14.1 us
  local copies, waits for them, and re-layouts: 14.2 us -> 9.28 us
    dot_general x7 -> x0, matrix products: 28.6 us -> none  [the longest x1 16 us: on_device(): jnp.einsum('rfc,rpc->rfp', own_rows, blocks_wide, precision=lax.Precision...]
    all_to_all x3 -> x1, starting transfers between devices: 29.5 us -> 11.5 us  [on_device(): lax.all_to_all(send.reshape(DEV, BLOCK, 1, CELLS), axes, split_axis=0, co...]
    all_to_all x0 -> x1, blocking collectives: none -> 17.9 us  [on_device(): lax.all_to_all(answer, axes, split_axis=0, concat_axis=0, tiled=True)]
    pallas_call x0 -> x5, Pallas kernels: none -> 14.1 us  [the longest x1 6.92 us: state(): pl.pallas_call(state_kernel, out_shape=jax.ShapeDtypeStruct((ROWS, 2, 128...]
    all_to_all x3 -> x1, waiting for transfers between devices: 17.8 us -> 5.82 us  [on_device(): lax.all_to_all(send.reshape(DEV, BLOCK, 1, CELLS), axes, split_axis=0, co...]
    unnamed x41 -> x20, local copies, waits for them, and re-layouts: 2.52 us -> 9.28 us
    mul x5 -> x0, other arithmetic: 4.18 us -> none  [the longest x1 3.14 us: step_tracers(): heat_level = wetness[level_idx] * sw_fraction[level_idx] * forcing[0]]
    slice x9 -> x0, local copies, waits for them, and re-layouts: 2.61 us -> none  [the longest x1 0.89 us: with_halo(): lax.slice_in_dim(block, 0, width, axis=dim)]
  transfers between devices with their start and end apart: 7 -> 5, of which waited for: 4 -> 4; matrix products, arithmetic and copies ran while one was open for 22% -> 0% of each run, Pallas kernels for 0% -> 2%
where the time goes in v1:
time: 73.3 us; the launch traced here: 72.9 us
  blocking collectives  17.9 us (24%)
  starting transfers between devices  17.7 us (24%)
  Pallas kernels  14.1 us (19%)
  waiting for transfers between devices  13.1 us (18%)
  local copies, waits for them, and re-layouts  9.28 us (13%)
  between operations  0.77 us (1%)
    all_to_all x1, blocking collectives, on_device(): lax.all_to_all(answer, axes, split_axis=0, concat_axis=0, tiled=True)  17.9 us
    all_to_all x1, starting transfers between devices, on_device(): lax.all_to_all(send.reshape(DEV, BLOCK, 1, CELLS), axes, split_axis=0, co...  11.5 us
    unnamed x20, local copies, waits for them, and re-layouts  9.28 us
    pallas_call x1, Pallas kernels, state(): pl.pallas_call(state_kernel, out_shape=jax.ShapeDtypeStruct((ROWS, 2, 128...  6.92 us
    all_to_all x1, waiting for transfers between devices, on_device(): lax.all_to_all(send.reshape(DEV, BLOCK, 1, CELLS), axes, split_axis=0, co...  5.82 us
    pallas_call x1, Pallas kernels, contributions(): pl.pallas_call(contrib_kernel, out_shape=(jax.ShapeDtypeStruct((DEV * BLO...  4.83 us
    ppermute x1, waiting for transfers between devices, on_device(): south_in = lax.ppermute(to_north, 'lat', northward)  3.53 us
    ppermute x1, starting transfers between devices, on_device(): south_in = lax.ppermute(to_north, 'lat', northward)  3.09 us
  transfers between devices with their start and end apart: 5, of which 4 were waited for; matrix products, arithmetic and copies ran while one was open for 0% of the time, Pallas kernels for 2%

profile of v1, /device:TPU:1, one launch (start us, length us, event | category | flops | bytes accessed | tf_op | source)
XLA Modules:
  0.0 72.9 jit_solution(6965223500892020265)
XLA Ops:
  0.6 0.0 copy-start
  0.6 3.4 %copy-done = bf16[256,128,128]{2,1,0:T(8,128)(2,1)S(1)} copy-done((bf16[256,128,128]{2,1,0:T(8,128)(2,1)S(1)}, bf16[256,128,128]{2,1,0:T(8,128)(2,1)}, u32[]{:S(2)}) %copy-start) | copy-done | bytes 8388632
  4.0 0.0 copy-start.3
  4.0 1.1 %copy-done.3 = f32[256,6,128]{2,0,1:T(8,128)S(1)} copy-done((f32[256,6,128]{2,0,1:T(8,128)S(1)}, f32[256,6,128]{2,0,1:T(8,128)}, u32[]{:S(2)}) %copy-start.3) | copy-done | bytes 786456
  5.1 0.0 copy-start.8
  5.2 0.7 copy-done.8
  5.8 0.0 copy-start.9
  5.8 0.7 copy-done.9
  6.5 4.8 %contrib.1 = (f32[2176,128]{1,0:T(8,128)}, s32[2,128]{1,0:T(2,128)S(1)}) custom-call(s32[2,128]{1,0:T(2,128)S(1)} %bitcast.13, s32[2,128]{1,0:T(2,128)S(1)} %bitcast.14, f32[6,256,128]{2,1,0:T(8,128)S(1)} %bitcast.12, bf16[256,128,128]{2,1,0:T(8,128)(2,1)S(1)} %copy-done), custom_call_target="tpu_custom_call" | custom-call | flops 1000000000 | bytes 10000000 | tf_op jit(solution)/shard_map/contrib/pallas_call | solution.py:110
  11.3 0.0 copy-start.2
  11.4 0.0 copy-start.4
  11.4 0.0 copy-start.5
  11.4 0.0 copy-start.6
  11.4 11.5 %all-to-all-start = ((f32[128,17,1,128]{3,2,1,0:T(1,128)}), f32[128,17,1,128]{3,2,1,0:T(1,128)S(1)}, u32[]{:S(2)}, u32[]{:S(2)}) async-start(f32[128,17,1,128]{3,2,1,0:T(1,128)} %bitcast.3), calls=%async_computation | async-start | bytes 2228224 | tf_op jit(solution)/shard_map/all_to_all | solution.py:378
  22.9 0.0 copy-start.7
  22.9 0.0 copy-done.2
  22.9 0.0 copy-done.4
  22.9 0.0 copy-done.5
  22.9 0.0 copy-done.6
  23.0 0.2 edges.1
  23.2 1.8 %collective-permute-start = (f32[32,128]{1,0:T(8,128)S(1)}, f32[32,128]{1,0:T(8,128)S(1)}, u32[]{:S(2)}, u32[]{:S(2)}) collective-permute-start(f32[32,128]{1,0:T(8,128)S(1)} %get-tuple-element.11), channel_id=1, source_target_pairs={{0,4},{4,8},{8,12},{12,16},{16,20},{20,24},{24,28},{28,32},{32,36}... | collective-permute-start | bytes 49160 | tf_op jit(solution)/shard_map/ppermute | solution.py:368
  25.0 0.0 collective-permute-start.1
  25.0 3.1 %collective-permute-start.2 = (f32[32,128]{1,0:T(8,128)S(1)}, f32[32,128]{1,0:T(8,128)S(1)}, u32[]{:S(2)}, u32[]{:S(2)}) collective-permute-start(f32[32,128]{1,0:T(8,128)S(1)} %get-tuple-element.13), channel_id=1, source_target_pairs={{0,1},{1,2},{2,3},{4,5},{5,6},{6,7},{8,9},{9,10},{10,11},{12,13},{... | collective-permute-start | bytes 49160 | tf_op jit(solution)/shard_map/ppermute | solution.py:370
  28.1 1.3 %collective-permute-start.3 = (f32[32,128]{1,0:T(8,128)S(1)}, f32[32,128]{1,0:T(8,128)S(1)}, u32[]{:S(2)}, u32[]{:S(2)}) collective-permute-start(f32[32,128]{1,0:T(8,128)S(1)} %get-tuple-element.14), channel_id=1, source_target_pairs={{1,0},{2,1},{3,2},{5,4},{6,5},{7,6},{9,8},{10,9},{11,10},{13,12},{... | collective-permute-start | bytes 49160 | tf_op jit(solution)/shard_map/ppermute | solution.py:371
  29.4 0.0 collective-permute-done.west_in
  29.4 0.9 %collective-permute-done.1.east_in = f32[32,128]{1,0:T(8,128)S(1)} collective-permute-done((f32[32,128]{1,0:T(8,128)S(1)}, f32[32,128]{1,0:T(8,128)S(1)}, u32[]{:S(2)}, u32[]{:S(2)}) %collective-permute-start.1) | collective-permute-done | bytes 16416 | tf_op jit(solution)/shard_map/ppermute | solution.py:369
  30.4 3.5 %collective-permute-done.2.south_in = f32[32,128]{1,0:T(8,128)S(1)} collective-permute-done((f32[32,128]{1,0:T(8,128)S(1)}, f32[32,128]{1,0:T(8,128)S(1)}, u32[]{:S(2)}, u32[]{:S(2)}) %collective-permute-start.2) | collective-permute-done | bytes 16416 | tf_op jit(solution)/shard_map/ppermute | solution.py:370
  33.9 2.8 %collective-permute-done.3.north_in = f32[32,128]{1,0:T(8,128)S(1)} collective-permute-done((f32[32,128]{1,0:T(8,128)S(1)}, f32[32,128]{1,0:T(8,128)S(1)}, u32[]{:S(2)}, u32[]{:S(2)}) %collective-permute-start.3) | collective-permute-done | bytes 16416 | tf_op jit(solution)/shard_map/ppermute | solution.py:371
  36.7 1.0 %advect.1.carried = f32[16,32,128]{2,1,0:T(8,128)S(1)} custom-call(f32[16,32,128]{2,1,0:T(8,128)S(1)} %bitcast.11, f32[8,32,128]{2,1,0:T(8,128)S(1)} %copy-done.4, f32[8,32,128]{2,1,0:T(8,128)S(1)} %copy-done.5, s32[32,128]{1,0:T(8,128)S(1)} %copy-done.6, f32[32,128]{1,0:T(8,128)S(1)} %collective-permute-done.west_in, ...), custom_call_target="tpu_custom_call" | custom-call | flops 1000000 | bytes 2000000 | tf_op jit(solution)/shard_map/advect/pallas_call | solution.py:213
  37.7 5.8 %all-to-all-done = f32[128,17,1,128]{3,2,1,0:T(1,128)S(1)} async-done(((f32[128,17,1,128]{3,2,1,0:T(1,128)}), f32[128,17,1,128]{3,2,1,0:T(1,128)S(1)}, u32[]{:S(2)}, u32[]{:S(2)}) %all-to-all-start) | async-done | bytes 1114144 | tf_op jit(solution)/shard_map/all_to_all | solution.py:378
  43.5 0.0 copy-done.7
  43.5 1.1 %ocean.1 = (f32[16,32,128]{2,1,0:T(8,128)}, f32[128,8,128]{2,1,0:T(8,128)S(1)}) custom-call(f32[2176,128]{1,0:T(8,128)S(1)} %bitcast.8, f32[16,32,128]{2,1,0:T(8,128)S(1)} %advect.1.carried, f32[8,32,128]{2,1,0:T(8,128)S(1)} %copy-done.7, s32[32,128]{1,0:T(8,128)S(1)} %copy-done.6), custom_call_target="tpu_custom_call" | custom-call | flops 100000000 | bytes 4000000 | tf_op jit(solution)/shard_map/ocean/pallas_call | solution.py:286
  44.7 17.9 %all_to_all.10 = f32[128,8,128]{2,1,0:T(8,128)S(1)} all-to-all(f32[128,8,128]{2,1,0:T(8,128)S(1)} %get-tuple-element.17), channel_id=1, replica_groups=mesh['lon'=32,'lat'=4] {'lon','lat'}, dimensions={0} | all-to-all | bytes 1048576 | tf_op jit(solution)/shard_map/all_to_all | solution.py:383
  62.6 0.0 copy-start.1
  62.6 3.4 %copy-done.1 = bf16[256,128,128]{2,1,0:T(8,128)(2,1)S(1)} copy-done((bf16[256,128,128]{2,1,0:T(8,128)(2,1)S(1)}, bf16[256,128,128]{2,1,0:T(8,128)(2,1)}, u32[]{:S(2)}) %copy-start.1) | copy-done | bytes 8388632
  66.0 6.9 %state.1 = f32[256,2,128]{2,1,0:T(2,128)} custom-call(s32[2,128]{1,0:T(2,128)S(1)} %get-tuple-element.16.slots, f32[1024,128]{1,0:T(8,128)S(1)} %bitcast.9, bf16[256,128,128]{2,1,0:T(8,128)(2,1)S(1)} %copy-done.1), custom_call_target="tpu_custom_call" | custom-call | flops 1000000000 | bytes 9000000 | tf_op jit(solution)/shard_map/state/pallas_call | solution.py:335
Async XLA Ops:
  0.6 3.4 %copy-start = (bf16[256,128,128]{2,1,0:T(8,128)(2,1)S(1)}, bf16[256,128,128]{2,1,0:T(8,128)(2,1)}, u32[]{:S(2)}) copy-start(bf16[256,128,128]{2,1,0:T(8,128)(2,1)} %remap_hbm.3) | copy-start | bytes 25165828
  4.0 1.1 %copy-start.3 = (f32[256,6,128]{2,0,1:T(8,128)S(1)}, f32[256,6,128]{2,0,1:T(8,128)}, u32[]{:S(2)}) copy-start(f32[256,6,128]{2,0,1:T(8,128)} %param.9) | copy-start | bytes 2359300
  5.1 0.7 copy-start.8
  5.8 0.7 copy-start.9
  11.3 11.6 %copy-start.2 = (f32[2,8,32,128]{3,2,1,0:T(8,128)S(1)}, f32[2,8,32,128]{3,2,1,0:T(8,128)}, u32[]{:S(2)}) copy-start(f32[2,8,32,128]{3,2,1,0:T(8,128)} %param.13) | copy-start | bytes 786436
  11.4 11.6 %copy-start.4 = (f32[8,32,128]{2,1,0:T(8,128)S(1)}, f32[8,32,128]{2,1,0:T(8,128)}, u32[]{:S(2)}) copy-start(f32[8,32,128]{2,1,0:T(8,128)} %east_vel.3) | copy-start | bytes 393220
  11.4 11.6 %copy-start.5 = (f32[8,32,128]{2,1,0:T(8,128)S(1)}, f32[8,32,128]{2,1,0:T(8,128)}, u32[]{:S(2)}) copy-start(f32[8,32,128]{2,1,0:T(8,128)} %north_vel.3) | copy-start | bytes 393220
  11.4 11.6 %copy-start.6 = (s32[32,128]{1,0:T(8,128)S(1)}, s32[32,128]{1,0:T(8,128)}, u32[]{:S(2)}) copy-start(s32[32,128]{1,0:T(8,128)} %levels.5) | copy-start | bytes 49156
  11.4 32.1 %all-to-all-start = ((f32[128,17,1,128]{3,2,1,0:T(1,128)}), f32[128,17,1,128]{3,2,1,0:T(1,128)S(1)}, u32[]{:S(2)}, u32[]{:S(2)}) async-start(f32[128,17,1,128]{3,2,1,0:T(1,128)} %bitcast.3), calls=%async_computation | async-start | bytes 2228224 | tf_op jit(solution)/shard_map/all_to_all | solution.py:378
  22.9 20.6 %copy-start.7 = (f32[8,32,128]{2,1,0:T(8,128)S(1)}, f32[8,32,128]{2,1,0:T(8,128)}, u32[]{:S(2)}) copy-start(f32[8,32,128]{2,1,0:T(8,128)} %kappa.1) | copy-start | bytes 393220
  23.2 6.2 %collective-permute-start = (f32[32,128]{1,0:T(8,128)S(1)}, f32[32,128]{1,0:T(8,128)S(1)}, u32[]{:S(2)}, u32[]{:S(2)}) collective-permute-start(f32[32,128]{1,0:T(8,128)S(1)} %get-tuple-element.11), channel_id=1, source_target_pairs={{0,4},{4,8},{8,12},{12,16},{16,20},{20,24},{24,28},{28,32},{32,36}... | collective-permute-start | bytes 49160 | tf_op jit(solution)/shard_map/ppermute | solution.py:368
  25.0 5.4 %collective-permute-start.1 = (f32[32,128]{1,0:T(8,128)S(1)}, f32[32,128]{1,0:T(8,128)S(1)}, u32[]{:S(2)}, u32[]{:S(2)}) collective-permute-start(f32[32,128]{1,0:T(8,128)S(1)} %get-tuple-element.12), channel_id=1, source_target_pairs={{4,0},{8,4},{12,8},{16,12},{20,16},{24,20},{28,24},{32,28},{36,32}... | collective-permute-start | bytes 49160 | tf_op jit(solution)/shard_map/ppermute | solution.py:369
  25.0 8.9 %collective-permute-start.2 = (f32[32,128]{1,0:T(8,128)S(1)}, f32[32,128]{1,0:T(8,128)S(1)}, u32[]{:S(2)}, u32[]{:S(2)}) collective-permute-start(f32[32,128]{1,0:T(8,128)S(1)} %get-tuple-element.13), channel_id=1, source_target_pairs={{0,1},{1,2},{2,3},{4,5},{5,6},{6,7},{8,9},{9,10},{10,11},{12,13},{... | collective-permute-start | bytes 49160 | tf_op jit(solution)/shard_map/ppermute | solution.py:370
  28.1 8.6 %collective-permute-start.3 = (f32[32,128]{1,0:T(8,128)S(1)}, f32[32,128]{1,0:T(8,128)S(1)}, u32[]{:S(2)}, u32[]{:S(2)}) collective-permute-start(f32[32,128]{1,0:T(8,128)S(1)} %get-tuple-element.14), channel_id=1, source_target_pairs={{1,0},{2,1},{3,2},{5,4},{6,5},{7,6},{9,8},{10,9},{11,10},{13,12},{... | collective-permute-start | bytes 49160 | tf_op jit(solution)/shard_map/ppermute | solution.py:371
  62.6 3.4 %copy-start.1 = (bf16[256,128,128]{2,1,0:T(8,128)(2,1)S(1)}, bf16[256,128,128]{2,1,0:T(8,128)(2,1)}, u32[]{:S(2)}) copy-start(bf16[256,128,128]{2,1,0:T(8,128)(2,1)} %remap_hbm.3) | copy-start | bytes 25165828

commit v2 on v1

--- a/solution.py
+++ b/solution.py
@@ -34,6 +34,10 @@
     return lax.broadcasted_iota(jnp.int32, shape, axis)
 
 
+def in_hbm(x):
+    return pltpu.with_memory_space_constraint(x, pltpu.HBM)
+
+
 def params(mib):
     return pltpu.CompilerParams(vmem_limit_bytes=mib * 1024 * 1024)
 
@@ -42,7 +46,9 @@
     return [pl.BlockSpec(memory_space=VMEM)] * count
 
 
-def contrib_kernel(owner, target, flux_hbm, remap_hbm, send, slot_out, weights, flux, fields, slot_v, slot_s, sems, sem2):
+def contrib_kernel(
+    owner, target, flux_hbm, remap_hbm, send, slot_out, weights, flux, fields, slot_v, slot_s, sems, sem2
+):
     chunk_copies = [
         pltpu.make_async_copy(
             remap_hbm.at[pl.ds(c * PER, PER)], weights.at[pl.ds(c * PER, PER)], sems.at[c]
@@ -113,7 +119,7 @@
             jax.ShapeDtypeStruct((DEV * BLOCK, CELLS), F32),
             jax.ShapeDtypeStruct((2, 128), jnp.int32),
         ),
-        in_specs=vmem_specs(2) + [pl.BlockSpec(memory_space=pl.ANY)] * 2,
+        in_specs=vmem_specs(2) + [pl.BlockSpec(memory_space=pltpu.HBM)] * 2,
         out_specs=tuple(vmem_specs(2)),
         scratch_shapes=[
             VMEM((ROWS, 128, 128), BF16),
@@ -338,7 +344,7 @@
         in_specs=[
             pl.BlockSpec(memory_space=SMEM),
             pl.BlockSpec(memory_space=VMEM),
-            pl.BlockSpec(memory_space=pl.ANY),
+            pl.BlockSpec(memory_space=pltpu.HBM),
         ],
         out_specs=pl.BlockSpec(memory_space=VMEM),
         scratch_shapes=[
@@ -372,8 +378,8 @@
     send, slots = contributions(
         row_owner.reshape(2, 128),
         row_target.reshape(2, 128),
-        jnp.transpose(atmos_flux, (1, 0, 2)),
-        remap_blocks,
+        in_hbm(jnp.transpose(atmos_flux, (1, 0, 2))),
+        in_hbm(remap_blocks),
     )
     got = lax.all_to_all(
         send.reshape(DEV, BLOCK, 1, CELLS), axes, split_axis=0, concat_axis=0, tiled=True
@@ -381,7 +387,7 @@
     carried = advected(planes, east_vel, north_vel, levels, west_in, east_in, south_in, north_in)
     after, answer = ocean(got.reshape(DEV * BLOCK, CELLS), carried, mix_kappa, levels)
     returned = lax.all_to_all(answer, axes, split_axis=0, concat_axis=0, tiled=True)
-    atmos_state = state(slots, returned.reshape(DEV * 2 * CAP, CELLS), remap_blocks)
+    atmos_state = state(slots, returned.reshape(DEV * 2 * CAP, CELLS), in_hbm(remap_blocks))
     return after.reshape(2, LEV, CY, CELLS), atmos_state
 
 

time: 73.3 us -> 66.1 us (0.902)
  local copies, waits for them, and re-layouts: 9.28 us -> 1.38 us
  Pallas kernels: 14.1 us -> 15 us
    unnamed x20 -> x14, local copies, waits for them, and re-layouts: 9.28 us -> 1.38 us
    pallas_call x1, Pallas kernels: 4.83 us -> 6.24 us  [contributions(): pl.pallas_call(contrib_kernel, out_shape=(jax.ShapeDtypeStruct((DEV * BLO...]
where the time goes in v2:
time: 66.1 us; the launch traced here: 65.9 us
  blocking collectives  17.9 us (27%)
  starting transfers between devices  17.7 us (27%)
  Pallas kernels  15 us (23%)
  waiting for transfers between devices  13.1 us (20%)
  local copies, waits for them, and re-layouts  1.38 us (2%)
  between operations  0.77 us (1%)
    all_to_all x1, blocking collectives, on_device(): lax.all_to_all(answer, axes, split_axis=0, concat_axis=0, tiled=True)  17.9 us
    all_to_all x1, starting transfers between devices, on_device(): lax.all_to_all(send.reshape(DEV, BLOCK, 1, CELLS), axes, split_axis=0, co...  11.5 us
    pallas_call x1, Pallas kernels, state(): pl.pallas_call(state_kernel, out_shape=jax.ShapeDtypeStruct((ROWS, 2, 128...  6.37 us
    pallas_call x1, Pallas kernels, contributions(): pl.pallas_call(contrib_kernel, out_shape=(jax.ShapeDtypeStruct((DEV * BLO...  6.24 us
    all_to_all x1, waiting for transfers between devices, on_device(): lax.all_to_all(send.reshape(DEV, BLOCK, 1, CELLS), axes, split_axis=0, co...  5.82 us
    ppermute x1, waiting for transfers between devices, on_device(): south_in = lax.ppermute(to_north, 'lat', northward)  3.53 us
    ppermute x1, starting transfers between devices, on_device(): south_in = lax.ppermute(to_north, 'lat', northward)  3.09 us
    ppermute x1, waiting for transfers between devices, on_device(): north_in = lax.ppermute(to_south, 'lat', southward)  2.78 us
  transfers between devices with their start and end apart: 5, of which 4 were waited for; matrix products, arithmetic and copies ran while one was open for 0% of the time, Pallas kernels for 2%

profile of v2, /device:TPU:1, one launch (start us, length us, event | category | flops | bytes accessed | tf_op | source)
XLA Modules:
  0.0 65.9 jit_solution(16427702514146893380)
XLA Ops:
  0.6 0.0 copy-start.5
  0.6 0.7 %copy-done.5 = s32[256,1]{0,1:T(1,128)S(1)} copy-done((s32[256,1]{0,1:T(1,128)S(1)}, s32[256,1]{0,1:T(1,128)}, u32[]{:S(2)}) %copy-start.5) | copy-done | bytes 1048
  1.3 0.0 copy-start.6
  1.3 0.7 %copy-done.6 = s32[256]{0:T(256)S(1)} copy-done((s32[256]{0:T(256)S(1)}, s32[256]{0:T(256)}, u32[]{:S(2)}) %copy-start.6) | copy-done | bytes 1048
  2.0 6.2 %contrib.1 = (f32[2176,128]{1,0:T(8,128)}, s32[2,128]{1,0:T(2,128)S(1)}) custom-call(s32[2,128]{1,0:T(2,128)S(1)} %bitcast.12, s32[2,128]{1,0:T(2,128)S(1)} %bitcast.13, f32[6,256,128]{2,1,0:T(8,128)} %bitcast.14, bf16[256,128,128]{2,1,0:T(8,128)(2,1)} %remap_hbm.3), custom_call_target="tpu_custom_call" | custom-call | flops 1000000000 | bytes 10000000 | tf_op jit(solution)/shard_map/contrib/pallas_call | solution.py:116
  8.2 0.0 copy-start
  8.2 0.0 copy-start.1
  8.3 0.0 copy-start.2
  8.3 0.0 copy-start.3
  8.3 11.5 %all-to-all-start = ((f32[128,17,1,128]{3,2,1,0:T(1,128)}), f32[128,17,1,128]{3,2,1,0:T(1,128)S(1)}, u32[]{:S(2)}, u32[]{:S(2)}) async-start(f32[128,17,1,128]{3,2,1,0:T(1,128)} %bitcast.3), calls=%async_computation | async-start | bytes 2228224 | tf_op jit(solution)/shard_map/all_to_all | solution.py:384
  19.8 0.0 copy-start.4
  19.8 0.0 copy-done
  19.8 0.0 copy-done.1
  19.8 0.0 copy-done.2
  19.8 0.0 copy-done.3
  19.8 0.2 edges.1
  20.1 1.8 %collective-permute-start = (f32[32,128]{1,0:T(8,128)S(1)}, f32[32,128]{1,0:T(8,128)S(1)}, u32[]{:S(2)}, u32[]{:S(2)}) collective-permute-start(f32[32,128]{1,0:T(8,128)S(1)} %get-tuple-element.11), channel_id=1, source_target_pairs={{0,4},{4,8},{8,12},{12,16},{16,20},{20,24},{24,28},{28,32},{32,36}... | collective-permute-start | bytes 49160 | tf_op jit(solution)/shard_map/ppermute | solution.py:374
  21.9 0.0 collective-permute-start.1
  21.9 3.1 %collective-permute-start.2 = (f32[32,128]{1,0:T(8,128)S(1)}, f32[32,128]{1,0:T(8,128)S(1)}, u32[]{:S(2)}, u32[]{:S(2)}) collective-permute-start(f32[32,128]{1,0:T(8,128)S(1)} %get-tuple-element.13), channel_id=1, source_target_pairs={{0,1},{1,2},{2,3},{4,5},{5,6},{6,7},{8,9},{9,10},{10,11},{12,13},{... | collective-permute-start | bytes 49160 | tf_op jit(solution)/shard_map/ppermute | solution.py:376
  25.0 1.3 %collective-permute-start.3 = (f32[32,128]{1,0:T(8,128)S(1)}, f32[32,128]{1,0:T(8,128)S(1)}, u32[]{:S(2)}, u32[]{:S(2)}) collective-permute-start(f32[32,128]{1,0:T(8,128)S(1)} %get-tuple-element.14), channel_id=1, source_target_pairs={{1,0},{2,1},{3,2},{5,4},{6,5},{7,6},{9,8},{10,9},{11,10},{13,12},{... | collective-permute-start | bytes 49160 | tf_op jit(solution)/shard_map/ppermute | solution.py:377
  26.3 0.0 collective-permute-done.west_in
  26.3 0.9 %collective-permute-done.1.east_in = f32[32,128]{1,0:T(8,128)S(1)} collective-permute-done((f32[32,128]{1,0:T(8,128)S(1)}, f32[32,128]{1,0:T(8,128)S(1)}, u32[]{:S(2)}, u32[]{:S(2)}) %collective-permute-start.1) | collective-permute-done | bytes 16416 | tf_op jit(solution)/shard_map/ppermute | solution.py:375
  27.3 3.5 %collective-permute-done.2.south_in = f32[32,128]{1,0:T(8,128)S(1)} collective-permute-done((f32[32,128]{1,0:T(8,128)S(1)}, f32[32,128]{1,0:T(8,128)S(1)}, u32[]{:S(2)}, u32[]{:S(2)}) %collective-permute-start.2) | collective-permute-done | bytes 16416 | tf_op jit(solution)/shard_map/ppermute | solution.py:376
  30.8 2.8 %collective-permute-done.3.north_in = f32[32,128]{1,0:T(8,128)S(1)} collective-permute-done((f32[32,128]{1,0:T(8,128)S(1)}, f32[32,128]{1,0:T(8,128)S(1)}, u32[]{:S(2)}, u32[]{:S(2)}) %collective-permute-start.3) | collective-permute-done | bytes 16416 | tf_op jit(solution)/shard_map/ppermute | solution.py:377
  33.6 1.0 %advect.1.carried = f32[16,32,128]{2,1,0:T(8,128)S(1)} custom-call(f32[16,32,128]{2,1,0:T(8,128)S(1)} %bitcast.11, f32[8,32,128]{2,1,0:T(8,128)S(1)} %copy-done.1, f32[8,32,128]{2,1,0:T(8,128)S(1)} %copy-done.2, s32[32,128]{1,0:T(8,128)S(1)} %copy-done.3, f32[32,128]{1,0:T(8,128)S(1)} %collective-permute-done.west_in, ...), custom_call_target="tpu_custom_call" | custom-call | flops 1000000 | bytes 2000000 | tf_op jit(solution)/shard_map/advect/pallas_call | solution.py:219
  34.6 5.8 %all-to-all-done = f32[128,17,1,128]{3,2,1,0:T(1,128)S(1)} async-done(((f32[128,17,1,128]{3,2,1,0:T(1,128)}), f32[128,17,1,128]{3,2,1,0:T(1,128)S(1)}, u32[]{:S(2)}, u32[]{:S(2)}) %all-to-all-start) | async-done | bytes 1114144 | tf_op jit(solution)/shard_map/all_to_all | solution.py:384
  40.4 0.0 copy-done.4
  40.4 1.1 %ocean.1 = (f32[16,32,128]{2,1,0:T(8,128)}, f32[128,8,128]{2,1,0:T(8,128)S(1)}) custom-call(f32[2176,128]{1,0:T(8,128)S(1)} %bitcast.8, f32[16,32,128]{2,1,0:T(8,128)S(1)} %advect.1.carried, f32[8,32,128]{2,1,0:T(8,128)S(1)} %copy-done.4, s32[32,128]{1,0:T(8,128)S(1)} %copy-done.3), custom_call_target="tpu_custom_call" | custom-call | flops 100000000 | bytes 4000000 | tf_op jit(solution)/shard_map/ocean/pallas_call | solution.py:292
  41.6 17.9 %all_to_all.10 = f32[128,8,128]{2,1,0:T(8,128)S(1)} all-to-all(f32[128,8,128]{2,1,0:T(8,128)S(1)} %get-tuple-element.17), channel_id=1, replica_groups=mesh['lon'=32,'lat'=4] {'lon','lat'}, dimensions={0} | all-to-all | bytes 1048576 | tf_op jit(solution)/shard_map/all_to_all | solution.py:389
  59.5 6.4 %state.1 = f32[256,2,128]{2,1,0:T(2,128)} custom-call(s32[2,128]{1,0:T(2,128)S(1)} %get-tuple-element.16.slots, f32[1024,128]{1,0:T(8,128)S(1)} %bitcast.9, bf16[256,128,128]{2,1,0:T(8,128)(2,1)} %remap_hbm.3), custom_call_target="tpu_custom_call" | custom-call | flops 1000000000 | bytes 9000000 | tf_op jit(solution)/shard_map/state/pallas_call | solution.py:341
Async XLA Ops:
  0.6 0.7 %copy-start.5 = (s32[256,1]{0,1:T(1,128)S(1)}, s32[256,1]{0,1:T(1,128)}, u32[]{:S(2)}) copy-start(s32[256,1]{0,1:T(1,128)} %param.11) | copy-start | bytes 3076
  1.3 0.7 %copy-start.6 = (s32[256]{0:T(256)S(1)}, s32[256]{0:T(256)}, u32[]{:S(2)}) copy-start(s32[256]{0:T(256)} %param.12) | copy-start | bytes 3076
  8.2 11.6 %copy-start = (f32[2,8,32,128]{3,2,1,0:T(8,128)S(1)}, f32[2,8,32,128]{3,2,1,0:T(8,128)}, u32[]{:S(2)}) copy-start(f32[2,8,32,128]{3,2,1,0:T(8,128)} %param.13) | copy-start | bytes 786436
  8.2 11.6 %copy-start.1 = (f32[8,32,128]{2,1,0:T(8,128)S(1)}, f32[8,32,128]{2,1,0:T(8,128)}, u32[]{:S(2)}) copy-start(f32[8,32,128]{2,1,0:T(8,128)} %east_vel.3) | copy-start | bytes 393220
  8.3 11.6 %copy-start.2 = (f32[8,32,128]{2,1,0:T(8,128)S(1)}, f32[8,32,128]{2,1,0:T(8,128)}, u32[]{:S(2)}) copy-start(f32[8,32,128]{2,1,0:T(8,128)} %north_vel.3) | copy-start | bytes 393220
  8.3 11.6 %copy-start.3 = (s32[32,128]{1,0:T(8,128)S(1)}, s32[32,128]{1,0:T(8,128)}, u32[]{:S(2)}) copy-start(s32[32,128]{1,0:T(8,128)} %levels.5) | copy-start | bytes 49156
  8.3 32.1 %all-to-all-start = ((f32[128,17,1,128]{3,2,1,0:T(1,128)}), f32[128,17,1,128]{3,2,1,0:T(1,128)S(1)}, u32[]{:S(2)}, u32[]{:S(2)}) async-start(f32[128,17,1,128]{3,2,1,0:T(1,128)} %bitcast.3), calls=%async_computation | async-start | bytes 2228224 | tf_op jit(solution)/shard_map/all_to_all | solution.py:384
  19.8 20.6 %copy-start.4 = (f32[8,32,128]{2,1,0:T(8,128)S(1)}, f32[8,32,128]{2,1,0:T(8,128)}, u32[]{:S(2)}) copy-start(f32[8,32,128]{2,1,0:T(8,128)} %kappa.1) | copy-start | bytes 393220
  20.1 6.2 %collective-permute-start = (f32[32,128]{1,0:T(8,128)S(1)}, f32[32,128]{1,0:T(8,128)S(1)}, u32[]{:S(2)}, u32[]{:S(2)}) collective-permute-start(f32[32,128]{1,0:T(8,128)S(1)} %get-tuple-element.11), channel_id=1, source_target_pairs={{0,4},{4,8},{8,12},{12,16},{16,20},{20,24},{24,28},{28,32},{32,36}... | collective-permute-start | bytes 49160 | tf_op jit(solution)/shard_map/ppermute | solution.py:374
  21.9 5.4 %collective-permute-start.1 = (f32[32,128]{1,0:T(8,128)S(1)}, f32[32,128]{1,0:T(8,128)S(1)}, u32[]{:S(2)}, u32[]{:S(2)}) collective-permute-start(f32[32,128]{1,0:T(8,128)S(1)} %get-tuple-element.12), channel_id=1, source_target_pairs={{4,0},{8,4},{12,8},{16,12},{20,16},{24,20},{28,24},{32,28},{36,32}... | collective-permute-start | bytes 49160 | tf_op jit(solution)/shard_map/ppermute | solution.py:375
  21.9 8.9 %collective-permute-start.2 = (f32[32,128]{1,0:T(8,128)S(1)}, f32[32,128]{1,0:T(8,128)S(1)}, u32[]{:S(2)}, u32[]{:S(2)}) collective-permute-start(f32[32,128]{1,0:T(8,128)S(1)} %get-tuple-element.13), channel_id=1, source_target_pairs={{0,1},{1,2},{2,3},{4,5},{5,6},{6,7},{8,9},{9,10},{10,11},{12,13},{... | collective-permute-start | bytes 49160 | tf_op jit(solution)/shard_map/ppermute | solution.py:376
  25.0 8.6 %collective-permute-start.3 = (f32[32,128]{1,0:T(8,128)S(1)}, f32[32,128]{1,0:T(8,128)S(1)}, u32[]{:S(2)}, u32[]{:S(2)}) collective-permute-start(f32[32,128]{1,0:T(8,128)S(1)} %get-tuple-element.14), channel_id=1, source_target_pairs={{1,0},{2,1},{3,2},{5,4},{6,5},{7,6},{9,8},{10,9},{11,10},{13,12},{... | collective-permute-start | bytes 49160 | tf_op jit(solution)/shard_map/ppermute | solution.py:377

commit v3 on v2

--- a/solution.py
+++ b/solution.py
@@ -18,8 +18,8 @@
 BLOCK = CAP * SENT + 1
 LEV = 8
 CY = 32
-CHUNKS = 8
-PER = ROWS // CHUNKS
+CONTRIB_SIZES = (16, 32, 48, 64, 96)
+STATE_SIZES = (64, 64, 64, 64)
 
 VMEM = pltpu.VMEM
 SMEM = pltpu.SMEM
@@ -34,6 +34,19 @@
     return lax.broadcasted_iota(jnp.int32, shape, axis)
 
 
+def spans(sizes):
+    return [(sum(sizes[:i]), size) for i, size in enumerate(sizes)]
+
+
+def block_copies(remap_hbm, weights, sems, sizes):
+    return [
+        pltpu.make_async_copy(
+            remap_hbm.at[pl.ds(start, size)], weights.at[pl.ds(start, size)], sems.at[i]
+        )
+        for i, (start, size) in enumerate(spans(sizes))
+    ]
+
+
 def in_hbm(x):
     return pltpu.with_memory_space_constraint(x, pltpu.HBM)
 
@@ -47,18 +60,34 @@
 
 
 def contrib_kernel(
-    owner, target, flux_hbm, remap_hbm, send, slot_out, weights, flux, fields, slot_v, slot_s, sems, sem2
+    owner_hbm,
+    target_hbm,
+    flux_hbm,
+    remap_hbm,
+    send,
+    slot_out,
+    weights,
+    flux,
+    fields,
+    owner,
+    target,
+    slot_v,
+    slot_s,
+    sems,
+    sem2,
 ):
-    chunk_copies = [
-        pltpu.make_async_copy(
-            remap_hbm.at[pl.ds(c * PER, PER)], weights.at[pl.ds(c * PER, PER)], sems.at[c]
-        )
-        for c in range(CHUNKS)
-    ]
+    chunk_copies = block_copies(remap_hbm, weights, sems, CONTRIB_SIZES)
+    owner_copy = pltpu.make_async_copy(owner_hbm, owner, sem2.at[2])
+    target_copy = pltpu.make_async_copy(target_hbm, target, sem2.at[3])
     flux_copy = pltpu.make_async_copy(flux_hbm, flux, sem2.at[0])
+    owner_copy.start()
+    target_copy.start()
     flux_copy.start()
     for copy in chunk_copies:
         copy.start()
+    send[...] = jnp.zeros_like(send)
+    owner_copy.wait()
+    target_copy.wait()
 
     dev_iota = iota((DEV, 128), 0)
     own = owner[...]
@@ -80,7 +109,6 @@
     tags = lax.dot_general(
         member.astype(BF16), slot_tags, (((1,), (1,)), ((), ())), preferred_element_type=F32
     )
-    send[...] = jnp.zeros_like(send)
     send[pl.ds(CAP * SENT, DEV, stride=BLOCK), :] = tags
 
     flux_copy.wait()
@@ -101,15 +129,10 @@
         send[pl.ds(first, SENT), :] = both[:4, :CELLS]
         send[pl.ds(second, SENT), :] = both[4:, CELLS:]
 
-    def chunk(c, carry):
-        pltpu.make_async_copy(
-            remap_hbm.at[pl.ds(c * PER, PER)], weights.at[pl.ds(c * PER, PER)], sems.at[c]
-        ).wait()
-        for i in range(0, PER, 2):
-            pair(c * PER + i)
-        return carry
-
-    lax.fori_loop(0, CHUNKS, chunk, 0)
+    for copy, (start, size) in zip(chunk_copies, spans(CONTRIB_SIZES)):
+        copy.wait()
+        for r in range(start, start + size, 2):
+            pair(r)
 
 
 def contributions(row_owner, row_target, flux, remap):
@@ -119,16 +142,18 @@
             jax.ShapeDtypeStruct((DEV * BLOCK, CELLS), F32),
             jax.ShapeDtypeStruct((2, 128), jnp.int32),
         ),
-        in_specs=vmem_specs(2) + [pl.BlockSpec(memory_space=pltpu.HBM)] * 2,
+        in_specs=[pl.BlockSpec(memory_space=pltpu.HBM)] * 4,
         out_specs=tuple(vmem_specs(2)),
         scratch_shapes=[
             VMEM((ROWS, 128, 128), BF16),
             VMEM((6, ROWS, 128), F32),
             VMEM((ROWS * SENT, 128), F32),
             VMEM((2, 128), jnp.int32),
+            VMEM((2, 128), jnp.int32),
+            VMEM((2, 128), jnp.int32),
             SMEM((2, 128), jnp.int32),
-            pltpu.SemaphoreType.DMA((CHUNKS,)),
-            pltpu.SemaphoreType.DMA((2,)),
+            pltpu.SemaphoreType.DMA((len(CONTRIB_SIZES),)),
+            pltpu.SemaphoreType.DMA((4,)),
         ],
         compiler_params=params(24),
         cost_estimate=pl.CostEstimate(flops=10**9, bytes_accessed=10_000_000, transcendentals=0),
@@ -304,37 +329,24 @@
 
 
 def state_kernel(slots, returned, remap_hbm, out, weights, rows, sems):
-    for c in range(CHUNKS):
-        pltpu.make_async_copy(
-            remap_hbm.at[pl.ds(c * PER, PER)], weights.at[pl.ds(c * PER, PER)], sems.at[c]
-        ).start()
-
-    def gather(g, carry):
-        for i in range(16):
-            r = g * 16 + i
-            rows[pl.ds(2 * r, 2), :] = returned[pl.ds(slots[r // 128, r % 128], 2), :]
-        return carry
-
-    lax.fori_loop(0, ROWS // 16, gather, 0)
-
-    def chunk(c, carry):
-        pltpu.make_async_copy(
-            remap_hbm.at[pl.ds(c * PER, PER)], weights.at[pl.ds(c * PER, PER)], sems.at[c]
-        ).wait()
-        for i in range(0, PER, 4):
-            r = c * PER + i
-            high, low = split(rows[pl.ds(pl.multiple_of(2 * r, 8), 8), :])
+    chunk_copies = block_copies(remap_hbm, weights, sems, STATE_SIZES)
+    for copy in chunk_copies:
+        copy.start()
+
+    for r in range(ROWS):
+        rows[2 * r : 2 * r + 2, :] = returned[pl.ds(slots[r // 128, r % 128], 2), :]
+    for copy, (start, size) in zip(chunk_copies, spans(STATE_SIZES)):
+        copy.wait()
+        for r in range(start, start + size, 4):
+            high, low = split(rows[2 * r : 2 * r + 8, :])
             left = jnp.concatenate([high, low], axis=0)
-            right = weights[pl.ds(r, 4)].reshape(4 * 128, 128)
+            right = weights[r : r + 4].reshape(4 * 128, 128)
             four = lax.dot_general(
                 left, right, (((1,), (1,)), ((), ())), preferred_element_type=F32
             )
             four = four[:8] + four[8:]
             for j in range(4):
                 out[r + j] = four[2 * j : 2 * j + 2, j * 128 : (j + 1) * 128]
-        return carry
-
-    lax.fori_loop(0, CHUNKS, chunk, 0)
 
 
 def state(slots, returned, remap):
@@ -350,7 +362,7 @@
         scratch_shapes=[
             VMEM((ROWS, 128, 128), BF16),
             VMEM((2 * ROWS, 128), F32),
-            pltpu.SemaphoreType.DMA((CHUNKS,)),
+            pltpu.SemaphoreType.DMA((len(STATE_SIZES),)),
         ],
         compiler_params=params(24),
         cost_estimate=pl.CostEstimate(flops=10**9, bytes_accessed=9_000_000, transcendentals=0),
@@ -376,8 +388,8 @@
     south_in = lax.ppermute(to_north, "lat", northward)
     north_in = lax.ppermute(to_south, "lat", southward)
     send, slots = contributions(
-        row_owner.reshape(2, 128),
-        row_target.reshape(2, 128),
+        in_hbm(row_owner.reshape(2, 128)),
+        in_hbm(row_target.reshape(2, 128)),
         in_hbm(jnp.transpose(atmos_flux, (1, 0, 2))),
         in_hbm(remap_blocks),
     )

time: 66.1 us -> 63.2 us (0.956)
  Pallas kernels: 15 us -> 13.5 us
  local copies, waits for them, and re-layouts: 1.38 us -> 0.03 us
    unnamed x14 -> x10, local copies, waits for them, and re-layouts: 1.38 us -> 0.03 us
    pallas_call x1, Pallas kernels: 6.37 us -> 5.53 us  [state(): pl.pallas_call(state_kernel, out_shape=jax.ShapeDtypeStruct((ROWS, 2, 128...]
where the time goes in v3:
time: 63.2 us; the launch traced here: 63 us
  blocking collectives  17.9 us (28%)
  starting transfers between devices  17.7 us (28%)
  Pallas kernels  13.5 us (21%)
  waiting for transfers between devices  13.1 us (21%)
  between operations  0.76 us (1%)
    all_to_all x1, blocking collectives, on_device(): lax.all_to_all(answer, axes, split_axis=0, concat_axis=0, tiled=True)  17.9 us
    all_to_all x1, starting transfers between devices, on_device(): lax.all_to_all(send.reshape(DEV, BLOCK, 1, CELLS), axes, split_axis=0, co...  11.5 us
    all_to_all x1, waiting for transfers between devices, on_device(): lax.all_to_all(send.reshape(DEV, BLOCK, 1, CELLS), axes, split_axis=0, co...  5.82 us
    pallas_call x1, Pallas kernels, contributions(): pl.pallas_call(contrib_kernel, out_shape=(jax.ShapeDtypeStruct((DEV * BLO...  5.59 us
    pallas_call x1, Pallas kernels, state(): pl.pallas_call(state_kernel, out_shape=jax.ShapeDtypeStruct((ROWS, 2, 128...  5.53 us
    ppermute x1, waiting for transfers between devices, on_device(): south_in = lax.ppermute(to_north, 'lat', northward)  3.53 us
    ppermute x1, starting transfers between devices, on_device(): south_in = lax.ppermute(to_north, 'lat', northward)  3.09 us
    ppermute x1, waiting for transfers between devices, on_device(): north_in = lax.ppermute(to_south, 'lat', southward)  2.78 us
  transfers between devices with their start and end apart: 5, of which 4 were waited for; matrix products, arithmetic and copies ran while one was open for 0% of the time, Pallas kernels for 2%

profile of v3, /device:TPU:1, one launch (start us, length us, event | category | flops | bytes accessed | tf_op | source)
XLA Modules:
  0.0 63.0 jit_solution(2418108681724356245)
XLA Ops:
  0.6 5.6 %contrib.1 = (f32[2176,128]{1,0:T(8,128)}, s32[2,128]{1,0:T(2,128)S(1)}) custom-call(s32[2,128]{1,0:T(2,128)} %bitcast.13, s32[2,128]{1,0:T(2,128)} %bitcast.14, f32[6,256,128]{2,1,0:T(8,128)} %bitcast.12, bf16[256,128,128]{2,1,0:T(8,128)(2,1)} %remap_hbm.3), custom_call_target="tpu_custom_call" | custom-call | flops 1000000000 | bytes 10000000 | tf_op jit(solution)/shard_map/contrib/pallas_call | solution.py:139
  6.2 0.0 copy-start
  6.2 0.0 copy-start.1
  6.3 0.0 copy-start.2
  6.3 0.0 copy-start.3
  6.3 11.5 %all-to-all-start = ((f32[128,17,1,128]{3,2,1,0:T(1,128)}), f32[128,17,1,128]{3,2,1,0:T(1,128)S(1)}, u32[]{:S(2)}, u32[]{:S(2)}) async-start(f32[128,17,1,128]{3,2,1,0:T(1,128)} %bitcast.3), calls=%async_computation | async-start | bytes 2228224 | tf_op jit(solution)/shard_map/all_to_all | solution.py:396
  17.8 0.0 copy-start.4
  17.8 0.0 copy-done
  17.8 0.0 copy-done.1
  17.8 0.0 copy-done.2
  17.8 0.0 copy-done.3
  17.8 0.2 edges.1
  18.1 1.8 %collective-permute-start = (f32[32,128]{1,0:T(8,128)S(1)}, f32[32,128]{1,0:T(8,128)S(1)}, u32[]{:S(2)}, u32[]{:S(2)}) collective-permute-start(f32[32,128]{1,0:T(8,128)S(1)} %get-tuple-element.11), channel_id=1, source_target_pairs={{0,4},{4,8},{8,12},{12,16},{16,20},{20,24},{24,28},{28,32},{32,36}... | collective-permute-start | bytes 49160 | tf_op jit(solution)/shard_map/ppermute | solution.py:386
  19.9 0.0 collective-permute-start.1
  19.9 3.1 %collective-permute-start.2 = (f32[32,128]{1,0:T(8,128)S(1)}, f32[32,128]{1,0:T(8,128)S(1)}, u32[]{:S(2)}, u32[]{:S(2)}) collective-permute-start(f32[32,128]{1,0:T(8,128)S(1)} %get-tuple-element.13), channel_id=1, source_target_pairs={{0,1},{1,2},{2,3},{4,5},{5,6},{6,7},{8,9},{9,10},{10,11},{12,13},{... | collective-permute-start | bytes 49160 | tf_op jit(solution)/shard_map/ppermute | solution.py:388
  23.0 1.3 %collective-permute-start.3 = (f32[32,128]{1,0:T(8,128)S(1)}, f32[32,128]{1,0:T(8,128)S(1)}, u32[]{:S(2)}, u32[]{:S(2)}) collective-permute-start(f32[32,128]{1,0:T(8,128)S(1)} %get-tuple-element.14), channel_id=1, source_target_pairs={{1,0},{2,1},{3,2},{5,4},{6,5},{7,6},{9,8},{10,9},{11,10},{13,12},{... | collective-permute-start | bytes 49160 | tf_op jit(solution)/shard_map/ppermute | solution.py:389
  24.3 0.0 collective-permute-done.west_in
  24.3 0.9 %collective-permute-done.1.east_in = f32[32,128]{1,0:T(8,128)S(1)} collective-permute-done((f32[32,128]{1,0:T(8,128)S(1)}, f32[32,128]{1,0:T(8,128)S(1)}, u32[]{:S(2)}, u32[]{:S(2)}) %collective-permute-start.1) | collective-permute-done | bytes 16416 | tf_op jit(solution)/shard_map/ppermute | solution.py:387
  25.3 3.5 %collective-permute-done.2.south_in = f32[32,128]{1,0:T(8,128)S(1)} collective-permute-done((f32[32,128]{1,0:T(8,128)S(1)}, f32[32,128]{1,0:T(8,128)S(1)}, u32[]{:S(2)}, u32[]{:S(2)}) %collective-permute-start.2) | collective-permute-done | bytes 16416 | tf_op jit(solution)/shard_map/ppermute | solution.py:388
  28.8 2.8 %collective-permute-done.3.north_in = f32[32,128]{1,0:T(8,128)S(1)} collective-permute-done((f32[32,128]{1,0:T(8,128)S(1)}, f32[32,128]{1,0:T(8,128)S(1)}, u32[]{:S(2)}, u32[]{:S(2)}) %collective-permute-start.3) | collective-permute-done | bytes 16416 | tf_op jit(solution)/shard_map/ppermute | solution.py:389
  31.6 1.0 %advect.1.carried = f32[16,32,128]{2,1,0:T(8,128)S(1)} custom-call(f32[16,32,128]{2,1,0:T(8,128)S(1)} %bitcast.11, f32[8,32,128]{2,1,0:T(8,128)S(1)} %copy-done.1, f32[8,32,128]{2,1,0:T(8,128)S(1)} %copy-done.2, s32[32,128]{1,0:T(8,128)S(1)} %copy-done.3, f32[32,128]{1,0:T(8,128)S(1)} %collective-permute-done.west_in, ...), custom_call_target="tpu_custom_call" | custom-call | flops 1000000 | bytes 2000000 | tf_op jit(solution)/shard_map/advect/pallas_call | solution.py:244
  32.6 5.8 %all-to-all-done = f32[128,17,1,128]{3,2,1,0:T(1,128)S(1)} async-done(((f32[128,17,1,128]{3,2,1,0:T(1,128)}), f32[128,17,1,128]{3,2,1,0:T(1,128)S(1)}, u32[]{:S(2)}, u32[]{:S(2)}) %all-to-all-start) | async-done | bytes 1114144 | tf_op jit(solution)/shard_map/all_to_all | solution.py:396
  38.4 0.0 copy-done.4
  38.4 1.1 %ocean.1 = (f32[16,32,128]{2,1,0:T(8,128)}, f32[128,8,128]{2,1,0:T(8,128)S(1)}) custom-call(f32[2176,128]{1,0:T(8,128)S(1)} %bitcast.8, f32[16,32,128]{2,1,0:T(8,128)S(1)} %advect.1.carried, f32[8,32,128]{2,1,0:T(8,128)S(1)} %copy-done.4, s32[32,128]{1,0:T(8,128)S(1)} %copy-done.3), custom_call_target="tpu_custom_call" | custom-call | flops 100000000 | bytes 4000000 | tf_op jit(solution)/shard_map/ocean/pallas_call | solution.py:317
  39.6 17.9 %all_to_all.10 = f32[128,8,128]{2,1,0:T(8,128)S(1)} all-to-all(f32[128,8,128]{2,1,0:T(8,128)S(1)} %get-tuple-element.17), channel_id=1, replica_groups=mesh['lon'=32,'lat'=4] {'lon','lat'}, dimensions={0} | all-to-all | bytes 1048576 | tf_op jit(solution)/shard_map/all_to_all | solution.py:401
  57.5 5.5 %state.1 = f32[256,2,128]{2,1,0:T(2,128)} custom-call(s32[2,128]{1,0:T(2,128)S(1)} %get-tuple-element.16.slots, f32[1024,128]{1,0:T(8,128)S(1)} %bitcast.9, bf16[256,128,128]{2,1,0:T(8,128)(2,1)} %remap_hbm.3), custom_call_target="tpu_custom_call" | custom-call | flops 1000000000 | bytes 9000000 | tf_op jit(solution)/shard_map/state/pallas_call | solution.py:353
Async XLA Ops:
  6.2 11.6 %copy-start = (f32[2,8,32,128]{3,2,1,0:T(8,128)S(1)}, f32[2,8,32,128]{3,2,1,0:T(8,128)}, u32[]{:S(2)}) copy-start(f32[2,8,32,128]{3,2,1,0:T(8,128)} %param.13) | copy-start | bytes 786436
  6.2 11.6 %copy-start.1 = (f32[8,32,128]{2,1,0:T(8,128)S(1)}, f32[8,32,128]{2,1,0:T(8,128)}, u32[]{:S(2)}) copy-start(f32[8,32,128]{2,1,0:T(8,128)} %east_vel.3) | copy-start | bytes 393220
  6.3 11.6 %copy-start.2 = (f32[8,32,128]{2,1,0:T(8,128)S(1)}, f32[8,32,128]{2,1,0:T(8,128)}, u32[]{:S(2)}) copy-start(f32[8,32,128]{2,1,0:T(8,128)} %north_vel.3) | copy-start | bytes 393220
  6.3 11.6 %copy-start.3 = (s32[32,128]{1,0:T(8,128)S(1)}, s32[32,128]{1,0:T(8,128)}, u32[]{:S(2)}) copy-start(s32[32,128]{1,0:T(8,128)} %levels.5) | copy-start | bytes 49156
  6.3 32.1 %all-to-all-start = ((f32[128,17,1,128]{3,2,1,0:T(1,128)}), f32[128,17,1,128]{3,2,1,0:T(1,128)S(1)}, u32[]{:S(2)}, u32[]{:S(2)}) async-start(f32[128,17,1,128]{3,2,1,0:T(1,128)} %bitcast.3), calls=%async_computation | async-start | bytes 2228224 | tf_op jit(solution)/shard_map/all_to_all | solution.py:396
  17.8 20.6 %copy-start.4 = (f32[8,32,128]{2,1,0:T(8,128)S(1)}, f32[8,32,128]{2,1,0:T(8,128)}, u32[]{:S(2)}) copy-start(f32[8,32,128]{2,1,0:T(8,128)} %kappa.1) | copy-start | bytes 393220
  18.1 6.2 %collective-permute-start = (f32[32,128]{1,0:T(8,128)S(1)}, f32[32,128]{1,0:T(8,128)S(1)}, u32[]{:S(2)}, u32[]{:S(2)}) collective-permute-start(f32[32,128]{1,0:T(8,128)S(1)} %get-tuple-element.11), channel_id=1, source_target_pairs={{0,4},{4,8},{8,12},{12,16},{16,20},{20,24},{24,28},{28,32},{32,36}... | collective-permute-start | bytes 49160 | tf_op jit(solution)/shard_map/ppermute | solution.py:386
  19.9 5.4 %collective-permute-start.1 = (f32[32,128]{1,0:T(8,128)S(1)}, f32[32,128]{1,0:T(8,128)S(1)}, u32[]{:S(2)}, u32[]{:S(2)}) collective-permute-start(f32[32,128]{1,0:T(8,128)S(1)} %get-tuple-element.12), channel_id=1, source_target_pairs={{4,0},{8,4},{12,8},{16,12},{20,16},{24,20},{28,24},{32,28},{36,32}... | collective-permute-start | bytes 49160 | tf_op jit(solution)/shard_map/ppermute | solution.py:387
  19.9 8.9 %collective-permute-start.2 = (f32[32,128]{1,0:T(8,128)S(1)}, f32[32,128]{1,0:T(8,128)S(1)}, u32[]{:S(2)}, u32[]{:S(2)}) collective-permute-start(f32[32,128]{1,0:T(8,128)S(1)} %get-tuple-element.13), channel_id=1, source_target_pairs={{0,1},{1,2},{2,3},{4,5},{5,6},{6,7},{8,9},{9,10},{10,11},{12,13},{... | collective-permute-start | bytes 49160 | tf_op jit(solution)/shard_map/ppermute | solution.py:388
  23.0 8.6 %collective-permute-start.3 = (f32[32,128]{1,0:T(8,128)S(1)}, f32[32,128]{1,0:T(8,128)S(1)}, u32[]{:S(2)}, u32[]{:S(2)}) collective-permute-start(f32[32,128]{1,0:T(8,128)S(1)} %get-tuple-element.14), channel_id=1, source_target_pairs={{1,0},{2,1},{3,2},{5,4},{6,5},{7,6},{9,8},{10,9},{11,10},{13,12},{... | collective-permute-start | bytes 49160 | tf_op jit(solution)/shard_map/ppermute | solution.py:389

commit v4 on v3

--- a/solution.py
+++ b/solution.py
@@ -18,8 +18,9 @@
 BLOCK = CAP * SENT + 1
 LEV = 8
 CY = 32
-CONTRIB_SIZES = (16, 32, 48, 64, 96)
-STATE_SIZES = (64, 64, 64, 64)
+CONTRIB_SIZES = (32, 48, 80, 96)
+NEAR = 32
+FAR_SIZES = (48, 80, 96)
 
 VMEM = pltpu.VMEM
 SMEM = pltpu.SMEM
@@ -38,13 +39,14 @@
     return [(sum(sizes[:i]), size) for i, size in enumerate(sizes)]
 
 
-def block_copies(remap_hbm, weights, sems, sizes):
-    return [
-        pltpu.make_async_copy(
-            remap_hbm.at[pl.ds(start, size)], weights.at[pl.ds(start, size)], sems.at[i]
-        )
-        for i, (start, size) in enumerate(spans(sizes))
-    ]
+def block_copies(remap_hbm, near, far, sems, sizes, skipped=0):
+    copies = []
+    for i, (start, size) in enumerate(spans(sizes)):
+        first = skipped + start
+        inside = first < NEAR
+        target = near.at[pl.ds(first, size)] if inside else far.at[pl.ds(first - NEAR, size)]
+        copies.append(pltpu.make_async_copy(remap_hbm.at[pl.ds(first, size)], target, sems.at[i]))
+    return copies
 
 
 def in_hbm(x):
@@ -66,7 +68,8 @@
     remap_hbm,
     send,
     slot_out,
-    weights,
+    near,
+    far,
     flux,
     fields,
     owner,
@@ -76,7 +79,7 @@
     sems,
     sem2,
 ):
-    chunk_copies = block_copies(remap_hbm, weights, sems, CONTRIB_SIZES)
+    chunk_copies = block_copies(remap_hbm, near, far, sems, CONTRIB_SIZES)
     owner_copy = pltpu.make_async_copy(owner_hbm, owner, sem2.at[2])
     target_copy = pltpu.make_async_copy(target_hbm, target, sem2.at[3])
     flux_copy = pltpu.make_async_copy(flux_hbm, flux, sem2.at[0])
@@ -121,7 +124,8 @@
     def pair(r):
         high, low = split(fields[pl.ds(pl.multiple_of(r * SENT, 8), 8), :])
         left = jnp.concatenate([high, low], axis=0)
-        right = jnp.concatenate([weights[r], weights[r + 1]], axis=1)
+        blocks = [near[i] if i < NEAR else far[i - NEAR] for i in (r, r + 1)]
+        right = jnp.concatenate(blocks, axis=1)
         both = jnp.dot(left, right, preferred_element_type=F32)
         both = both[:8] + both[8:]
         first = slot_s[r // 128, r % 128]
@@ -141,11 +145,12 @@
         out_shape=(
             jax.ShapeDtypeStruct((DEV * BLOCK, CELLS), F32),
             jax.ShapeDtypeStruct((2, 128), jnp.int32),
+            VMEM((NEAR, 128, 128), BF16),
         ),
         in_specs=[pl.BlockSpec(memory_space=pltpu.HBM)] * 4,
-        out_specs=tuple(vmem_specs(2)),
+        out_specs=tuple(vmem_specs(3)),
         scratch_shapes=[
-            VMEM((ROWS, 128, 128), BF16),
+            VMEM((ROWS - NEAR, 128, 128), BF16),
             VMEM((6, ROWS, 128), F32),
             VMEM((ROWS * SENT, 128), F32),
             VMEM((2, 128), jnp.int32),
@@ -328,46 +333,68 @@
     )(got, carried, kappa, levels)
 
 
-def state_kernel(slots, returned, remap_hbm, out, weights, rows, sems):
-    chunk_copies = block_copies(remap_hbm, weights, sems, STATE_SIZES)
-    for copy in chunk_copies:
+def state_kernel(slots_in, returned, near, remap_hbm, out_hbm, far, rows, out, slots, sems, out_sems, sem):
+    far_copies = block_copies(remap_hbm, near, far, sems, FAR_SIZES, NEAR)
+    slot_copy = pltpu.make_async_copy(slots_in, slots, sem)
+    slot_copy.start()
+    for copy in far_copies:
         copy.start()
-
+    slot_copy.wait()
     for r in range(ROWS):
         rows[2 * r : 2 * r + 2, :] = returned[pl.ds(slots[r // 128, r % 128], 2), :]
-    for copy, (start, size) in zip(chunk_copies, spans(STATE_SIZES)):
+
+    def four_rows(r, blocks):
+        high, low = split(rows[2 * r : 2 * r + 8, :])
+        left = jnp.concatenate([high, low], axis=0)
+        four = lax.dot_general(
+            left,
+            blocks.reshape(4 * 128, 128),
+            (((1,), (1,)), ((), ())),
+            preferred_element_type=F32,
+        )
+        four = four[:8] + four[8:]
+        for j in range(4):
+            out[r + j] = four[2 * j : 2 * j + 2, j * 128 : (j + 1) * 128]
+
+    out_copies = []
+
+    def hand_on(start, size):
+        part = pl.ds(start, size)
+        copy = pltpu.make_async_copy(out.at[part], out_hbm.at[part], out_sems.at[len(out_copies)])
+        copy.start()
+        out_copies.append(copy)
+
+    for r in range(0, NEAR, 4):
+        four_rows(r, near[r : r + 4])
+    hand_on(0, NEAR)
+    for copy, (start, size) in zip(far_copies, spans(FAR_SIZES)):
         copy.wait()
         for r in range(start, start + size, 4):
-            high, low = split(rows[2 * r : 2 * r + 8, :])
-            left = jnp.concatenate([high, low], axis=0)
-            right = weights[r : r + 4].reshape(4 * 128, 128)
-            four = lax.dot_general(
-                left, right, (((1,), (1,)), ((), ())), preferred_element_type=F32
-            )
-            four = four[:8] + four[8:]
-            for j in range(4):
-                out[r + j] = four[2 * j : 2 * j + 2, j * 128 : (j + 1) * 128]
-
-
-def state(slots, returned, remap):
+            four_rows(NEAR + r, far[r : r + 4])
+        hand_on(NEAR + start, size)
+    for copy in out_copies:
+        copy.wait()
+
+
+def state(slots, returned, near, remap):
     return pl.pallas_call(
         state_kernel,
-        out_shape=jax.ShapeDtypeStruct((ROWS, 2, 128), F32),
-        in_specs=[
-            pl.BlockSpec(memory_space=SMEM),
-            pl.BlockSpec(memory_space=VMEM),
-            pl.BlockSpec(memory_space=pltpu.HBM),
+        out_shape=pltpu.HBM((ROWS, 2, 128), F32),
+        in_specs=vmem_specs(3) + [pl.BlockSpec(memory_space=pltpu.HBM)],
+        out_specs=pl.BlockSpec(memory_space=pltpu.HBM),
+        scratch_shapes=[
+            VMEM((ROWS - NEAR, 128, 128), BF16),
+            VMEM((2 * ROWS, 128), F32),
+            VMEM((ROWS, 2, 128), F32),
+            SMEM((2, 128), jnp.int32),
+            pltpu.SemaphoreType.DMA((len(FAR_SIZES),)),
+            pltpu.SemaphoreType.DMA((len(FAR_SIZES) + 1,)),
+            pltpu.SemaphoreType.DMA,
         ],
-        out_specs=pl.BlockSpec(memory_space=VMEM),
-        scratch_shapes=[
-            VMEM((ROWS, 128, 128), BF16),
-            VMEM((2 * ROWS, 128), F32),
-            pltpu.SemaphoreType.DMA((len(STATE_SIZES),)),
-        ],
-        compiler_params=params(24),
+        compiler_params=params(20),
         cost_estimate=pl.CostEstimate(flops=10**9, bytes_accessed=9_000_000, transcendentals=0),
         name="state",
-    )(slots, returned, remap)
+    )(slots, returned, near, remap)
 
 
 def shifts(count, wraps):
@@ -387,7 +414,7 @@
     east_in = lax.ppermute(to_west, "lon", westward)
     south_in = lax.ppermute(to_north, "lat", northward)
     north_in = lax.ppermute(to_south, "lat", southward)
-    send, slots = contributions(
+    send, slots, near = contributions(
         in_hbm(row_owner.reshape(2, 128)),
         in_hbm(row_target.reshape(2, 128)),
         in_hbm(jnp.transpose(atmos_flux, (1, 0, 2))),
@@ -399,7 +426,12 @@
     carried = advected(planes, east_vel, north_vel, levels, west_in, east_in, south_in, north_in)
     after, answer = ocean(got.reshape(DEV * BLOCK, CELLS), carried, mix_kappa, levels)
     returned = lax.all_to_all(answer, axes, split_axis=0, concat_axis=0, tiled=True)
-    atmos_state = state(slots, returned.reshape(DEV * 2 * CAP, CELLS), in_hbm(remap_blocks))
+    atmos_state = state(
+        slots,
+        returned.reshape(DEV * 2 * CAP, CELLS),
+        pltpu.with_memory_space_constraint(near, VMEM),
+        in_hbm(remap_blocks),
+    )
     return after.reshape(2, LEV, CY, CELLS), atmos_state
 
 

time: 63.2 us -> 62.4 us (0.987)
  Pallas kernels: 13.5 us -> 12.7 us
    pallas_call x1, Pallas kernels: 5.53 us -> 4.84 us  [state(): pl.pallas_call(state_kernel, out_shape=pltpu.HBM((ROWS, 2, 128), F32), in...]
where the time goes in v4:
time: 62.4 us; the launch traced here: 62.2 us
  blocking collectives  17.9 us (29%)
  starting transfers between devices  17.7 us (28%)
  waiting for transfers between devices  13.1 us (21%)
  Pallas kernels  12.7 us (20%)
  between operations  0.76 us (1%)
    all_to_all x1, blocking collectives, on_device(): lax.all_to_all(answer, axes, split_axis=0, concat_axis=0, tiled=True)  17.9 us
    all_to_all x1, starting transfers between devices, on_device(): lax.all_to_all(send.reshape(DEV, BLOCK, 1, CELLS), axes, split_axis=0, co...  11.5 us
    all_to_all x1, waiting for transfers between devices, on_device(): lax.all_to_all(send.reshape(DEV, BLOCK, 1, CELLS), axes, split_axis=0, co...  5.82 us
    pallas_call x1, Pallas kernels, contributions(): pl.pallas_call(contrib_kernel, out_shape=(jax.ShapeDtypeStruct((DEV * BLO...  5.46 us
    pallas_call x1, Pallas kernels, state(): pl.pallas_call(state_kernel, out_shape=pltpu.HBM((ROWS, 2, 128), F32), in...  4.84 us
    ppermute x1, waiting for transfers between devices, on_device(): south_in = lax.ppermute(to_north, 'lat', northward)  3.53 us
    ppermute x1, starting transfers between devices, on_device(): south_in = lax.ppermute(to_north, 'lat', northward)  3.09 us
    ppermute x1, waiting for transfers between devices, on_device(): north_in = lax.ppermute(to_south, 'lat', southward)  2.78 us
  transfers between devices with their start and end apart: 5, of which 4 were waited for; matrix products, arithmetic and copies ran while one was open for 0% of the time, Pallas kernels for 2%

profile of v4, /device:TPU:1, one launch (start us, length us, event | category | flops | bytes accessed | tf_op | source)
XLA Modules:
  0.0 62.2 jit_solution(9009342129788606058)
XLA Ops:
  0.6 5.5 %contrib.1 = (f32[2176,128]{1,0:T(8,128)}, s32[2,128]{1,0:T(2,128)S(1)}, bf16[32,128,128]{2,1,0:T(8,128)(2,1)S(1)}) custom-call(s32[2,128]{1,0:T(2,128)} %bitcast.13, s32[2,128]{1,0:T(2,128)} %bitcast.14, f32[6,256,128]{2,1,0:T(8,128)} %bitcast.12, bf16[256,128,128]{2,1,0:T(8,128)(2,1)} %remap_hbm.3), custom_call_target="tpu_custom_call" | custom-call | flops 1000000000 | bytes 10000000 | tf_op jit(solution)/shard_map/contrib/pallas_call | solution.py:143
  6.1 0.0 copy-start
  6.1 0.0 copy-start.1
  6.1 0.0 copy-start.2
  6.1 0.0 copy-start.3
  6.1 11.5 %all-to-all-start = ((f32[128,17,1,128]{3,2,1,0:T(1,128)}), f32[128,17,1,128]{3,2,1,0:T(1,128)S(1)}, u32[]{:S(2)}, u32[]{:S(2)}) async-start(f32[128,17,1,128]{3,2,1,0:T(1,128)} %bitcast.3), calls=%async_computation | async-start | bytes 2228224 | tf_op jit(solution)/shard_map/all_to_all | solution.py:423
  17.7 0.0 copy-start.4
  17.7 0.0 copy-done
  17.7 0.0 copy-done.1
  17.7 0.0 copy-done.2
  17.7 0.0 copy-done.3
  17.7 0.2 edges.1
  17.9 1.8 %collective-permute-start = (f32[32,128]{1,0:T(8,128)S(1)}, f32[32,128]{1,0:T(8,128)S(1)}, u32[]{:S(2)}, u32[]{:S(2)}) collective-permute-start(f32[32,128]{1,0:T(8,128)S(1)} %get-tuple-element.12), channel_id=1, source_target_pairs={{0,4},{4,8},{8,12},{12,16},{16,20},{20,24},{24,28},{28,32},{32,36}... | collective-permute-start | bytes 49160 | tf_op jit(solution)/shard_map/ppermute | solution.py:413
  19.8 0.0 collective-permute-start.1
  19.8 3.1 %collective-permute-start.2 = (f32[32,128]{1,0:T(8,128)S(1)}, f32[32,128]{1,0:T(8,128)S(1)}, u32[]{:S(2)}, u32[]{:S(2)}) collective-permute-start(f32[32,128]{1,0:T(8,128)S(1)} %get-tuple-element.14), channel_id=1, source_target_pairs={{0,1},{1,2},{2,3},{4,5},{5,6},{6,7},{8,9},{9,10},{10,11},{12,13},{... | collective-permute-start | bytes 49160 | tf_op jit(solution)/shard_map/ppermute | solution.py:415
  22.9 1.3 %collective-permute-start.3 = (f32[32,128]{1,0:T(8,128)S(1)}, f32[32,128]{1,0:T(8,128)S(1)}, u32[]{:S(2)}, u32[]{:S(2)}) collective-permute-start(f32[32,128]{1,0:T(8,128)S(1)} %get-tuple-element.15), channel_id=1, source_target_pairs={{1,0},{2,1},{3,2},{5,4},{6,5},{7,6},{9,8},{10,9},{11,10},{13,12},{... | collective-permute-start | bytes 49160 | tf_op jit(solution)/shard_map/ppermute | solution.py:416
  24.2 0.0 collective-permute-done.west_in
  24.2 0.9 %collective-permute-done.1.east_in = f32[32,128]{1,0:T(8,128)S(1)} collective-permute-done((f32[32,128]{1,0:T(8,128)S(1)}, f32[32,128]{1,0:T(8,128)S(1)}, u32[]{:S(2)}, u32[]{:S(2)}) %collective-permute-start.1) | collective-permute-done | bytes 16416 | tf_op jit(solution)/shard_map/ppermute | solution.py:414
  25.1 3.5 %collective-permute-done.2.south_in = f32[32,128]{1,0:T(8,128)S(1)} collective-permute-done((f32[32,128]{1,0:T(8,128)S(1)}, f32[32,128]{1,0:T(8,128)S(1)}, u32[]{:S(2)}, u32[]{:S(2)}) %collective-permute-start.2) | collective-permute-done | bytes 16416 | tf_op jit(solution)/shard_map/ppermute | solution.py:415
  28.7 2.8 %collective-permute-done.3.north_in = f32[32,128]{1,0:T(8,128)S(1)} collective-permute-done((f32[32,128]{1,0:T(8,128)S(1)}, f32[32,128]{1,0:T(8,128)S(1)}, u32[]{:S(2)}, u32[]{:S(2)}) %collective-permute-start.3) | collective-permute-done | bytes 16416 | tf_op jit(solution)/shard_map/ppermute | solution.py:416
  31.4 1.0 %advect.1.carried = f32[16,32,128]{2,1,0:T(8,128)S(1)} custom-call(f32[16,32,128]{2,1,0:T(8,128)S(1)} %bitcast.11, f32[8,32,128]{2,1,0:T(8,128)S(1)} %copy-done.1, f32[8,32,128]{2,1,0:T(8,128)S(1)} %copy-done.2, s32[32,128]{1,0:T(8,128)S(1)} %copy-done.3, f32[32,128]{1,0:T(8,128)S(1)} %collective-permute-done.west_in, ...), custom_call_target="tpu_custom_call" | custom-call | flops 1000000 | bytes 2000000 | tf_op jit(solution)/shard_map/advect/pallas_call | solution.py:249
  32.5 5.8 %all-to-all-done = f32[128,17,1,128]{3,2,1,0:T(1,128)S(1)} async-done(((f32[128,17,1,128]{3,2,1,0:T(1,128)}), f32[128,17,1,128]{3,2,1,0:T(1,128)S(1)}, u32[]{:S(2)}, u32[]{:S(2)}) %all-to-all-start) | async-done | bytes 1114144 | tf_op jit(solution)/shard_map/all_to_all | solution.py:423
  38.3 0.0 copy-done.4
  38.3 1.1 %ocean.1 = (f32[16,32,128]{2,1,0:T(8,128)}, f32[128,8,128]{2,1,0:T(8,128)S(1)}) custom-call(f32[2176,128]{1,0:T(8,128)S(1)} %bitcast.8, f32[16,32,128]{2,1,0:T(8,128)S(1)} %advect.1.carried, f32[8,32,128]{2,1,0:T(8,128)S(1)} %copy-done.4, s32[32,128]{1,0:T(8,128)S(1)} %copy-done.3), custom_call_target="tpu_custom_call" | custom-call | flops 100000000 | bytes 4000000 | tf_op jit(solution)/shard_map/ocean/pallas_call | solution.py:322
  39.4 17.9 %all_to_all.10 = f32[128,8,128]{2,1,0:T(8,128)S(1)} all-to-all(f32[128,8,128]{2,1,0:T(8,128)S(1)} %get-tuple-element.18), channel_id=1, replica_groups=mesh['lon'=32,'lat'=4] {'lon','lat'}, dimensions={0} | all-to-all | bytes 1048576 | tf_op jit(solution)/shard_map/all_to_all | solution.py:428
  57.3 4.8 %state.1 = f32[256,2,128]{2,1,0:T(2,128)} custom-call(s32[2,128]{1,0:T(2,128)S(1)} %get-tuple-element.17.slots_in, f32[1024,128]{1,0:T(8,128)S(1)} %bitcast.9, bf16[32,128,128]{2,1,0:T(8,128)(2,1)S(1)} %get-tuple-element.19.near, bf16[256,128,128]{2,1,0:T(8,128)(2,1)} %remap_hbm.3), custom_call_target="tpu_custom_call" | custom-call | flops 1000000000 | bytes 9000000 | tf_op jit(solution)/shard_map/state/pallas_call | solution.py:380
Async XLA Ops:
  6.1 11.6 %copy-start = (f32[2,8,32,128]{3,2,1,0:T(8,128)S(1)}, f32[2,8,32,128]{3,2,1,0:T(8,128)}, u32[]{:S(2)}) copy-start(f32[2,8,32,128]{3,2,1,0:T(8,128)} %param.13) | copy-start | bytes 786436
  6.1 11.6 %copy-start.1 = (f32[8,32,128]{2,1,0:T(8,128)S(1)}, f32[8,32,128]{2,1,0:T(8,128)}, u32[]{:S(2)}) copy-start(f32[8,32,128]{2,1,0:T(8,128)} %east_vel.3) | copy-start | bytes 393220
  6.1 11.6 %copy-start.2 = (f32[8,32,128]{2,1,0:T(8,128)S(1)}, f32[8,32,128]{2,1,0:T(8,128)}, u32[]{:S(2)}) copy-start(f32[8,32,128]{2,1,0:T(8,128)} %north_vel.3) | copy-start | bytes 393220
  6.1 11.6 %copy-start.3 = (s32[32,128]{1,0:T(8,128)S(1)}, s32[32,128]{1,0:T(8,128)}, u32[]{:S(2)}) copy-start(s32[32,128]{1,0:T(8,128)} %levels.5) | copy-start | bytes 49156
  6.1 32.1 %all-to-all-start = ((f32[128,17,1,128]{3,2,1,0:T(1,128)}), f32[128,17,1,128]{3,2,1,0:T(1,128)S(1)}, u32[]{:S(2)}, u32[]{:S(2)}) async-start(f32[128,17,1,128]{3,2,1,0:T(1,128)} %bitcast.3), calls=%async_computation | async-start | bytes 2228224 | tf_op jit(solution)/shard_map/all_to_all | solution.py:423
  17.7 20.6 %copy-start.4 = (f32[8,32,128]{2,1,0:T(8,128)S(1)}, f32[8,32,128]{2,1,0:T(8,128)}, u32[]{:S(2)}) copy-start(f32[8,32,128]{2,1,0:T(8,128)} %kappa.1) | copy-start | bytes 393220
  17.9 6.2 %collective-permute-start = (f32[32,128]{1,0:T(8,128)S(1)}, f32[32,128]{1,0:T(8,128)S(1)}, u32[]{:S(2)}, u32[]{:S(2)}) collective-permute-start(f32[32,128]{1,0:T(8,128)S(1)} %get-tuple-element.12), channel_id=1, source_target_pairs={{0,4},{4,8},{8,12},{12,16},{16,20},{20,24},{24,28},{28,32},{32,36}... | collective-permute-start | bytes 49160 | tf_op jit(solution)/shard_map/ppermute | solution.py:413
  19.8 5.4 %collective-permute-start.1 = (f32[32,128]{1,0:T(8,128)S(1)}, f32[32,128]{1,0:T(8,128)S(1)}, u32[]{:S(2)}, u32[]{:S(2)}) collective-permute-start(f32[32,128]{1,0:T(8,128)S(1)} %get-tuple-element.13), channel_id=1, source_target_pairs={{4,0},{8,4},{12,8},{16,12},{20,16},{24,20},{28,24},{32,28},{36,32}... | collective-permute-start | bytes 49160 | tf_op jit(solution)/shard_map/ppermute | solution.py:414
  19.8 8.9 %collective-permute-start.2 = (f32[32,128]{1,0:T(8,128)S(1)}, f32[32,128]{1,0:T(8,128)S(1)}, u32[]{:S(2)}, u32[]{:S(2)}) collective-permute-start(f32[32,128]{1,0:T(8,128)S(1)} %get-tuple-element.14), channel_id=1, source_target_pairs={{0,1},{1,2},{2,3},{4,5},{5,6},{6,7},{8,9},{9,10},{10,11},{12,13},{... | collective-permute-start | bytes 49160 | tf_op jit(solution)/shard_map/ppermute | solution.py:415
  22.9 8.6 %collective-permute-start.3 = (f32[32,128]{1,0:T(8,128)S(1)}, f32[32,128]{1,0:T(8,128)S(1)}, u32[]{:S(2)}, u32[]{:S(2)}) collective-permute-start(f32[32,128]{1,0:T(8,128)S(1)} %get-tuple-element.15), channel_id=1, source_target_pairs={{1,0},{2,1},{3,2},{5,4},{6,5},{7,6},{9,8},{10,9},{11,10},{13,12},{... | collective-permute-start | bytes 49160 | tf_op jit(solution)/shard_map/ppermute | solution.py:416

commit v5 on v4

--- a/solution.py
+++ b/solution.py
@@ -201,55 +201,33 @@
     )(tracers, east_vel, north_vel, levels)
 
 
-def advect_kernel(tracers, east_vel, north_vel, levels, west_in, east_in, south_in, north_in, out):
-    lane0 = iota((CY, 128), 1) == 0
+def advect_kernel(tracers, east_vel, north_vel, levels, out):
     lane_last = iota((CY, 128), 1) == 127
-    row0 = iota((CY, 128), 0) == 0
     row_last = iota((CY, 128), 0) == CY - 1
     lev = levels[...].astype(F32)
-
-    def from_west(p):
-        return west_in[...] if p == 0 else pltpu.roll(west_in[...], 128 - p, 1)
-
-    def from_east(p):
-        return pltpu.roll(east_in[...], 127 - p, 1)
-
-    lev_w = from_west(16)
-    lev_e = jnp.where(lane_last, from_east(16), pltpu.roll(lev, 127, 1))
-    lev_s = south_in[16:17, :]
-    lev_n = jnp.where(row_last, north_in[16:17, :], pltpu.roll(lev, CY - 1, 0))
+    lev_e = jnp.where(lane_last, 0.0, pltpu.roll(lev, 127, 1))
+    lev_n = jnp.where(row_last, 0.0, pltpu.roll(lev, CY - 1, 0))
     for k in range(LEV):
         depth = float(k)
         wet = (lev > depth).astype(F32)
-        wet_w = wet * (lev_w > depth).astype(F32)
         wet_e = wet * (lev_e > depth).astype(F32)
-        wet_s = wet * (lev_s > depth).astype(F32)
         wet_n = wet * (lev_n > depth).astype(F32)
         vel_e, vel_n = east_vel[k], north_vel[k]
-        vel_w, vel_s = from_west(17 + k), south_in[17 + k : 18 + k, :]
         e_pos, e_neg = jnp.maximum(vel_e, 0.0), jnp.minimum(vel_e, 0.0)
         n_pos, n_neg = jnp.maximum(vel_n, 0.0), jnp.minimum(vel_n, 0.0)
-        w_pos, w_neg = jnp.maximum(vel_w, 0.0), jnp.minimum(vel_w, 0.0)
-        s_pos, s_neg = jnp.maximum(vel_s, 0.0), jnp.minimum(vel_s, 0.0)
         for t in range(2):
             p = t * LEV + k
             here = tracers[p]
-            at_e = jnp.where(lane_last, from_east(p), pltpu.roll(here, 127, 1))
-            at_n = jnp.where(row_last, north_in[p : p + 1, :], pltpu.roll(here, CY - 1, 0))
-            flux_e = (e_pos * here + e_neg * at_e) * wet_e
-            flux_n = (n_pos * here + n_neg * at_n) * wet_n
-            edge_w = (w_pos * from_west(p) + w_neg * here) * wet_w
-            edge_s = (s_pos * south_in[p : p + 1, :] + s_neg * here) * wet_s
-            flux_w = jnp.where(lane0, edge_w, pltpu.roll(flux_e, 1, 1))
-            flux_s = jnp.where(row0, edge_s, pltpu.roll(flux_n, 1, 0))
-            out[p] = here - (flux_e - flux_w) - (flux_n - flux_s)
+            flux_e = (e_pos * here + e_neg * pltpu.roll(here, 127, 1)) * wet_e
+            flux_n = (n_pos * here + n_neg * pltpu.roll(here, CY - 1, 0)) * wet_n
+            out[p] = here - (flux_e - pltpu.roll(flux_e, 1, 1)) - (flux_n - pltpu.roll(flux_n, 1, 0))
 
 
 def advected(*args):
     return pl.pallas_call(
         advect_kernel,
         out_shape=jax.ShapeDtypeStruct((16, CY, 128), F32),
-        in_specs=vmem_specs(8),
+        in_specs=vmem_specs(4),
         out_specs=pl.BlockSpec(memory_space=VMEM),
         compiler_params=params(8),
         cost_estimate=pl.CostEstimate(flops=10**6, bytes_accessed=2_000_000, transcendentals=0),
@@ -257,7 +235,55 @@
     )(*args)
 
 
-def ocean_kernel(got, carried, kappa, levels, after, answer):
+def face(vel, low, high, lev_low, lev_high, depth):
+    wet = (lev_low > depth).astype(F32) * (lev_high > depth).astype(F32)
+    return (jnp.maximum(vel, 0.0) * low + jnp.minimum(vel, 0.0) * high) * wet
+
+
+def side_face(low, high):
+    lane = iota((CY, 128), 1)
+    packed = low[...]
+    vel = jnp.where(lane < LEV, pltpu.roll(packed, 128 - 17, 1), pltpu.roll(packed, 128 - 9, 1))
+    return face(
+        vel, packed, high[...], low[:, 16:17], high[:, 16:17], (lane % LEV).astype(F32)
+    )
+
+
+def end_face(low, high):
+    vel = jnp.concatenate([low[17 : 17 + LEV, :]] * 2, axis=0)
+    depth = (iota((2 * LEV, 128), 0) % LEV).astype(F32)
+    return face(
+        vel, low[0 : 2 * LEV, :], high[0 : 2 * LEV, :], low[16:17, :], high[16:17, :], depth
+    )
+
+
+def ocean_kernel(
+    got,
+    inner,
+    kappa,
+    levels,
+    to_east,
+    to_west,
+    to_north,
+    to_south,
+    west_in,
+    east_in,
+    south_in,
+    north_in,
+    after,
+    answer,
+):
+    lane, row = iota((CY, 128), 1), iota((CY, 128), 0)
+    from_west, to_next = side_face(west_in, to_west), side_face(to_east, east_in)
+    from_south, to_top = end_face(south_in, to_south), end_face(to_north, north_in)
+    carried = []
+    for p in range(2 * LEV):
+        west = from_west if p == 0 else pltpu.roll(from_west, 128 - p, 1)
+        sides = jnp.where(lane == 0, west, 0.0)
+        sides = jnp.where(lane == 127, -pltpu.roll(to_next, 127 - p, 1), sides)
+        ends = jnp.where(row == 0, from_south[p : p + 1, :], 0.0)
+        ends = jnp.where(row == CY - 1, -to_top[p : p + 1, :], ends)
+        carried.append(inner[p] + sides + ends)
     tags = jnp.transpose(got[pl.ds(CAP * SENT, DEV, stride=BLOCK), :])
     labels = iota((CY, DEV), 0).astype(F32) + 1.0
     select = jnp.concatenate(
@@ -318,19 +344,19 @@
             )
 
 
-def ocean(got, carried, kappa, levels):
+def ocean(*args):
     return pl.pallas_call(
         ocean_kernel,
         out_shape=(
             jax.ShapeDtypeStruct((16, CY, 128), F32),
             jax.ShapeDtypeStruct((DEV, 2 * CAP, CELLS), F32),
         ),
-        in_specs=vmem_specs(4),
+        in_specs=vmem_specs(12),
         out_specs=tuple(vmem_specs(2)),
         compiler_params=params(24),
         cost_estimate=pl.CostEstimate(flops=10**8, bytes_accessed=4_000_000, transcendentals=0),
         name="ocean",
-    )(got, carried, kappa, levels)
+    )(*args)
 
 
 def state_kernel(slots_in, returned, near, remap_hbm, out_hbm, far, rows, out, slots, sems, out_sems, sem):
@@ -423,8 +449,21 @@
     got = lax.all_to_all(
         send.reshape(DEV, BLOCK, 1, CELLS), axes, split_axis=0, concat_axis=0, tiled=True
     )
-    carried = advected(planes, east_vel, north_vel, levels, west_in, east_in, south_in, north_in)
-    after, answer = ocean(got.reshape(DEV * BLOCK, CELLS), carried, mix_kappa, levels)
+    inner = advected(planes, east_vel, north_vel, levels)
+    after, answer = ocean(
+        got.reshape(DEV * BLOCK, CELLS),
+        inner,
+        mix_kappa,
+        levels,
+        to_east,
+        to_west,
+        to_north,
+        to_south,
+        west_in,
+        east_in,
+        south_in,
+        north_in,
+    )
     returned = lax.all_to_all(answer, axes, split_axis=0, concat_axis=0, tiled=True)
     atmos_state = state(
         slots,

time: 62.4 us -> 61.7 us (0.989)
  waiting for transfers between devices: 13.1 us -> 13.8 us
  Pallas kernels: 12.7 us -> 12 us
  blocking collectives: 17.9 us -> 17.2 us
    all_to_all x1, waiting for transfers between devices: 5.82 us -> 6.85 us  [on_device(): lax.all_to_all(send.reshape(DEV, BLOCK, 1, CELLS), axes, split_axis=0, co...]
    pallas_call x1, Pallas kernels: 1.02 us -> 0.3 us  [advected(): pl.pallas_call(advect_kernel, out_shape=jax.ShapeDtypeStruct((16, CY, 128...]
    all_to_all x1, blocking collectives: 17.9 us -> 17.2 us  [on_device(): lax.all_to_all(answer, axes, split_axis=0, concat_axis=0, tiled=True)]
  transfers between devices with their start and end apart: 5 -> 5, of which waited for: 4 -> 4; matrix products, arithmetic and copies ran while one was open for 0% -> 0% of each run, Pallas kernels for 2% -> 1%
where the time goes in v5:
time: 61.7 us; the launch traced here: 61.5 us
  starting transfers between devices  17.7 us (29%)
  blocking collectives  17.2 us (28%)
  waiting for transfers between devices  13.8 us (22%)
  Pallas kernels  12 us (19%)
  between operations  0.76 us (1%)
    all_to_all x1, blocking collectives, on_device(): lax.all_to_all(answer, axes, split_axis=0, concat_axis=0, tiled=True)  17.2 us
    all_to_all x1, starting transfers between devices, on_device(): lax.all_to_all(send.reshape(DEV, BLOCK, 1, CELLS), axes, split_axis=0, co...  11.5 us
    all_to_all x1, waiting for transfers between devices, on_device(): lax.all_to_all(send.reshape(DEV, BLOCK, 1, CELLS), axes, split_axis=0, co...  6.85 us
    pallas_call x1, Pallas kernels, contributions(): pl.pallas_call(contrib_kernel, out_shape=(jax.ShapeDtypeStruct((DEV * BLO...  5.46 us
    pallas_call x1, Pallas kernels, state(): pl.pallas_call(state_kernel, out_shape=pltpu.HBM((ROWS, 2, 128), F32), in...  4.84 us
    ppermute x1, waiting for transfers between devices, on_device(): south_in = lax.ppermute(to_north, 'lat', northward)  3.53 us
    ppermute x1, starting transfers between devices, on_device(): south_in = lax.ppermute(to_north, 'lat', northward)  3.09 us
    ppermute x1, waiting for transfers between devices, on_device(): north_in = lax.ppermute(to_south, 'lat', southward)  2.78 us
  transfers between devices with their start and end apart: 5, of which 4 were waited for; matrix products, arithmetic and copies ran while one was open for 0% of the time, Pallas kernels for 1%

profile of v5, /device:TPU:1, one launch (start us, length us, event | category | flops | bytes accessed | tf_op | source)
XLA Modules:
  0.0 61.5 jit_solution(5097257768225134752)
XLA Ops:
  0.6 5.5 %contrib.1 = (f32[2176,128]{1,0:T(8,128)}, s32[2,128]{1,0:T(2,128)S(1)}, bf16[32,128,128]{2,1,0:T(8,128)(2,1)S(1)}) custom-call(s32[2,128]{1,0:T(2,128)} %bitcast.13, s32[2,128]{1,0:T(2,128)} %bitcast.14, f32[6,256,128]{2,1,0:T(8,128)} %bitcast.12, bf16[256,128,128]{2,1,0:T(8,128)(2,1)} %remap_hbm.3), custom_call_target="tpu_custom_call" | custom-call | flops 1000000000 | bytes 10000000 | tf_op jit(solution)/shard_map/contrib/pallas_call | solution.py:143
  6.1 0.0 copy-start
  6.1 0.0 copy-start.1
  6.1 0.0 copy-start.2
  6.1 0.0 copy-start.3
  6.1 11.5 %all-to-all-start = ((f32[128,17,1,128]{3,2,1,0:T(1,128)}), f32[128,17,1,128]{3,2,1,0:T(1,128)S(1)}, u32[]{:S(2)}, u32[]{:S(2)}) async-start(f32[128,17,1,128]{3,2,1,0:T(1,128)} %bitcast.3), calls=%async_computation | async-start | bytes 2228224 | tf_op jit(solution)/shard_map/all_to_all | solution.py:449
  17.7 0.0 copy-start.4
  17.7 0.0 copy-done
  17.7 0.0 copy-done.1
  17.7 0.0 copy-done.2
  17.7 0.0 copy-done.3
  17.7 0.2 edges.1
  17.9 1.8 %collective-permute-start = (f32[32,128]{1,0:T(8,128)S(1)}, f32[32,128]{1,0:T(8,128)S(1)}, u32[]{:S(2)}, u32[]{:S(2)}) collective-permute-start(f32[32,128]{1,0:T(8,128)S(1)} %get-tuple-element.12.to_east), channel_id=1, source_target_pairs={{0,4},{4,8},{8,12},{12,16},{16,20},{20,24},{24,28},{28,32},{32,36}... | collective-permute-start | bytes 49160 | tf_op jit(solution)/shard_map/ppermute | solution.py:439
  19.8 0.0 collective-permute-start.1
  19.8 3.1 %collective-permute-start.2 = (f32[32,128]{1,0:T(8,128)S(1)}, f32[32,128]{1,0:T(8,128)S(1)}, u32[]{:S(2)}, u32[]{:S(2)}) collective-permute-start(f32[32,128]{1,0:T(8,128)S(1)} %get-tuple-element.14.to_north), channel_id=1, source_target_pairs={{0,1},{1,2},{2,3},{4,5},{5,6},{6,7},{8,9},{9,10},{10,11},{12,13},{... | collective-permute-start | bytes 49160 | tf_op jit(solution)/shard_map/ppermute | solution.py:441
  22.9 1.3 %collective-permute-start.3 = (f32[32,128]{1,0:T(8,128)S(1)}, f32[32,128]{1,0:T(8,128)S(1)}, u32[]{:S(2)}, u32[]{:S(2)}) collective-permute-start(f32[32,128]{1,0:T(8,128)S(1)} %get-tuple-element.15.to_south), channel_id=1, source_target_pairs={{1,0},{2,1},{3,2},{5,4},{6,5},{7,6},{9,8},{10,9},{11,10},{13,12},{... | collective-permute-start | bytes 49160 | tf_op jit(solution)/shard_map/ppermute | solution.py:442
  24.2 0.3 advect.1.inner
  24.5 0.0 collective-permute-done.west_in
  24.5 0.6 %collective-permute-done.1.east_in = f32[32,128]{1,0:T(8,128)S(1)} collective-permute-done((f32[32,128]{1,0:T(8,128)S(1)}, f32[32,128]{1,0:T(8,128)S(1)}, u32[]{:S(2)}, u32[]{:S(2)}) %collective-permute-start.1) | collective-permute-done | bytes 16416 | tf_op jit(solution)/shard_map/ppermute | solution.py:440
  25.1 3.5 %collective-permute-done.2.south_in = f32[32,128]{1,0:T(8,128)S(1)} collective-permute-done((f32[32,128]{1,0:T(8,128)S(1)}, f32[32,128]{1,0:T(8,128)S(1)}, u32[]{:S(2)}, u32[]{:S(2)}) %collective-permute-start.2) | collective-permute-done | bytes 16416 | tf_op jit(solution)/shard_map/ppermute | solution.py:441
  28.7 2.8 %collective-permute-done.3.north_in = f32[32,128]{1,0:T(8,128)S(1)} collective-permute-done((f32[32,128]{1,0:T(8,128)S(1)}, f32[32,128]{1,0:T(8,128)S(1)}, u32[]{:S(2)}, u32[]{:S(2)}) %collective-permute-start.3) | collective-permute-done | bytes 16416 | tf_op jit(solution)/shard_map/ppermute | solution.py:442
  31.4 6.9 %all-to-all-done = f32[128,17,1,128]{3,2,1,0:T(1,128)S(1)} async-done(((f32[128,17,1,128]{3,2,1,0:T(1,128)}), f32[128,17,1,128]{3,2,1,0:T(1,128)S(1)}, u32[]{:S(2)}, u32[]{:S(2)}) %all-to-all-start) | async-done | bytes 1114144 | tf_op jit(solution)/shard_map/all_to_all | solution.py:449
  38.3 0.0 copy-done.4
  38.3 1.2 %ocean.1 = (f32[16,32,128]{2,1,0:T(8,128)}, f32[128,8,128]{2,1,0:T(8,128)S(1)}) custom-call(f32[2176,128]{1,0:T(8,128)S(1)} %bitcast.8, f32[16,32,128]{2,1,0:T(8,128)S(1)} %advect.1.inner, f32[8,32,128]{2,1,0:T(8,128)S(1)} %copy-done.4, s32[32,128]{1,0:T(8,128)S(1)} %copy-done.3, f32[32,128]{1,0:T(8,128)S(1)} %get-tuple-element.12.to_east, ...), custom_call_target="tpu_custom_call" | custom-call | flops 100000000 | bytes 4000000 | tf_op jit(solution)/shard_map/ocean/pallas_call | solution.py:348
  39.4 17.2 %all_to_all.10 = f32[128,8,128]{2,1,0:T(8,128)S(1)} all-to-all(f32[128,8,128]{2,1,0:T(8,128)S(1)} %get-tuple-element.18), channel_id=1, replica_groups=mesh['lon'=32,'lat'=4] {'lon','lat'}, dimensions={0} | all-to-all | bytes 1048576 | tf_op jit(solution)/shard_map/all_to_all | solution.py:467
  56.7 4.8 %state.1 = f32[256,2,128]{2,1,0:T(2,128)} custom-call(s32[2,128]{1,0:T(2,128)S(1)} %get-tuple-element.17.slots_in, f32[1024,128]{1,0:T(8,128)S(1)} %bitcast.9, bf16[32,128,128]{2,1,0:T(8,128)(2,1)S(1)} %get-tuple-element.19.near, bf16[256,128,128]{2,1,0:T(8,128)(2,1)} %remap_hbm.3), custom_call_target="tpu_custom_call" | custom-call | flops 1000000000 | bytes 9000000 | tf_op jit(solution)/shard_map/state/pallas_call | solution.py:406
Async XLA Ops:
  6.1 11.6 %copy-start = (f32[2,8,32,128]{3,2,1,0:T(8,128)S(1)}, f32[2,8,32,128]{3,2,1,0:T(8,128)}, u32[]{:S(2)}) copy-start(f32[2,8,32,128]{3,2,1,0:T(8,128)} %param.13) | copy-start | bytes 786436
  6.1 11.6 %copy-start.1 = (f32[8,32,128]{2,1,0:T(8,128)S(1)}, f32[8,32,128]{2,1,0:T(8,128)}, u32[]{:S(2)}) copy-start(f32[8,32,128]{2,1,0:T(8,128)} %east_vel.3) | copy-start | bytes 393220
  6.1 11.6 %copy-start.2 = (f32[8,32,128]{2,1,0:T(8,128)S(1)}, f32[8,32,128]{2,1,0:T(8,128)}, u32[]{:S(2)}) copy-start(f32[8,32,128]{2,1,0:T(8,128)} %north_vel.3) | copy-start | bytes 393220
  6.1 11.6 %copy-start.3 = (s32[32,128]{1,0:T(8,128)S(1)}, s32[32,128]{1,0:T(8,128)}, u32[]{:S(2)}) copy-start(s32[32,128]{1,0:T(8,128)} %levels.5) | copy-start | bytes 49156
  6.1 32.1 %all-to-all-start = ((f32[128,17,1,128]{3,2,1,0:T(1,128)}), f32[128,17,1,128]{3,2,1,0:T(1,128)S(1)}, u32[]{:S(2)}, u32[]{:S(2)}) async-start(f32[128,17,1,128]{3,2,1,0:T(1,128)} %bitcast.3), calls=%async_computation | async-start | bytes 2228224 | tf_op jit(solution)/shard_map/all_to_all | solution.py:449
  17.7 20.6 %copy-start.4 = (f32[8,32,128]{2,1,0:T(8,128)S(1)}, f32[8,32,128]{2,1,0:T(8,128)}, u32[]{:S(2)}) copy-start(f32[8,32,128]{2,1,0:T(8,128)} %kappa.1) | copy-start | bytes 393220
  17.9 6.5 %collective-permute-start = (f32[32,128]{1,0:T(8,128)S(1)}, f32[32,128]{1,0:T(8,128)S(1)}, u32[]{:S(2)}, u32[]{:S(2)}) collective-permute-start(f32[32,128]{1,0:T(8,128)S(1)} %get-tuple-element.12.to_east), channel_id=1, source_target_pairs={{0,4},{4,8},{8,12},{12,16},{16,20},{20,24},{24,28},{28,32},{32,36}... | collective-permute-start | bytes 49160 | tf_op jit(solution)/shard_map/ppermute | solution.py:439
  19.8 5.4 %collective-permute-start.1 = (f32[32,128]{1,0:T(8,128)S(1)}, f32[32,128]{1,0:T(8,128)S(1)}, u32[]{:S(2)}, u32[]{:S(2)}) collective-permute-start(f32[32,128]{1,0:T(8,128)S(1)} %get-tuple-element.13.to_west), channel_id=1, source_target_pairs={{4,0},{8,4},{12,8},{16,12},{20,16},{24,20},{28,24},{32,28},{36,32}... | collective-permute-start | bytes 49160 | tf_op jit(solution)/shard_map/ppermute | solution.py:440
  19.8 8.9 %collective-permute-start.2 = (f32[32,128]{1,0:T(8,128)S(1)}, f32[32,128]{1,0:T(8,128)S(1)}, u32[]{:S(2)}, u32[]{:S(2)}) collective-permute-start(f32[32,128]{1,0:T(8,128)S(1)} %get-tuple-element.14.to_north), channel_id=1, source_target_pairs={{0,1},{1,2},{2,3},{4,5},{5,6},{6,7},{8,9},{9,10},{10,11},{12,13},{... | collective-permute-start | bytes 49160 | tf_op jit(solution)/shard_map/ppermute | solution.py:441
  22.9 8.6 %collective-permute-start.3 = (f32[32,128]{1,0:T(8,128)S(1)}, f32[32,128]{1,0:T(8,128)S(1)}, u32[]{:S(2)}, u32[]{:S(2)}) collective-permute-start(f32[32,128]{1,0:T(8,128)S(1)} %get-tuple-element.15.to_south), channel_id=1, source_target_pairs={{1,0},{2,1},{3,2},{5,4},{6,5},{7,6},{9,8},{10,9},{11,10},{13,12},{... | collective-permute-start | bytes 49160 | tf_op jit(solution)/shard_map/ppermute | solution.py:442

commit v6 on v5

--- a/solution.py
+++ b/solution.py
@@ -20,7 +20,10 @@
 CY = 32
 CONTRIB_SIZES = (32, 48, 80, 96)
 NEAR = 32
-FAR_SIZES = (48, 80, 96)
+MID = 24
+FAR_SIZES = (40, 64)
+TURNED = 96
+PIECE = 32
 
 VMEM = pltpu.VMEM
 SMEM = pltpu.SMEM
@@ -270,6 +273,7 @@
     east_in,
     south_in,
     north_in,
+    turned_hbm,
     after,
     answer,
 ):
@@ -351,7 +355,7 @@
             jax.ShapeDtypeStruct((16, CY, 128), F32),
             jax.ShapeDtypeStruct((DEV, 2 * CAP, CELLS), F32),
         ),
-        in_specs=vmem_specs(12),
+        in_specs=vmem_specs(12) + [pl.BlockSpec(memory_space=pltpu.HBM)],
         out_specs=tuple(vmem_specs(2)),
         compiler_params=params(24),
         cost_estimate=pl.CostEstimate(flops=10**8, bytes_accessed=4_000_000, transcendentals=0),
@@ -359,25 +363,80 @@
     )(*args)
 
 
-def state_kernel(slots_in, returned, near, remap_hbm, out_hbm, far, rows, out, slots, sems, out_sems, sem):
-    far_copies = block_copies(remap_hbm, near, far, sems, FAR_SIZES, NEAR)
+def turn_kernel(inner, remap_hbm, turned_hbm, mid, blocks, turned, mid_blocks, in_sems, out_sems):
+    parts = [pl.ds(i * PIECE, PIECE) for i in range(TURNED // PIECE)]
+    reads = [
+        pltpu.make_async_copy(
+            remap_hbm.at[pl.ds(ROWS - TURNED + i * PIECE, PIECE)], blocks.at[part], in_sems.at[i]
+        )
+        for i, part in enumerate(parts)
+    ]
+    writes = [
+        pltpu.make_async_copy(turned.at[part], turned_hbm.at[part], out_sems.at[i])
+        for i, part in enumerate(parts)
+    ]
+    mid_read = pltpu.make_async_copy(
+        remap_hbm.at[pl.ds(NEAR, MID)], mid_blocks, in_sems.at[TURNED // PIECE]
+    )
+    for read in reads:
+        read.start()
+    mid_read.start()
+    for i, (read, write) in enumerate(zip(reads, writes)):
+        read.wait()
+        for r in range(i * PIECE, (i + 1) * PIECE):
+            turned[r] = blocks[r].T
+        write.start()
+    mid_read.wait()
+    for r in range(MID):
+        mid[r] = mid_blocks[r].T
+    for write in writes:
+        write.wait()
+
+
+def turn(inner, remap):
+    return pl.pallas_call(
+        turn_kernel,
+        out_shape=(pltpu.HBM((TURNED, 128, 128), BF16), VMEM((MID, 128, 128), BF16)),
+        in_specs=vmem_specs(1) + [pl.BlockSpec(memory_space=pltpu.HBM)],
+        out_specs=(pl.BlockSpec(memory_space=pltpu.HBM), pl.BlockSpec(memory_space=VMEM)),
+        scratch_shapes=[
+            VMEM((TURNED, 128, 128), BF16),
+            VMEM((TURNED, 128, 128), BF16),
+            VMEM((MID, 128, 128), BF16),
+            pltpu.SemaphoreType.DMA((TURNED // PIECE + 1,)),
+            pltpu.SemaphoreType.DMA((TURNED // PIECE,)),
+        ],
+        compiler_params=params(16),
+        cost_estimate=pl.CostEstimate(flops=10**6, bytes_accessed=6_000_000, transcendentals=0),
+        name="turn",
+    )(inner, remap)
+
+
+def state_kernel(slots_in, returned, near, mid, remap_hbm, turned_hbm, out_hbm, far, turned, rows, out, slots, sems, out_sems, sem):
+    far_copies = block_copies(remap_hbm, near, far, sems, FAR_SIZES, NEAR + MID)
     slot_copy = pltpu.make_async_copy(slots_in, slots, sem)
     slot_copy.start()
+    turned_copy = pltpu.make_async_copy(turned_hbm, turned, sems.at[len(FAR_SIZES)])
     for copy in far_copies:
         copy.start()
+    turned_copy.start()
     slot_copy.wait()
     for r in range(ROWS):
         rows[2 * r : 2 * r + 2, :] = returned[pl.ds(slots[r // 128, r % 128], 2), :]
 
-    def four_rows(r, blocks):
+    def four_rows(r, blocks, transposed=False):
         high, low = split(rows[2 * r : 2 * r + 8, :])
         left = jnp.concatenate([high, low], axis=0)
-        four = lax.dot_general(
-            left,
-            blocks.reshape(4 * 128, 128),
-            (((1,), (1,)), ((), ())),
-            preferred_element_type=F32,
-        )
+        if transposed:
+            right = jnp.concatenate([blocks[j] for j in range(4)], axis=1)
+            four = jnp.dot(left, right, preferred_element_type=F32)
+        else:
+            four = lax.dot_general(
+                left,
+                blocks.reshape(4 * 128, 128),
+                (((1,), (1,)), ((), ())),
+                preferred_element_type=F32,
+            )
         four = four[:8] + four[8:]
         for j in range(4):
             out[r + j] = four[2 * j : 2 * j + 2, j * 128 : (j + 1) * 128]
@@ -392,35 +451,42 @@
 
     for r in range(0, NEAR, 4):
         four_rows(r, near[r : r + 4])
-    hand_on(0, NEAR)
+    for r in range(0, MID, 4):
+        four_rows(NEAR + r, mid[r : r + 4], True)
+    hand_on(0, NEAR + MID)
     for copy, (start, size) in zip(far_copies, spans(FAR_SIZES)):
         copy.wait()
-        for r in range(start, start + size, 4):
+        for r in range(MID + start, MID + start + size, 4):
             four_rows(NEAR + r, far[r : r + 4])
-        hand_on(NEAR + start, size)
+        hand_on(NEAR + MID + start, size)
+    turned_copy.wait()
+    for r in range(0, TURNED, 4):
+        four_rows(ROWS - TURNED + r, turned[r : r + 4], True)
+    hand_on(ROWS - TURNED, TURNED)
     for copy in out_copies:
         copy.wait()
 
 
-def state(slots, returned, near, remap):
+def state(slots, returned, near, mid, remap, turned):
     return pl.pallas_call(
         state_kernel,
         out_shape=pltpu.HBM((ROWS, 2, 128), F32),
-        in_specs=vmem_specs(3) + [pl.BlockSpec(memory_space=pltpu.HBM)],
+        in_specs=vmem_specs(4) + [pl.BlockSpec(memory_space=pltpu.HBM)] * 2,
         out_specs=pl.BlockSpec(memory_space=pltpu.HBM),
         scratch_shapes=[
-            VMEM((ROWS - NEAR, 128, 128), BF16),
+            VMEM((ROWS - NEAR - TURNED, 128, 128), BF16),
+            VMEM((TURNED, 128, 128), BF16),
             VMEM((2 * ROWS, 128), F32),
             VMEM((ROWS, 2, 128), F32),
             SMEM((2, 128), jnp.int32),
-            pltpu.SemaphoreType.DMA((len(FAR_SIZES),)),
             pltpu.SemaphoreType.DMA((len(FAR_SIZES) + 1,)),
+            pltpu.SemaphoreType.DMA((len(FAR_SIZES) + 2,)),
             pltpu.SemaphoreType.DMA,
         ],
         compiler_params=params(20),
         cost_estimate=pl.CostEstimate(flops=10**9, bytes_accessed=9_000_000, transcendentals=0),
         name="state",
-    )(slots, returned, near, remap)
+    )(slots, returned, near, mid, remap, turned)
 
 
 def shifts(count, wraps):
@@ -450,6 +516,7 @@
         send.reshape(DEV, BLOCK, 1, CELLS), axes, split_axis=0, concat_axis=0, tiled=True
     )
     inner = advected(planes, east_vel, north_vel, levels)
+    turned, mid = turn(inner, in_hbm(remap_blocks))
     after, answer = ocean(
         got.reshape(DEV * BLOCK, CELLS),
         inner,
@@ -463,13 +530,16 @@
         east_in,
         south_in,
         north_in,
+        in_hbm(turned),
     )
     returned = lax.all_to_all(answer, axes, split_axis=0, concat_axis=0, tiled=True)
     atmos_state = state(
         slots,
         returned.reshape(DEV * 2 * CAP, CELLS),
         pltpu.with_memory_space_constraint(near, VMEM),
+        pltpu.with_memory_space_constraint(mid, VMEM),
         in_hbm(remap_blocks),
+        in_hbm(turned),
     )
     return after.reshape(2, LEV, CY, CELLS), atmos_state
 

time: 61.7 us -> 61.2 us (level)
  waiting for transfers between devices: 13.8 us -> 10.5 us
  Pallas kernels: 12 us -> 14.7 us
    pallas_call x0 -> x1, Pallas kernels: none -> 3.29 us  [turn(): pl.pallas_call(turn_kernel, out_shape=(pltpu.HBM((TURNED, 128, 128), BF16...]
    ppermute x1, waiting for transfers between devices: 3.53 us -> 0.86 us  [on_device(): south_in = lax.ppermute(to_north, 'lat', northward)]
    pallas_call x1, Pallas kernels: 4.84 us -> 4.2 us  [state(): pl.pallas_call(state_kernel, out_shape=pltpu.HBM((ROWS, 2, 128), F32), in...]
    ppermute x1, waiting for transfers between devices: 0.64 us -> 0.01 us  [on_device(): east_in = lax.ppermute(to_west, 'lon', westward)]
  transfers between devices with their start and end apart: 5 -> 5, of which waited for: 4 -> 3; matrix products, arithmetic and copies ran while one was open for 0% -> 0% of each run, Pallas kernels for 1% -> 6%
where the time goes in v6:
time: 61.2 us; the launch traced here: 60.9 us
  starting transfers between devices  17.7 us (29%)
  blocking collectives  17.2 us (28%)
  Pallas kernels  14.7 us (24%)
  waiting for transfers between devices  10.5 us (17%)
  between operations  0.77 us (1%)
    all_to_all x1, blocking collectives, on_device(): lax.all_to_all(answer, axes, split_axis=0, concat_axis=0, tiled=True)  17.2 us
    all_to_all x1, starting transfers between devices, on_device(): lax.all_to_all(send.reshape(DEV, BLOCK, 1, CELLS), axes, split_axis=0, co...  11.5 us
    all_to_all x1, waiting for transfers between devices, on_device(): lax.all_to_all(send.reshape(DEV, BLOCK, 1, CELLS), axes, split_axis=0, co...  6.85 us
    pallas_call x1, Pallas kernels, contributions(): pl.pallas_call(contrib_kernel, out_shape=(jax.ShapeDtypeStruct((DEV * BLO...  5.52 us
    pallas_call x1, Pallas kernels, state(): pl.pallas_call(state_kernel, out_shape=pltpu.HBM((ROWS, 2, 128), F32), in...  4.2 us
    pallas_call x1, Pallas kernels, turn(): pl.pallas_call(turn_kernel, out_shape=(pltpu.HBM((TURNED, 128, 128), BF16...  3.29 us
    ppermute x1, starting transfers between devices, on_device(): south_in = lax.ppermute(to_north, 'lat', northward)  3.09 us
    ppermute x1, waiting for transfers between devices, on_device(): north_in = lax.ppermute(to_south, 'lat', southward)  2.78 us
  transfers between devices with their start and end apart: 5, of which 3 were waited for; matrix products, arithmetic and copies ran while one was open for 0% of the time, Pallas kernels for 6%

profile of v6, /device:TPU:1, one launch (start us, length us, event | category | flops | bytes accessed | tf_op | source)
XLA Modules:
  0.0 60.9 jit_solution(7008814842468365679)
XLA Ops:
  0.6 0.0 copy-start
  0.6 0.0 copy-start.1
  0.7 0.0 copy-start.2
  0.7 0.0 copy-start.3
  0.7 5.5 %contrib.1 = (f32[2176,128]{1,0:T(8,128)}, s32[2,128]{1,0:T(2,128)S(1)}, bf16[32,128,128]{2,1,0:T(8,128)(2,1)S(1)}) custom-call(s32[2,128]{1,0:T(2,128)} %bitcast.13, s32[2,128]{1,0:T(2,128)} %bitcast.14, f32[6,256,128]{2,1,0:T(8,128)} %bitcast.12, bf16[256,128,128]{2,1,0:T(8,128)(2,1)} %remap_hbm.5), custom_call_target="tpu_custom_call" | custom-call | flops 1000000000 | bytes 10000000 | tf_op jit(solution)/shard_map/contrib/pallas_call | solution.py:146
  6.2 11.5 %all-to-all-start = ((f32[128,17,1,128]{3,2,1,0:T(1,128)}), f32[128,17,1,128]{3,2,1,0:T(1,128)S(1)}, u32[]{:S(2)}, u32[]{:S(2)}) async-start(f32[128,17,1,128]{3,2,1,0:T(1,128)} %bitcast.3), calls=%async_computation | async-start | bytes 2228224 | tf_op jit(solution)/shard_map/all_to_all | solution.py:515
  17.7 0.0 copy-done
  17.7 0.0 copy-done.1
  17.7 0.0 copy-done.2
  17.7 0.0 copy-done.3
  17.8 0.2 edges.1
  18.0 1.8 %collective-permute-start = (f32[32,128]{1,0:T(8,128)S(1)}, f32[32,128]{1,0:T(8,128)S(1)}, u32[]{:S(2)}, u32[]{:S(2)}) collective-permute-start(f32[32,128]{1,0:T(8,128)S(1)} %get-tuple-element.14.to_east), channel_id=1, source_target_pairs={{0,4},{4,8},{8,12},{12,16},{16,20},{20,24},{24,28},{28,32},{32,36}... | collective-permute-start | bytes 49160 | tf_op jit(solution)/shard_map/ppermute | solution.py:505
  19.8 0.0 collective-permute-start.1
  19.8 3.1 %collective-permute-start.2 = (f32[32,128]{1,0:T(8,128)S(1)}, f32[32,128]{1,0:T(8,128)S(1)}, u32[]{:S(2)}, u32[]{:S(2)}) collective-permute-start(f32[32,128]{1,0:T(8,128)S(1)} %get-tuple-element.16.to_north), channel_id=1, source_target_pairs={{0,1},{1,2},{2,3},{4,5},{5,6},{6,7},{8,9},{9,10},{10,11},{12,13},{... | collective-permute-start | bytes 49160 | tf_op jit(solution)/shard_map/ppermute | solution.py:507
  22.9 1.3 %collective-permute-start.3 = (f32[32,128]{1,0:T(8,128)S(1)}, f32[32,128]{1,0:T(8,128)S(1)}, u32[]{:S(2)}, u32[]{:S(2)}) collective-permute-start(f32[32,128]{1,0:T(8,128)S(1)} %get-tuple-element.17.to_south), channel_id=1, source_target_pairs={{1,0},{2,1},{3,2},{5,4},{6,5},{7,6},{9,8},{10,9},{11,10},{13,12},{... | collective-permute-start | bytes 49160 | tf_op jit(solution)/shard_map/ppermute | solution.py:508
  24.2 0.3 advect.1.inner
  24.5 0.0 copy-start.4
  24.5 3.3 %turn.1 = (bf16[96,128,128]{2,1,0:T(8,128)(2,1)}, bf16[24,128,128]{2,1,0:T(8,128)(2,1)S(1)}) custom-call(f32[16,32,128]{2,1,0:T(8,128)S(1)} %advect.1.inner, bf16[256,128,128]{2,1,0:T(8,128)(2,1)} %remap_hbm.5), custom_call_target="tpu_custom_call" | custom-call | flops 1000000 | bytes 6000000 | tf_op jit(solution)/shard_map/turn/pallas_call | solution.py:397
  27.8 0.0 collective-permute-done.west_in
  27.8 0.0 collective-permute-done.1.east_in
  27.9 0.9 %collective-permute-done.2.south_in = f32[32,128]{1,0:T(8,128)S(1)} collective-permute-done((f32[32,128]{1,0:T(8,128)S(1)}, f32[32,128]{1,0:T(8,128)S(1)}, u32[]{:S(2)}, u32[]{:S(2)}) %collective-permute-start.2) | collective-permute-done | bytes 16416 | tf_op jit(solution)/shard_map/ppermute | solution.py:507
  28.7 2.8 %collective-permute-done.3.north_in = f32[32,128]{1,0:T(8,128)S(1)} collective-permute-done((f32[32,128]{1,0:T(8,128)S(1)}, f32[32,128]{1,0:T(8,128)S(1)}, u32[]{:S(2)}, u32[]{:S(2)}) %collective-permute-start.3) | collective-permute-done | bytes 16416 | tf_op jit(solution)/shard_map/ppermute | solution.py:508
  31.5 6.9 %all-to-all-done = f32[128,17,1,128]{3,2,1,0:T(1,128)S(1)} async-done(((f32[128,17,1,128]{3,2,1,0:T(1,128)}), f32[128,17,1,128]{3,2,1,0:T(1,128)S(1)}, u32[]{:S(2)}, u32[]{:S(2)}) %all-to-all-start) | async-done | bytes 1114144 | tf_op jit(solution)/shard_map/all_to_all | solution.py:515
  38.3 0.0 copy-done.4
  38.3 1.2 %ocean.1 = (f32[16,32,128]{2,1,0:T(8,128)}, f32[128,8,128]{2,1,0:T(8,128)S(1)}) custom-call(f32[2176,128]{1,0:T(8,128)S(1)} %bitcast.8, f32[16,32,128]{2,1,0:T(8,128)S(1)} %advect.1.inner, f32[8,32,128]{2,1,0:T(8,128)S(1)} %copy-done.4, s32[32,128]{1,0:T(8,128)S(1)} %copy-done.3, f32[32,128]{1,0:T(8,128)S(1)} %get-tuple-element.14.to_east, ...), custom_call_target="tpu_custom_call" | custom-call | flops 100000000 | bytes 4000000 | tf_op jit(solution)/shard_map/ocean/pallas_call | solution.py:352
  39.5 17.2 %all_to_all.10 = f32[128,8,128]{2,1,0:T(8,128)S(1)} all-to-all(f32[128,8,128]{2,1,0:T(8,128)S(1)} %get-tuple-element.21), channel_id=1, replica_groups=mesh['lon'=32,'lat'=4] {'lon','lat'}, dimensions={0} | all-to-all | bytes 1048576 | tf_op jit(solution)/shard_map/all_to_all | solution.py:535
  56.7 4.2 %state.1 = f32[256,2,128]{2,1,0:T(2,128)} custom-call(s32[2,128]{1,0:T(2,128)S(1)} %get-tuple-element.20.slots_in, f32[1024,128]{1,0:T(8,128)S(1)} %bitcast.9, bf16[32,128,128]{2,1,0:T(8,128)(2,1)S(1)} %get-tuple-element.22.near, bf16[24,128,128]{2,1,0:T(8,128)(2,1)S(1)} %get-tuple-element.23.mid, bf16[256,128,128]{2,1,0:T(8,128)(2,1)} %remap_hbm.5, ...), custom_call_target="tpu_custom_call" | custom-call | flops 1000000000 | bytes 9000000 | tf_op jit(solution)/shard_map/state/pallas_call | solution.py:471
Async XLA Ops:
  0.6 17.1 %copy-start = (f32[2,8,32,128]{3,2,1,0:T(8,128)S(1)}, f32[2,8,32,128]{3,2,1,0:T(8,128)}, u32[]{:S(2)}) copy-start(f32[2,8,32,128]{3,2,1,0:T(8,128)} %param.13) | copy-start | bytes 786436
  0.6 17.1 %copy-start.1 = (f32[8,32,128]{2,1,0:T(8,128)S(1)}, f32[8,32,128]{2,1,0:T(8,128)}, u32[]{:S(2)}) copy-start(f32[8,32,128]{2,1,0:T(8,128)} %east_vel.3) | copy-start | bytes 393220
  0.7 17.1 %copy-start.2 = (f32[8,32,128]{2,1,0:T(8,128)S(1)}, f32[8,32,128]{2,1,0:T(8,128)}, u32[]{:S(2)}) copy-start(f32[8,32,128]{2,1,0:T(8,128)} %north_vel.3) | copy-start | bytes 393220
  0.7 17.1 %copy-start.3 = (s32[32,128]{1,0:T(8,128)S(1)}, s32[32,128]{1,0:T(8,128)}, u32[]{:S(2)}) copy-start(s32[32,128]{1,0:T(8,128)} %levels.5) | copy-start | bytes 49156
  6.2 32.1 %all-to-all-start = ((f32[128,17,1,128]{3,2,1,0:T(1,128)}), f32[128,17,1,128]{3,2,1,0:T(1,128)S(1)}, u32[]{:S(2)}, u32[]{:S(2)}) async-start(f32[128,17,1,128]{3,2,1,0:T(1,128)} %bitcast.3), calls=%async_computation | async-start | bytes 2228224 | tf_op jit(solution)/shard_map/all_to_all | solution.py:515
  18.0 9.8 %collective-permute-start = (f32[32,128]{1,0:T(8,128)S(1)}, f32[32,128]{1,0:T(8,128)S(1)}, u32[]{:S(2)}, u32[]{:S(2)}) collective-permute-start(f32[32,128]{1,0:T(8,128)S(1)} %get-tuple-element.14.to_east), channel_id=1, source_target_pairs={{0,4},{4,8},{8,12},{12,16},{16,20},{20,24},{24,28},{28,32},{32,36}... | collective-permute-start | bytes 49160 | tf_op jit(solution)/shard_map/ppermute | solution.py:505
  19.8 8.0 %collective-permute-start.1 = (f32[32,128]{1,0:T(8,128)S(1)}, f32[32,128]{1,0:T(8,128)S(1)}, u32[]{:S(2)}, u32[]{:S(2)}) collective-permute-start(f32[32,128]{1,0:T(8,128)S(1)} %get-tuple-element.15.to_west), channel_id=1, source_target_pairs={{4,0},{8,4},{12,8},{16,12},{20,16},{24,20},{28,24},{32,28},{36,32}... | collective-permute-start | bytes 49160 | tf_op jit(solution)/shard_map/ppermute | solution.py:506
  19.8 8.9 %collective-permute-start.2 = (f32[32,128]{1,0:T(8,128)S(1)}, f32[32,128]{1,0:T(8,128)S(1)}, u32[]{:S(2)}, u32[]{:S(2)}) collective-permute-start(f32[32,128]{1,0:T(8,128)S(1)} %get-tuple-element.16.to_north), channel_id=1, source_target_pairs={{0,1},{1,2},{2,3},{4,5},{5,6},{6,7},{8,9},{9,10},{10,11},{12,13},{... | collective-permute-start | bytes 49160 | tf_op jit(solution)/shard_map/ppermute | solution.py:507
  22.9 8.6 %collective-permute-start.3 = (f32[32,128]{1,0:T(8,128)S(1)}, f32[32,128]{1,0:T(8,128)S(1)}, u32[]{:S(2)}, u32[]{:S(2)}) collective-permute-start(f32[32,128]{1,0:T(8,128)S(1)} %get-tuple-element.17.to_south), channel_id=1, source_target_pairs={{1,0},{2,1},{3,2},{5,4},{6,5},{7,6},{9,8},{10,9},{11,10},{13,12},{... | collective-permute-start | bytes 49160 | tf_op jit(solution)/shard_map/ppermute | solution.py:508
  24.5 13.8 %copy-start.4 = (f32[8,32,128]{2,1,0:T(8,128)S(1)}, f32[8,32,128]{2,1,0:T(8,128)}, u32[]{:S(2)}) copy-start(f32[8,32,128]{2,1,0:T(8,128)} %kappa.1) | copy-start | bytes 393220

commit v7 on v6

--- a/solution.py
+++ b/solution.py
@@ -18,7 +18,7 @@
 BLOCK = CAP * SENT + 1
 LEV = 8
 CY = 32
-CONTRIB_SIZES = (32, 48, 80, 96)
+CONTRIB_SIZES = (32, 128, 96)
 NEAR = 32
 MID = 24
 FAR_SIZES = (40, 64)
@@ -274,8 +274,10 @@
     south_in,
     north_in,
     turned_hbm,
+    after_hbm,
+    answer,
     after,
-    answer,
+    sem,
 ):
     lane, row = iota((CY, 128), 1), iota((CY, 128), 0)
     from_west, to_next = side_face(west_in, to_west), side_face(to_east, east_in)
@@ -333,6 +335,8 @@
         warmth = offsets[k][0] + gains[k] * warmth
         salt = offsets[k][1] + gains[k] * salt
         after[k], after[LEV + k] = warmth, salt
+    after_copy = pltpu.make_async_copy(after, after_hbm, sem)
+    after_copy.start()
     high, low = split(jnp.concatenate([warmth, salt], axis=1))
     picked = lax.dot_general(
         select,
@@ -346,17 +350,19 @@
             answer[:, 2 * s + f, :] = (
                 rows[:, f * CELLS : (f + 1) * CELLS] + rows[:, (2 + f) * CELLS : (3 + f) * CELLS]
             )
+    after_copy.wait()
 
 
 def ocean(*args):
     return pl.pallas_call(
         ocean_kernel,
         out_shape=(
-            jax.ShapeDtypeStruct((16, CY, 128), F32),
+            pltpu.HBM((16, CY, 128), F32),
             jax.ShapeDtypeStruct((DEV, 2 * CAP, CELLS), F32),
         ),
         in_specs=vmem_specs(12) + [pl.BlockSpec(memory_space=pltpu.HBM)],
-        out_specs=tuple(vmem_specs(2)),
+        out_specs=(pl.BlockSpec(memory_space=pltpu.HBM), pl.BlockSpec(memory_space=VMEM)),
+        scratch_shapes=[VMEM((16, CY, 128), F32), pltpu.SemaphoreType.DMA],
         compiler_params=params(24),
         cost_estimate=pl.CostEstimate(flops=10**8, bytes_accessed=4_000_000, transcendentals=0),
         name="ocean",

time: 61.2 us -> 61.1 us (level)
  no operation moved by 1% of the time
where the time goes in v7:
time: 61.1 us; the launch traced here: 60.8 us
  starting transfers between devices  17.7 us (29%)
  blocking collectives  17.2 us (28%)
  Pallas kernels  14.6 us (24%)
  waiting for transfers between devices  10.5 us (17%)
  between operations  0.78 us (1%)
    all_to_all x1, blocking collectives, on_device(): lax.all_to_all(answer, axes, split_axis=0, concat_axis=0, tiled=True)  17.2 us
    all_to_all x1, starting transfers between devices, on_device(): lax.all_to_all(send.reshape(DEV, BLOCK, 1, CELLS), axes, split_axis=0, co...  11.5 us
    all_to_all x1, waiting for transfers between devices, on_device(): lax.all_to_all(send.reshape(DEV, BLOCK, 1, CELLS), axes, split_axis=0, co...  6.85 us
    pallas_call x1, Pallas kernels, contributions(): pl.pallas_call(contrib_kernel, out_shape=(jax.ShapeDtypeStruct((DEV * BLO...  5.39 us
    pallas_call x1, Pallas kernels, state(): pl.pallas_call(state_kernel, out_shape=pltpu.HBM((ROWS, 2, 128), F32), in...  4.2 us
    pallas_call x1, Pallas kernels, turn(): pl.pallas_call(turn_kernel, out_shape=(pltpu.HBM((TURNED, 128, 128), BF16...  3.29 us
    ppermute x1, starting transfers between devices, on_device(): south_in = lax.ppermute(to_north, 'lat', northward)  3.09 us
    ppermute x1, waiting for transfers between devices, on_device(): north_in = lax.ppermute(to_south, 'lat', southward)  2.78 us
  transfers between devices with their start and end apart: 5, of which 3 were waited for; matrix products, arithmetic and copies ran while one was open for 0% of the time, Pallas kernels for 6%

profile of v7, /device:TPU:1, one launch (start us, length us, event | category | flops | bytes accessed | tf_op | source)
XLA Modules:
  0.0 60.8 jit_solution(8464945071715388077)
XLA Ops:
  0.6 0.0 copy-start
  0.6 0.0 copy-start.1
  0.7 0.0 copy-start.2
  0.7 0.0 copy-start.3
  0.7 5.4 %contrib.1 = (f32[2176,128]{1,0:T(8,128)}, s32[2,128]{1,0:T(2,128)S(1)}, bf16[32,128,128]{2,1,0:T(8,128)(2,1)S(1)}) custom-call(s32[2,128]{1,0:T(2,128)} %bitcast.13, s32[2,128]{1,0:T(2,128)} %bitcast.14, f32[6,256,128]{2,1,0:T(8,128)} %bitcast.12, bf16[256,128,128]{2,1,0:T(8,128)(2,1)} %remap_hbm.5), custom_call_target="tpu_custom_call" | custom-call | flops 1000000000 | bytes 10000000 | tf_op jit(solution)/shard_map/contrib/pallas_call | solution.py:146
  6.1 11.5 %all-to-all-start = ((f32[128,17,1,128]{3,2,1,0:T(1,128)}), f32[128,17,1,128]{3,2,1,0:T(1,128)S(1)}, u32[]{:S(2)}, u32[]{:S(2)}) async-start(f32[128,17,1,128]{3,2,1,0:T(1,128)} %bitcast.3), calls=%async_computation | async-start | bytes 2228224 | tf_op jit(solution)/shard_map/all_to_all | solution.py:521
  17.6 0.0 copy-done
  17.6 0.0 copy-done.1
  17.6 0.0 copy-done.2
  17.6 0.0 copy-done.3
  17.6 0.2 edges.1
  17.9 1.8 %collective-permute-start = (f32[32,128]{1,0:T(8,128)S(1)}, f32[32,128]{1,0:T(8,128)S(1)}, u32[]{:S(2)}, u32[]{:S(2)}) collective-permute-start(f32[32,128]{1,0:T(8,128)S(1)} %get-tuple-element.14.to_east), channel_id=1, source_target_pairs={{0,4},{4,8},{8,12},{12,16},{16,20},{20,24},{24,28},{28,32},{32,36}... | collective-permute-start | bytes 49160 | tf_op jit(solution)/shard_map/ppermute | solution.py:511
  19.7 0.0 collective-permute-start.1
  19.7 3.1 %collective-permute-start.2 = (f32[32,128]{1,0:T(8,128)S(1)}, f32[32,128]{1,0:T(8,128)S(1)}, u32[]{:S(2)}, u32[]{:S(2)}) collective-permute-start(f32[32,128]{1,0:T(8,128)S(1)} %get-tuple-element.16.to_north), channel_id=1, source_target_pairs={{0,1},{1,2},{2,3},{4,5},{5,6},{6,7},{8,9},{9,10},{10,11},{12,13},{... | collective-permute-start | bytes 49160 | tf_op jit(solution)/shard_map/ppermute | solution.py:513
  22.8 1.3 %collective-permute-start.3 = (f32[32,128]{1,0:T(8,128)S(1)}, f32[32,128]{1,0:T(8,128)S(1)}, u32[]{:S(2)}, u32[]{:S(2)}) collective-permute-start(f32[32,128]{1,0:T(8,128)S(1)} %get-tuple-element.17.to_south), channel_id=1, source_target_pairs={{1,0},{2,1},{3,2},{5,4},{6,5},{7,6},{9,8},{10,9},{11,10},{13,12},{... | collective-permute-start | bytes 49160 | tf_op jit(solution)/shard_map/ppermute | solution.py:514
  24.1 0.3 advect.1.inner
  24.4 0.0 copy-start.4
  24.4 3.3 %turn.1 = (bf16[96,128,128]{2,1,0:T(8,128)(2,1)}, bf16[24,128,128]{2,1,0:T(8,128)(2,1)S(1)}) custom-call(f32[16,32,128]{2,1,0:T(8,128)S(1)} %advect.1.inner, bf16[256,128,128]{2,1,0:T(8,128)(2,1)} %remap_hbm.5), custom_call_target="tpu_custom_call" | custom-call | flops 1000000 | bytes 6000000 | tf_op jit(solution)/shard_map/turn/pallas_call | solution.py:403
  27.7 0.0 collective-permute-done.west_in
  27.7 0.0 collective-permute-done.1.east_in
  27.7 0.9 %collective-permute-done.2.south_in = f32[32,128]{1,0:T(8,128)S(1)} collective-permute-done((f32[32,128]{1,0:T(8,128)S(1)}, f32[32,128]{1,0:T(8,128)S(1)}, u32[]{:S(2)}, u32[]{:S(2)}) %collective-permute-start.2) | collective-permute-done | bytes 16416 | tf_op jit(solution)/shard_map/ppermute | solution.py:513
  28.6 2.8 %collective-permute-done.3.north_in = f32[32,128]{1,0:T(8,128)S(1)} collective-permute-done((f32[32,128]{1,0:T(8,128)S(1)}, f32[32,128]{1,0:T(8,128)S(1)}, u32[]{:S(2)}, u32[]{:S(2)}) %collective-permute-start.3) | collective-permute-done | bytes 16416 | tf_op jit(solution)/shard_map/ppermute | solution.py:514
  31.4 6.9 %all-to-all-done = f32[128,17,1,128]{3,2,1,0:T(1,128)S(1)} async-done(((f32[128,17,1,128]{3,2,1,0:T(1,128)}), f32[128,17,1,128]{3,2,1,0:T(1,128)S(1)}, u32[]{:S(2)}, u32[]{:S(2)}) %all-to-all-start) | async-done | bytes 1114144 | tf_op jit(solution)/shard_map/all_to_all | solution.py:521
  38.2 0.0 copy-done.4
  38.2 1.2 %ocean.1 = (f32[16,32,128]{2,1,0:T(8,128)}, f32[128,8,128]{2,1,0:T(8,128)S(1)}) custom-call(f32[2176,128]{1,0:T(8,128)S(1)} %bitcast.8, f32[16,32,128]{2,1,0:T(8,128)S(1)} %advect.1.inner, f32[8,32,128]{2,1,0:T(8,128)S(1)} %copy-done.4, s32[32,128]{1,0:T(8,128)S(1)} %copy-done.3, f32[32,128]{1,0:T(8,128)S(1)} %get-tuple-element.14.to_east, ...), custom_call_target="tpu_custom_call" | custom-call | flops 100000000 | bytes 4000000 | tf_op jit(solution)/shard_map/ocean/pallas_call | solution.py:357
  39.4 17.2 %all_to_all.10 = f32[128,8,128]{2,1,0:T(8,128)S(1)} all-to-all(f32[128,8,128]{2,1,0:T(8,128)S(1)} %get-tuple-element.21), channel_id=1, replica_groups=mesh['lon'=32,'lat'=4] {'lon','lat'}, dimensions={0} | all-to-all | bytes 1048576 | tf_op jit(solution)/shard_map/all_to_all | solution.py:541
  56.6 4.2 %state.1 = f32[256,2,128]{2,1,0:T(2,128)} custom-call(s32[2,128]{1,0:T(2,128)S(1)} %get-tuple-element.20.slots_in, f32[1024,128]{1,0:T(8,128)S(1)} %bitcast.9, bf16[32,128,128]{2,1,0:T(8,128)(2,1)S(1)} %get-tuple-element.22.near, bf16[24,128,128]{2,1,0:T(8,128)(2,1)S(1)} %get-tuple-element.23.mid, bf16[256,128,128]{2,1,0:T(8,128)(2,1)} %remap_hbm.5, ...), custom_call_target="tpu_custom_call" | custom-call | flops 1000000000 | bytes 9000000 | tf_op jit(solution)/shard_map/state/pallas_call | solution.py:477
Async XLA Ops:
  0.6 16.9 %copy-start = (f32[2,8,32,128]{3,2,1,0:T(8,128)S(1)}, f32[2,8,32,128]{3,2,1,0:T(8,128)}, u32[]{:S(2)}) copy-start(f32[2,8,32,128]{3,2,1,0:T(8,128)} %param.13) | copy-start | bytes 786436
  0.6 16.9 %copy-start.1 = (f32[8,32,128]{2,1,0:T(8,128)S(1)}, f32[8,32,128]{2,1,0:T(8,128)}, u32[]{:S(2)}) copy-start(f32[8,32,128]{2,1,0:T(8,128)} %east_vel.3) | copy-start | bytes 393220
  0.7 16.9 %copy-start.2 = (f32[8,32,128]{2,1,0:T(8,128)S(1)}, f32[8,32,128]{2,1,0:T(8,128)}, u32[]{:S(2)}) copy-start(f32[8,32,128]{2,1,0:T(8,128)} %north_vel.3) | copy-start | bytes 393220
  0.7 16.9 %copy-start.3 = (s32[32,128]{1,0:T(8,128)S(1)}, s32[32,128]{1,0:T(8,128)}, u32[]{:S(2)}) copy-start(s32[32,128]{1,0:T(8,128)} %levels.5) | copy-start | bytes 49156
  6.1 32.1 %all-to-all-start = ((f32[128,17,1,128]{3,2,1,0:T(1,128)}), f32[128,17,1,128]{3,2,1,0:T(1,128)S(1)}, u32[]{:S(2)}, u32[]{:S(2)}) async-start(f32[128,17,1,128]{3,2,1,0:T(1,128)} %bitcast.3), calls=%async_computation | async-start | bytes 2228224 | tf_op jit(solution)/shard_map/all_to_all | solution.py:521
  17.9 9.8 %collective-permute-start = (f32[32,128]{1,0:T(8,128)S(1)}, f32[32,128]{1,0:T(8,128)S(1)}, u32[]{:S(2)}, u32[]{:S(2)}) collective-permute-start(f32[32,128]{1,0:T(8,128)S(1)} %get-tuple-element.14.to_east), channel_id=1, source_target_pairs={{0,4},{4,8},{8,12},{12,16},{16,20},{20,24},{24,28},{28,32},{32,36}... | collective-permute-start | bytes 49160 | tf_op jit(solution)/shard_map/ppermute | solution.py:511
  19.7 8.0 %collective-permute-start.1 = (f32[32,128]{1,0:T(8,128)S(1)}, f32[32,128]{1,0:T(8,128)S(1)}, u32[]{:S(2)}, u32[]{:S(2)}) collective-permute-start(f32[32,128]{1,0:T(8,128)S(1)} %get-tuple-element.15.to_west), channel_id=1, source_target_pairs={{4,0},{8,4},{12,8},{16,12},{20,16},{24,20},{28,24},{32,28},{36,32}... | collective-permute-start | bytes 49160 | tf_op jit(solution)/shard_map/ppermute | solution.py:512
  19.7 8.9 %collective-permute-start.2 = (f32[32,128]{1,0:T(8,128)S(1)}, f32[32,128]{1,0:T(8,128)S(1)}, u32[]{:S(2)}, u32[]{:S(2)}) collective-permute-start(f32[32,128]{1,0:T(8,128)S(1)} %get-tuple-element.16.to_north), channel_id=1, source_target_pairs={{0,1},{1,2},{2,3},{4,5},{5,6},{6,7},{8,9},{9,10},{10,11},{12,13},{... | collective-permute-start | bytes 49160 | tf_op jit(solution)/shard_map/ppermute | solution.py:513
  22.8 8.6 %collective-permute-start.3 = (f32[32,128]{1,0:T(8,128)S(1)}, f32[32,128]{1,0:T(8,128)S(1)}, u32[]{:S(2)}, u32[]{:S(2)}) collective-permute-start(f32[32,128]{1,0:T(8,128)S(1)} %get-tuple-element.17.to_south), channel_id=1, source_target_pairs={{1,0},{2,1},{3,2},{5,4},{6,5},{7,6},{9,8},{10,9},{11,10},{13,12},{... | collective-permute-start | bytes 49160 | tf_op jit(solution)/shard_map/ppermute | solution.py:514
  24.4 13.8 %copy-start.4 = (f32[8,32,128]{2,1,0:T(8,128)S(1)}, f32[8,32,128]{2,1,0:T(8,128)}, u32[]{:S(2)}) copy-start(f32[8,32,128]{2,1,0:T(8,128)} %kappa.1) | copy-start | bytes 393220

commit v8 on v7

--- a/solution.py
+++ b/solution.py
@@ -21,7 +21,7 @@
 CONTRIB_SIZES = (32, 128, 96)
 NEAR = 32
 MID = 24
-FAR_SIZES = (40, 64)
+FAR_SIZES = (104,)
 TURNED = 96
 PIECE = 32
 

time: 61.1 us -> 61 us (level)
  no operation moved by 1% of the time
where the time goes in v8:
time: 61 us; the launch traced here: 60.8 us
  starting transfers between devices  17.7 us (29%)
  blocking collectives  17.2 us (28%)
  Pallas kernels  14.6 us (24%)
  waiting for transfers between devices  10.5 us (17%)
  between operations  0.78 us (1%)
    all_to_all x1, blocking collectives, on_device(): lax.all_to_all(answer, axes, split_axis=0, concat_axis=0, tiled=True)  17.2 us
    all_to_all x1, starting transfers between devices, on_device(): lax.all_to_all(send.reshape(DEV, BLOCK, 1, CELLS), axes, split_axis=0, co...  11.5 us
    all_to_all x1, waiting for transfers between devices, on_device(): lax.all_to_all(send.reshape(DEV, BLOCK, 1, CELLS), axes, split_axis=0, co...  6.85 us
    pallas_call x1, Pallas kernels, contributions(): pl.pallas_call(contrib_kernel, out_shape=(jax.ShapeDtypeStruct((DEV * BLO...  5.39 us
    pallas_call x1, Pallas kernels, state(): pl.pallas_call(state_kernel, out_shape=pltpu.HBM((ROWS, 2, 128), F32), in...  4.19 us
    pallas_call x1, Pallas kernels, turn(): pl.pallas_call(turn_kernel, out_shape=(pltpu.HBM((TURNED, 128, 128), BF16...  3.29 us
    ppermute x1, starting transfers between devices, on_device(): south_in = lax.ppermute(to_north, 'lat', northward)  3.09 us
    ppermute x1, waiting for transfers between devices, on_device(): north_in = lax.ppermute(to_south, 'lat', southward)  2.78 us
  transfers between devices with their start and end apart: 5, of which 3 were waited for; matrix products, arithmetic and copies ran while one was open for 0% of the time, Pallas kernels for 6%

profile of v8, /device:TPU:1, one launch (start us, length us, event | category | flops | bytes accessed | tf_op | source)
XLA Modules:
  0.0 60.8 jit_solution(13213953197696366006)
XLA Ops:
  0.6 0.0 copy-start
  0.6 0.0 copy-start.1
  0.7 0.0 copy-start.2
  0.7 0.0 copy-start.3
  0.7 5.4 %contrib.1 = (f32[2176,128]{1,0:T(8,128)}, s32[2,128]{1,0:T(2,128)S(1)}, bf16[32,128,128]{2,1,0:T(8,128)(2,1)S(1)}) custom-call(s32[2,128]{1,0:T(2,128)} %bitcast.13, s32[2,128]{1,0:T(2,128)} %bitcast.14, f32[6,256,128]{2,1,0:T(8,128)} %bitcast.12, bf16[256,128,128]{2,1,0:T(8,128)(2,1)} %remap_hbm.5), custom_call_target="tpu_custom_call" | custom-call | flops 1000000000 | bytes 10000000 | tf_op jit(solution)/shard_map/contrib/pallas_call | solution.py:146
  6.1 11.5 %all-to-all-start = ((f32[128,17,1,128]{3,2,1,0:T(1,128)}), f32[128,17,1,128]{3,2,1,0:T(1,128)S(1)}, u32[]{:S(2)}, u32[]{:S(2)}) async-start(f32[128,17,1,128]{3,2,1,0:T(1,128)} %bitcast.3), calls=%async_computation | async-start | bytes 2228224 | tf_op jit(solution)/shard_map/all_to_all | solution.py:521
  17.6 0.0 copy-done
  17.6 0.0 copy-done.1
  17.6 0.0 copy-done.2
  17.6 0.0 copy-done.3
  17.6 0.2 edges.1
  17.9 1.8 %collective-permute-start = (f32[32,128]{1,0:T(8,128)S(1)}, f32[32,128]{1,0:T(8,128)S(1)}, u32[]{:S(2)}, u32[]{:S(2)}) collective-permute-start(f32[32,128]{1,0:T(8,128)S(1)} %get-tuple-element.14.to_east), channel_id=1, source_target_pairs={{0,4},{4,8},{8,12},{12,16},{16,20},{20,24},{24,28},{28,32},{32,36}... | collective-permute-start | bytes 49160 | tf_op jit(solution)/shard_map/ppermute | solution.py:511
  19.7 0.0 collective-permute-start.1
  19.7 3.1 %collective-permute-start.2 = (f32[32,128]{1,0:T(8,128)S(1)}, f32[32,128]{1,0:T(8,128)S(1)}, u32[]{:S(2)}, u32[]{:S(2)}) collective-permute-start(f32[32,128]{1,0:T(8,128)S(1)} %get-tuple-element.16.to_north), channel_id=1, source_target_pairs={{0,1},{1,2},{2,3},{4,5},{5,6},{6,7},{8,9},{9,10},{10,11},{12,13},{... | collective-permute-start | bytes 49160 | tf_op jit(solution)/shard_map/ppermute | solution.py:513
  22.8 1.3 %collective-permute-start.3 = (f32[32,128]{1,0:T(8,128)S(1)}, f32[32,128]{1,0:T(8,128)S(1)}, u32[]{:S(2)}, u32[]{:S(2)}) collective-permute-start(f32[32,128]{1,0:T(8,128)S(1)} %get-tuple-element.17.to_south), channel_id=1, source_target_pairs={{1,0},{2,1},{3,2},{5,4},{6,5},{7,6},{9,8},{10,9},{11,10},{13,12},{... | collective-permute-start | bytes 49160 | tf_op jit(solution)/shard_map/ppermute | solution.py:514
  24.1 0.3 advect.1.inner
  24.4 0.0 copy-start.4
  24.4 3.3 %turn.1 = (bf16[96,128,128]{2,1,0:T(8,128)(2,1)}, bf16[24,128,128]{2,1,0:T(8,128)(2,1)S(1)}) custom-call(f32[16,32,128]{2,1,0:T(8,128)S(1)} %advect.1.inner, bf16[256,128,128]{2,1,0:T(8,128)(2,1)} %remap_hbm.5), custom_call_target="tpu_custom_call" | custom-call | flops 1000000 | bytes 6000000 | tf_op jit(solution)/shard_map/turn/pallas_call | solution.py:403
  27.7 0.0 collective-permute-done.west_in
  27.7 0.0 collective-permute-done.1.east_in
  27.7 0.9 %collective-permute-done.2.south_in = f32[32,128]{1,0:T(8,128)S(1)} collective-permute-done((f32[32,128]{1,0:T(8,128)S(1)}, f32[32,128]{1,0:T(8,128)S(1)}, u32[]{:S(2)}, u32[]{:S(2)}) %collective-permute-start.2) | collective-permute-done | bytes 16416 | tf_op jit(solution)/shard_map/ppermute | solution.py:513
  28.6 2.8 %collective-permute-done.3.north_in = f32[32,128]{1,0:T(8,128)S(1)} collective-permute-done((f32[32,128]{1,0:T(8,128)S(1)}, f32[32,128]{1,0:T(8,128)S(1)}, u32[]{:S(2)}, u32[]{:S(2)}) %collective-permute-start.3) | collective-permute-done | bytes 16416 | tf_op jit(solution)/shard_map/ppermute | solution.py:514
  31.4 6.9 %all-to-all-done = f32[128,17,1,128]{3,2,1,0:T(1,128)S(1)} async-done(((f32[128,17,1,128]{3,2,1,0:T(1,128)}), f32[128,17,1,128]{3,2,1,0:T(1,128)S(1)}, u32[]{:S(2)}, u32[]{:S(2)}) %all-to-all-start) | async-done | bytes 1114144 | tf_op jit(solution)/shard_map/all_to_all | solution.py:521
  38.2 0.0 copy-done.4
  38.2 1.2 %ocean.1 = (f32[16,32,128]{2,1,0:T(8,128)}, f32[128,8,128]{2,1,0:T(8,128)S(1)}) custom-call(f32[2176,128]{1,0:T(8,128)S(1)} %bitcast.8, f32[16,32,128]{2,1,0:T(8,128)S(1)} %advect.1.inner, f32[8,32,128]{2,1,0:T(8,128)S(1)} %copy-done.4, s32[32,128]{1,0:T(8,128)S(1)} %copy-done.3, f32[32,128]{1,0:T(8,128)S(1)} %get-tuple-element.14.to_east, ...), custom_call_target="tpu_custom_call" | custom-call | flops 100000000 | bytes 4000000 | tf_op jit(solution)/shard_map/ocean/pallas_call | solution.py:357
  39.4 17.2 %all_to_all.10 = f32[128,8,128]{2,1,0:T(8,128)S(1)} all-to-all(f32[128,8,128]{2,1,0:T(8,128)S(1)} %get-tuple-element.21), channel_id=1, replica_groups=mesh['lon'=32,'lat'=4] {'lon','lat'}, dimensions={0} | all-to-all | bytes 1048576 | tf_op jit(solution)/shard_map/all_to_all | solution.py:541
  56.6 4.2 %state.1 = f32[256,2,128]{2,1,0:T(2,128)} custom-call(s32[2,128]{1,0:T(2,128)S(1)} %get-tuple-element.20.slots_in, f32[1024,128]{1,0:T(8,128)S(1)} %bitcast.9, bf16[32,128,128]{2,1,0:T(8,128)(2,1)S(1)} %get-tuple-element.22.near, bf16[24,128,128]{2,1,0:T(8,128)(2,1)S(1)} %get-tuple-element.23.mid, bf16[256,128,128]{2,1,0:T(8,128)(2,1)} %remap_hbm.5, ...), custom_call_target="tpu_custom_call" | custom-call | flops 1000000000 | bytes 9000000 | tf_op jit(solution)/shard_map/state/pallas_call | solution.py:477
Async XLA Ops:
  0.6 16.9 %copy-start = (f32[2,8,32,128]{3,2,1,0:T(8,128)S(1)}, f32[2,8,32,128]{3,2,1,0:T(8,128)}, u32[]{:S(2)}) copy-start(f32[2,8,32,128]{3,2,1,0:T(8,128)} %param.13) | copy-start | bytes 786436
  0.6 16.9 %copy-start.1 = (f32[8,32,128]{2,1,0:T(8,128)S(1)}, f32[8,32,128]{2,1,0:T(8,128)}, u32[]{:S(2)}) copy-start(f32[8,32,128]{2,1,0:T(8,128)} %east_vel.3) | copy-start | bytes 393220
  0.7 16.9 %copy-start.2 = (f32[8,32,128]{2,1,0:T(8,128)S(1)}, f32[8,32,128]{2,1,0:T(8,128)}, u32[]{:S(2)}) copy-start(f32[8,32,128]{2,1,0:T(8,128)} %north_vel.3) | copy-start | bytes 393220
  0.7 16.9 %copy-start.3 = (s32[32,128]{1,0:T(8,128)S(1)}, s32[32,128]{1,0:T(8,128)}, u32[]{:S(2)}) copy-start(s32[32,128]{1,0:T(8,128)} %levels.5) | copy-start | bytes 49156
  6.1 32.1 %all-to-all-start = ((f32[128,17,1,128]{3,2,1,0:T(1,128)}), f32[128,17,1,128]{3,2,1,0:T(1,128)S(1)}, u32[]{:S(2)}, u32[]{:S(2)}) async-start(f32[128,17,1,128]{3,2,1,0:T(1,128)} %bitcast.3), calls=%async_computation | async-start | bytes 2228224 | tf_op jit(solution)/shard_map/all_to_all | solution.py:521
  17.9 9.8 %collective-permute-start = (f32[32,128]{1,0:T(8,128)S(1)}, f32[32,128]{1,0:T(8,128)S(1)}, u32[]{:S(2)}, u32[]{:S(2)}) collective-permute-start(f32[32,128]{1,0:T(8,128)S(1)} %get-tuple-element.14.to_east), channel_id=1, source_target_pairs={{0,4},{4,8},{8,12},{12,16},{16,20},{20,24},{24,28},{28,32},{32,36}... | collective-permute-start | bytes 49160 | tf_op jit(solution)/shard_map/ppermute | solution.py:511
  19.7 8.0 %collective-permute-start.1 = (f32[32,128]{1,0:T(8,128)S(1)}, f32[32,128]{1,0:T(8,128)S(1)}, u32[]{:S(2)}, u32[]{:S(2)}) collective-permute-start(f32[32,128]{1,0:T(8,128)S(1)} %get-tuple-element.15.to_west), channel_id=1, source_target_pairs={{4,0},{8,4},{12,8},{16,12},{20,16},{24,20},{28,24},{32,28},{36,32}... | collective-permute-start | bytes 49160 | tf_op jit(solution)/shard_map/ppermute | solution.py:512
  19.7 8.9 %collective-permute-start.2 = (f32[32,128]{1,0:T(8,128)S(1)}, f32[32,128]{1,0:T(8,128)S(1)}, u32[]{:S(2)}, u32[]{:S(2)}) collective-permute-start(f32[32,128]{1,0:T(8,128)S(1)} %get-tuple-element.16.to_north), channel_id=1, source_target_pairs={{0,1},{1,2},{2,3},{4,5},{5,6},{6,7},{8,9},{9,10},{10,11},{12,13},{... | collective-permute-start | bytes 49160 | tf_op jit(solution)/shard_map/ppermute | solution.py:513
  22.8 8.6 %collective-permute-start.3 = (f32[32,128]{1,0:T(8,128)S(1)}, f32[32,128]{1,0:T(8,128)S(1)}, u32[]{:S(2)}, u32[]{:S(2)}) collective-permute-start(f32[32,128]{1,0:T(8,128)S(1)} %get-tuple-element.17.to_south), channel_id=1, source_target_pairs={{1,0},{2,1},{3,2},{5,4},{6,5},{7,6},{9,8},{10,9},{11,10},{13,12},{... | collective-permute-start | bytes 49160 | tf_op jit(solution)/shard_map/ppermute | solution.py:514
  24.4 13.8 %copy-start.4 = (f32[8,32,128]{2,1,0:T(8,128)S(1)}, f32[8,32,128]{2,1,0:T(8,128)}, u32[]{:S(2)}) copy-start(f32[8,32,128]{2,1,0:T(8,128)} %kappa.1) | copy-start | bytes 393220
